TPU v7x, 128 devices: a whole 4x4x4 slice. The times are simulated.
128 devices in a mesh: gx: 4 (over y), gy: 16 (over x_hi, z, core), gz: 2 (over x_lo).
Axes of the slice: x: 4 (x_hi: 2, x_lo: 2; x = x_hi * 2 + x_lo), y: 4, z: 4, core: 2. Of those that a mesh axis runs over, the one named last changes fastest.
Arguments:
- inputs: bfloat16 [64, 16, 128, 256], P(None, 'gx', 'gy', 'gz'), may hold values from -6 to 6
- weight: bfloat16 [4, 4, 4, 64, 32], replicated, may hold values from -0.25 to 0.25
- cotangent: bfloat16 [2, 2, 2, 32, 16, 128, 256], P(None, None, None, None, 'gx', 'gy', 'gz'), may hold values from -3 to 3
Outputs:
- upsampled: bfloat16 [2, 2, 2, 32, 16, 128, 256], P(None, None, None, None, 'gx', 'gy', 'gz')
- input_grad: bfloat16 [64, 16, 128, 256], P(None, 'gx', 'gy', 'gz')
- weight_grad: float32 [4, 4, 4, 64, 32], replicated
All inputs are finite; a program needn't handle non-finite values.
Results may differ from a plain program's by a relative error of at most 0.0018.
Values may be sent and summed in bfloat16 or wider, within the bound.
No kernel may reach another device: no remote copies, remote signals or barrier semaphores. Data moves between devices by JAX's collectives and lax.ppermute only.
A program may use at most 192 MiB of HBM per device.

v0:
```python
import math

import jax
import jax.numpy as jnp
from jax import lax
from jax.sharding import PartitionSpec as P


def extended_2(cells, sides, width):
    for axis, dim in sides:
        count = lax.axis_size(axis)
        head = lax.slice_in_dim(cells, 0, width, axis=dim)
        tail = lax.slice_in_dim(cells, cells.shape[dim] - width, cells.shape[dim], axis=dim)
        cells = jnp.concatenate(
            [
                lax.ppermute(tail, axis, [(i, (i + 1) % count) for i in range(count)]),
                cells,
                lax.ppermute(head, axis, [((i + 1) % count, i) for i in range(count)]),
            ],
            axis=dim,
        )
    return cells


def open_ends(extended):
    length = extended.shape[-1]
    spots = jnp.arange(length)
    first_ok = lax.axis_index("gz") > 0
    last_ok = lax.axis_index("gz") < lax.axis_size("gz") - 1
    allowed = jnp.logical_and(
        jnp.logical_or(spots > 0, first_ok), jnp.logical_or(spots < length - 1, last_ok)
    )
    return jnp.where(allowed, extended, jnp.zeros((), extended.dtype))


def body(inputs, weight, cotangent):
    in_ch, cells_x, cells_y, cells_z = inputs.shape
    out_ch = weight.shape[4]
    parities = [(odd_x, odd_y, odd_z) for odd_x in (0, 1) for odd_y in (0, 1) for odd_z in (0, 1)]
    padded = extended_2(inputs, (("gx", 1), ("gy", 2), ("gz", 3)), 1)
    padded = open_ends(padded)
    pieces = []
    for odd_x, odd_y, odd_z in parities:
        summed = jnp.zeros((out_ch, cells_x, cells_y, cells_z), jnp.float32)
        for half_x, half_y, half_z in parities:
            tap = weight[1 - odd_x + 2 * half_x, 1 - odd_y + 2 * half_y, 1 - odd_z + 2 * half_z]
            start_x = 1 + odd_x - half_x
            start_y = 1 + odd_y - half_y
            start_z = 1 + odd_z - half_z
            window = lax.slice(
                padded,
                (0, start_x, start_y, start_z),
                (in_ch, start_x + cells_x, start_y + cells_y, start_z + cells_z),
            )
            summed = summed + jnp.einsum(
                "io,ixyz->oxyz", tap, window, preferred_element_type=jnp.float32
            )
        pieces.append(summed.astype(jnp.bfloat16))
    upsampled = jnp.stack(pieces).reshape((2, 2, 2, out_ch, cells_x, cells_y, cells_z))
    grad_ext = extended_2(cotangent, (("gx", 4), ("gy", 5), ("gz", 6)), 1)
    grad_ext = open_ends(grad_ext)
    input_sum = jnp.zeros((in_ch, cells_x, cells_y, cells_z), jnp.float32)
    tap_grads = {}
    for odd_x, odd_y, odd_z in parities:
        source = grad_ext[odd_x, odd_y, odd_z]
        for half_x, half_y, half_z in parities:
            tap_x = 1 - odd_x + 2 * half_x
            tap_y = 1 - odd_y + 2 * half_y
            tap_z = 1 - odd_z + 2 * half_z
            start_x = 1 - odd_x + half_x
            start_y = 1 - odd_y + half_y
            start_z = 1 - odd_z + half_z
            window = lax.slice(
                source,
                (0, start_x, start_y, start_z),
                (out_ch, start_x + cells_x, start_y + cells_y, start_z + cells_z),
            )
            input_sum = input_sum + jnp.einsum(
                "io,oxyz->ixyz",
                weight[tap_x, tap_y, tap_z],
                window,
                preferred_element_type=jnp.float32,
            )
            tap_grads[tap_x, tap_y, tap_z] = jnp.einsum(
                "ixyz,oxyz->io", inputs, window, preferred_element_type=jnp.float32
            )
    ordered = [
        tap_grads[tap_x, tap_y, tap_z]
        for tap_x in range(4)
        for tap_y in range(4)
        for tap_z in range(4)
    ]
    local_grad = jnp.stack(ordered).reshape((4, 4, 4, in_ch, out_ch))
    total_grad = lax.psum(local_grad, ("gx", "gy", "gz"))
    all_cells = (
        cells_x
        * lax.axis_size("gx")
        * cells_y
        * lax.axis_size("gy")
        * cells_z
        * lax.axis_size("gz")
    )
    factor = 1.0 / math.sqrt(all_cells)
    return (upsampled, input_sum.astype(jnp.bfloat16), total_grad * factor)


def solution(mesh):
    placed = (P(None, "gx", "gy", "gz"), P(), P(None, None, None, None, "gx", "gy", "gz"))
    return jax.shard_map(
        body,
        mesh=mesh,
        in_specs=placed,
        out_specs=(P(None, None, None, None, "gx", "gy", "gz"), P(None, "gx", "gy", "gz"), P()),
        check_vma=False,
    )
```

profile of v0, /device:TPU:1, one launch (start us, length us, event | category | flops | bytes accessed | tf_op | source)
XLA Modules:
  0.0 357.4 jit_solution(10003181567017914125)
XLA Ops:
  8.4 2.2 collective-permute-start
  12.1 3.0 collective-permute-done
  16.4 3.0 collective-permute-start.2
  21.6 2.6 collective-permute-start.7
  32.1 2.8 maximum_select_fusion.1
  61.1 3.4 collective-permute-start.8
  64.5 2.2 collective-permute-start.9
  69.7 2.0 collective-permute-done.9
  73.0 4.1 %fusion.754 = (bf16[2,2,2,32,6,10,1]{6,3,5,4,2,1,0:T(8,128)(2,1)}, bf16[2,2,2,32,6,10,1]{6,3,5,4,2,1,0:T(8,128)(2,1)}) fusion(bf16[2,2,2,32,6,10,128]{6,3,5,4,2,1,0:T(8,128)(2,1)S(1)} %pad_maximum_fusion), kind=kLoop, calls=%fused_computation.909 | loop fusion | bytes 122880 | tf_op jit(solution)/shard_map/slice | solution.py:13
  77.1 5.3 %copy.88 = bf16[2,2,2,32,6,10,1]{3,2,6,5,4,1,0:T(2,128)(2,1)} copy(bf16[2,2,2,32,6,10,1]{6,3,5,4,2,1,0:T(8,128)(2,1)} %get-tuple-element.17) | data formatting | bytes 61440 | tf_op jit(solution)/shard_map/slice | solution.py:13
  82.6 5.3 %copy.89 = bf16[2,2,2,32,6,10,1]{3,2,6,5,4,1,0:T(2,128)(2,1)} copy(bf16[2,2,2,32,6,10,1]{6,3,5,4,2,1,0:T(8,128)(2,1)} %get-tuple-element.18) | data formatting | bytes 61440 | tf_op jit(solution)/shard_map/slice | solution.py:12
  89.1 2.6 fusion.106
  91.8 3.7 %copy.156 = bf16[2,2,2,32,4,8,128]{6,5,4,3,2,1,0:T(8,128)(2,1)} copy(bf16[2,2,2,32,4,8,128]{6,3,5,4,2,1,0:T(8,128)(2,1)} %bitcast.1474) | data formatting | bytes 4194304
  95.5 5.0 %copy.90 = bf16[2,2,2,32,6,10,1]{6,3,5,4,2,1,0:T(8,128)(2,1)} copy(bf16[2,2,2,32,6,10,1]{3,2,6,5,4,1,0:T(2,128)(2,1)} %collective-permute-done.10) | data formatting | bytes 61440 | tf_op jit(solution)/shard_map/ppermute | solution.py:16
  100.5 5.1 %copy.91 = bf16[2,2,2,32,6,10,1]{6,3,5,4,2,1,0:T(8,128)(2,1)} copy(bf16[2,2,2,32,6,10,1]{3,2,6,5,4,1,0:T(2,128)(2,1)} %collective-permute-done.11) | data formatting | bytes 61440 | tf_op jit(solution)/shard_map/ppermute | solution.py:18
  105.6 8.7 %maximum_select_fusion = bf16[2,2,2,32,6,10,130]{6,3,5,4,2,1,0:T(8,128)(2,1)S(1)} fusion(bf16[2,2,2,32,6,10,1]{6,3,5,4,2,1,0:T(8,128)(2,1)} %copy.91, bf16[2,2,2,32,6,1,128]{6,3,5,4,2,1,0:T(8,128)(2,1)} %copy-done.58, bf16[2,2,2,32,6,8,128]{6,3,5,4,2,1,0:T(8,128)(2,1)S(1)} %copy-done.1, bf16[2,2,2,32,6,1,128]{6,3,5,4,2,1,0:T(8,128)(2,1)S(1)} %copy-done.57, ...), kind=kLoop, calls=%fused_computation | loop fusion | flops 21964800 | bytes 7987330 | tf_op jit(solution)/shard_map/jit(_where)/select_n | solution.py:33
  114.4 1.7 slice_bitcast_fusion.6
  116.1 1.7 convolution_bitcast_fusion.40
  167.1 1.5 convolution_bitcast_fusion.2
  196.7 1.8 convolution_add_fusion.15
  209.8 1.9 fusion.46
  213.1 1.9 fusion.45
  224.2 123.8 %all-reduce.2.cloned.1.call-done = f32[4,4,4,64,32]{3,4,2,1,0:T(8,128)} async-done(((f32[4,4,4,64,32]{3,4,2,1,0:T(8,128)}), f32[4,4,4,64,32]{3,4,2,1,0:T(8,128)}) %all-reduce.2.cloned.1.call-update) | async-done | bytes 524304 | tf_op jit(solution)/shard_map/psum | solution.py:94
  348.0 2.3 broadcast_multiply_fusion
  (350 shorter events, 144.4 us)
Async XLA Ops:
  7.2 12.3 %copy-start.10 = (bf16[2,2,2,32,4,8,128]{6,5,4,3,2,1,0:T(8,128)(2,1)S(1)}, bf16[2,2,2,32,4,8,128]{6,5,4,3,2,1,0:T(8,128)(2,1)}, u32[]{:S(2)}) copy-start(bf16[2,2,2,32,4,8,128]{6,5,4,3,2,1,0:T(8,128)(2,1)} %param.5) | copy-start | bytes 6291460
  7.2 340.8 %all-reduce.2.cloned.1.call-start = ((), (), s32[]{:S(2)}) async-start(), calls=%async_computation | async-start | bytes 2097152 | tf_op jit(solution)/shard_map/psum | solution.py:94
  8.4 6.7 %collective-permute-start = (bf16[64,1,8,128]{3,0,2,1:T(8,128)(2,1)S(1)}, bf16[64,1,8,128]{3,0,2,1:T(8,128)(2,1)S(1)}, u32[]{:S(2)}, u32[]{:S(2)}) collective-permute-start(bf16[64,1,8,128]{3,0,2,1:T(8,128)(2,1)S(1)} %copy.416), channel_id=1, source_target_pairs={{0,32},{32,64},{64,96},{96,0},{1,33},{33,65},{65,97},{97,1},{2,34}... | collective-permute-start | bytes 393224 | tf_op jit(solution)/shard_map/ppermute | solution.py:16
  10.6 5.8 %collective-permute-start.1 = (bf16[64,1,8,128]{3,0,2,1:T(8,128)(2,1)S(1)}, bf16[64,1,8,128]{3,0,2,1:T(8,128)(2,1)S(1)}, u32[]{:S(2)}, u32[]{:S(2)}) collective-permute-start(bf16[64,1,8,128]{3,0,2,1:T(8,128)(2,1)S(1)} %copy.417), channel_id=1, source_target_pairs={{32,0},{64,32},{96,64},{0,96},{33,1},{65,33},{97,65},{1,97},{34,2}... | collective-permute-start | bytes 393224 | tf_op jit(solution)/shard_map/ppermute | solution.py:18
  16.4 7.8 %collective-permute-start.2 = (bf16[64,6,1,128]{3,0,2,1:T(8,128)(2,1)S(1)}, bf16[64,6,1,128]{3,0,2,1:T(8,128)(2,1)S(1)}, u32[]{:S(2)}, u32[]{:S(2)}) collective-permute-start(bf16[64,6,1,128]{3,0,2,1:T(8,128)(2,1)S(1)} %get-tuple-element.25), channel_id=1, source_target_pairs={{0,2},{2,4},{4,6},{6,8},{8,10},{10,12},{12,14},{14,16},{16,18},{18... | collective-permute-start | bytes 294920 | tf_op jit(solution)/shard_map/ppermute | solution.py:16
  19.4 4.8 %collective-permute-start.3 = (bf16[64,6,1,128]{3,0,2,1:T(8,128)(2,1)S(1)}, bf16[64,6,1,128]{3,0,2,1:T(8,128)(2,1)S(1)}, u32[]{:S(2)}, u32[]{:S(2)}) collective-permute-start(bf16[64,6,1,128]{3,0,2,1:T(8,128)(2,1)S(1)} %get-tuple-element.26), channel_id=1, source_target_pairs={{2,0},{4,2},{6,4},{8,6},{10,8},{12,10},{14,12},{16,14},{18,16},{20... | collective-permute-start | bytes 294920 | tf_op jit(solution)/shard_map/ppermute | solution.py:18
  20.6 37.2 %collective-permute-start.6 = (bf16[2,2,2,32,1,8,128]{6,3,5,4,2,1,0:T(8,128)(2,1)}, bf16[2,2,2,32,1,8,128]{6,3,5,4,2,1,0:T(8,128)(2,1)}, u32[]{:S(2)}, u32[]{:S(2)}) collective-permute-start(bf16[2,2,2,32,1,8,128]{6,3,5,4,2,1,0:T(8,128)(2,1)} %copy.418), channel_id=1, source_target_pairs={{0,32},{32,64},{64,96},{96,0},{1,33},{33,65},{65,97},{97,1},{2,34}... | collective-permute-start | bytes 1572872 | tf_op jit(solution)/shard_map/ppermute | solution.py:16
  21.6 38.3 %collective-permute-start.7 = (bf16[2,2,2,32,1,8,128]{6,3,5,4,2,1,0:T(8,128)(2,1)}, bf16[2,2,2,32,1,8,128]{6,3,5,4,2,1,0:T(8,128)(2,1)}, u32[]{:S(2)}, u32[]{:S(2)}) collective-permute-start(bf16[2,2,2,32,1,8,128]{6,3,5,4,2,1,0:T(8,128)(2,1)} %copy.419), channel_id=1, source_target_pairs={{32,0},{64,32},{96,64},{0,96},{33,1},{65,33},{97,65},{1,97},{34,2}... | collective-permute-start | bytes 1572872 | tf_op jit(solution)/shard_map/ppermute | solution.py:18
  25.4 2.7 collective-permute-start.4
  27.2 3.6 collective-permute-start.5
  54.4 4.6 %copy-start.11 = (bf16[2,2,2,32,4,8,128]{6,5,4,3,2,1,0:T(8,128)(2,1)S(1)}, bf16[2,2,2,32,4,8,128]{6,5,4,3,2,1,0:T(8,128)(2,1)}, u32[]{:S(2)}) copy-start(bf16[2,2,2,32,4,8,128]{6,5,4,3,2,1,0:T(8,128)(2,1)} %param.5) | copy-start | bytes 6291460
  61.0 10.7 %copy-start = (bf16[2,2,2,32,6,8,128]{6,3,5,4,2,1,0:T(8,128)(2,1)}, bf16[2,2,2,32,6,8,128]{6,3,5,4,2,1,0:T(8,128)(2,1)S(1)}, u32[]{:S(2)}) copy-start(bf16[2,2,2,32,6,8,128]{6,3,5,4,2,1,0:T(8,128)(2,1)S(1)} %constant_dynamic-update-slice_fusion.3) | copy-start | bytes 9437188
  61.1 8.1 %collective-permute-start.8 = (bf16[2,2,2,32,6,1,128]{6,3,5,4,2,1,0:T(8,128)(2,1)S(1)}, bf16[2,2,2,32,6,1,128]{6,3,5,4,2,1,0:T(8,128)(2,1)S(1)}, u32[]{:S(2)}, u32[]{:S(2)}) collective-permute-start(bf16[2,2,2,32,6,1,128]{6,3,5,4,2,1,0:T(8,128)(2,1)S(1)} %get-tuple-element.19), channel_id=1, source_target_pairs={{0,2},{2,4},{4,6},{6,8},{8,10},{10,12},{12,14},{14,16},{16,18},{18... | collective-permute-start | bytes 1179656 | tf_op jit(solution)/shard_map/ppermute | solution.py:16
  64.5 7.2 %collective-permute-start.9 = (bf16[2,2,2,32,6,1,128]{6,3,5,4,2,1,0:T(8,128)(2,1)S(1)}, bf16[2,2,2,32,6,1,128]{6,3,5,4,2,1,0:T(8,128)(2,1)S(1)}, u32[]{:S(2)}, u32[]{:S(2)}) collective-permute-start(bf16[2,2,2,32,6,1,128]{6,3,5,4,2,1,0:T(8,128)(2,1)S(1)} %get-tuple-element.20), channel_id=1, source_target_pairs={{2,0},{4,2},{6,4},{8,6},{10,8},{12,10},{14,12},{16,14},{18,16},{20... | collective-permute-start | bytes 1179656 | tf_op jit(solution)/shard_map/ppermute | solution.py:18
  82.4 13.1 %collective-permute-start.10 = (bf16[2,2,2,32,6,10,1]{3,2,6,5,4,1,0:T(2,128)(2,1)}, bf16[2,2,2,32,6,10,1]{3,2,6,5,4,1,0:T(2,128)(2,1)}, u32[]{:S(2)}, u32[]{:S(2)}) collective-permute-start(bf16[2,2,2,32,6,10,1]{3,2,6,5,4,1,0:T(2,128)(2,1)} %copy.88), channel_id=1, source_target_pairs={{0,1},{1,0},{2,3},{3,2},{4,5},{5,4},{6,7},{7,6},{8,9},{9,8},{10,11... | collective-permute-start | bytes 92168 | tf_op jit(solution)/shard_map/ppermute | solution.py:16
  87.9 12.5 %collective-permute-start.11 = (bf16[2,2,2,32,6,10,1]{3,2,6,5,4,1,0:T(2,128)(2,1)}, bf16[2,2,2,32,6,10,1]{3,2,6,5,4,1,0:T(2,128)(2,1)}, u32[]{:S(2)}, u32[]{:S(2)}) collective-permute-start(bf16[2,2,2,32,6,10,1]{3,2,6,5,4,1,0:T(2,128)(2,1)} %copy.89), channel_id=1, source_target_pairs={{1,0},{0,1},{3,2},{2,3},{5,4},{4,5},{7,6},{6,7},{9,8},{8,9},{11,10... | collective-permute-start | bytes 92168 | tf_op jit(solution)/shard_map/ppermute | solution.py:18
  100.5 5.1 %copy-start.1 = (bf16[2,2,2,32,6,8,128]{6,3,5,4,2,1,0:T(8,128)(2,1)S(1)}, bf16[2,2,2,32,6,8,128]{6,3,5,4,2,1,0:T(8,128)(2,1)}, u32[]{:S(2)}) copy-start(bf16[2,2,2,32,6,8,128]{6,3,5,4,2,1,0:T(8,128)(2,1)} %copy-done) | copy-start | bytes 9437188
  100.5 5.1 %copy-start.57 = (bf16[2,2,2,32,6,1,128]{6,3,5,4,2,1,0:T(8,128)(2,1)S(1)}, bf16[2,2,2,32,6,1,128]{6,3,5,4,2,1,0:T(8,128)(2,1)}, u32[]{:S(2)}) copy-start(bf16[2,2,2,32,6,1,128]{6,3,5,4,2,1,0:T(8,128)(2,1)} %copy-done.56) | copy-start | bytes 1179652
  116.1 73.6 %copy-start.2 = (bf16[32,6,10,130]{3,0,2,1:T(8,128)(2,1)}, bf16[32,6,10,130]{3,0,2,1:T(8,128)(2,1)S(1)}, u32[]{:S(2)}) copy-start(bf16[32,6,10,130]{3,0,2,1:T(8,128)(2,1)S(1)} %get-tuple-element.13) | copy-start | bytes 1497604
  116.1 77.5 %copy-start.3 = (bf16[32,6,10,130]{3,0,2,1:T(8,128)(2,1)}, bf16[32,6,10,130]{3,0,2,1:T(8,128)(2,1)S(1)}, u32[]{:S(2)}) copy-start(bf16[32,6,10,130]{3,0,2,1:T(8,128)(2,1)S(1)} %get-tuple-element.14) | copy-start | bytes 1497604
  116.1 77.8 %copy-start.4 = (bf16[32,6,10,130]{3,0,2,1:T(8,128)(2,1)}, bf16[32,6,10,130]{3,0,2,1:T(8,128)(2,1)S(1)}, u32[]{:S(2)}) copy-start(bf16[32,6,10,130]{3,0,2,1:T(8,128)(2,1)S(1)} %get-tuple-element.15) | copy-start | bytes 1497604
  116.1 78.8 %copy-start.6 = (bf16[32,6,10,130]{3,0,2,1:T(8,128)(2,1)}, bf16[32,6,10,130]{3,0,2,1:T(8,128)(2,1)S(1)}, u32[]{:S(2)}) copy-start(bf16[32,6,10,130]{3,0,2,1:T(8,128)(2,1)S(1)} %get-tuple-element.9) | copy-start | bytes 1497604
  116.1 79.2 %copy-start.8 = (bf16[32,6,10,130]{3,0,2,1:T(8,128)(2,1)}, bf16[32,6,10,130]{3,0,2,1:T(8,128)(2,1)S(1)}, u32[]{:S(2)}) copy-start(bf16[32,6,10,130]{3,0,2,1:T(8,128)(2,1)S(1)} %get-tuple-element.16) | copy-start | bytes 1497604
  155.9 4.1 %copy-start.59 = (bf16[64,4,8,128]{3,2,1,0:T(8,128)(2,1)S(1)}, bf16[64,4,8,128]{3,2,1,0:T(8,128)(2,1)}, u32[]{:S(2)}) copy-start(bf16[64,4,8,128]{3,2,1,0:T(8,128)(2,1)} %param.3) | copy-start | bytes 1572868
  (50 other events, 106.4 us)
Sparse Core Ops, SparseCore 0:
  196.8 151.1 all-reduce.1
where the time goes:
time: 362 us; the launch traced here: 357 us
  waiting for transfers between devices  131 us (36%)
  matrix products  120 us (33%)
  local copies, waits for them, and re-layouts  57.8 us (16%)
  starting transfers between devices  18.5 us (5%)
  between operations  15.3 us (4%)
  other arithmetic  14.5 us (4%)
    psum x1, waiting for transfers between devices, body(): total_grad = lax.psum(local_grad, ('gx', 'gy', 'gz'))  124 us
    dot_general x64, matrix products, body(): jnp.einsum('io,oxyz->ixyz', weight[tap_x, tap_y, tap_z], window, preferre...  71.6 us
    dot_general x64, matrix products, body(): jnp.einsum('io,ixyz->oxyz', tap, window, preferred_element_type=jnp.float32)  26.9 us
    unnamed x132, local copies, waits for them, and re-layouts  24.3 us
    dot_general x64, matrix products, body(): jnp.einsum('ixyz,oxyz->io', inputs, window, preferred_element_type=jnp.fl...  21.7 us
    select_n x2, other arithmetic, open_ends(): return jnp.where(allowed, extended, jnp.zeros((), extended.dtype))  11.5 us
    slice x6, local copies, waits for them, and re-layouts, extended_2(): lax.slice_in_dim(cells, cells.shape[dim] - width, cells.shape[dim], axis=...  10.5 us
    ppermute x6, starting transfers between devices, extended_2(): lax.ppermute(tail, axis, [(i, (i + 1) % count) for i in range(count)])  10.2 us
  transfers between devices with their start and end apart: 13, of which 6 were waited for; matrix products, arithmetic and copies ran while one was open for 19% of the time, Pallas kernels for 0%

commit v1 on v0

v1 whole, which is shorter than its diff:
```python
import functools
import math

import jax
import jax.numpy as jnp
from jax import lax
from jax.experimental import pallas as pl
from jax.experimental.pallas import tpu as pltpu
from jax.sharding import PartitionSpec as P

AXES = ("gx", "gy", "gz")
F32, BF16 = jnp.float32, jnp.bfloat16
NT = (((1,), (1,)), ((), ()))
NN = (((1,), (0,)), ((), ()))
PARAMS = pltpu.CompilerParams(vmem_limit_bytes=56 * 1024 * 1024)
WHOLE = pl.BlockSpec(memory_space=pltpu.VMEM)


def shaped(shape, dtype=BF16):
    return jax.ShapeDtypeStruct(shape, dtype)


def call(kernel, out_shape, scratch=(), flops=0):
    def run(*operands):
        moved = sum(o.size * o.dtype.itemsize for o in (*operands, *jax.tree.leaves(out_shape)))
        return pl.pallas_call(
            kernel,
            out_shape=out_shape,
            in_specs=[WHOLE] * len(operands),
            out_specs=jax.tree.map(lambda _: WHOLE, out_shape),
            scratch_shapes=list(scratch),
            compiler_params=PARAMS,
            cost_estimate=pl.CostEstimate(flops=flops, bytes_accessed=moved, transcendentals=0),
        )(*operands)

    return run


def rolled(tile, column, before):
    lane = lax.broadcasted_iota(jnp.int32, tile.shape, 1)
    inside = lax.axis_index("gz") == (1 if before else 0)
    edge = jnp.where(inside, column.astype(F32), jnp.zeros(column.shape, F32))
    moved = pltpu.roll(tile, 1 if before else 127, 1).astype(F32)
    return jnp.where(lane == (0 if before else 127), edge, moved).astype(tile.dtype)


def plane_of(xe, own, left, right, z_own):
    if xe == 0:
        return left, left[:, 1024:1152]
    if xe == 5:
        return right, right[:, 1024:1152]
    return own.at[xe - 1], z_own[xe - 1]


def xor_pairs(fx, fy, fz):
    pairs = []
    for gx in range(4):
        for gy in range(16):
            for gz in range(2):
                pairs.append(((gx * 16 + gy) * 2 + gz, ((gx ^ fx) * 16 + (gy ^ fy)) * 2 + (gz ^ fz)))
    return pairs


def ring(count, step):
    return [(i, (i + step) % count) for i in range(count)]


OUTER = [(i, (i - 1) % 16 if i % 2 == 0 else (i + 1) % 16) for i in range(16)]
INNER = [(i, i ^ 1) for i in range(16)]


def first_core():
    return lax.rem(lax.axis_index("gy"), 2) == 0


def low_and_high(inner, outer, n):
    a, b, first = inner[n], outer[n], first_core()
    return jnp.where(first, b, a), jnp.where(first, a, b)


def side_picker():
    cell = lax.broadcasted_iota(jnp.int32, (1024, 128), 0)
    lane = lax.broadcasted_iota(jnp.int32, (1024, 128), 1)
    side = jnp.where(lax.axis_index("gz") == 0, 127, 0)
    return (cell == lane * 128 + side).astype(F32).astype(BF16)


def prepare_in_kernel(raw, own, z_face):
    pick = side_picker()
    for x in range(4):
        plane = raw[:, x].reshape(64, 1024)
        own[x] = plane
        z_face[x] = jnp.dot(plane, pick, preferred_element_type=F32).astype(BF16)


def prepare_cot_kernel(raw, cot, z_face):
    pick = side_picker()
    for n in range(8):
        cot[0, n * 32 : n * 32 + 32, :] = raw[n, :, 0].reshape(32, 1024)
    z_face[0] = jnp.dot(cot[0], pick, preferred_element_type=F32).astype(BF16)


def edge_in_kernel(own, left, right, z_own, inner_out, outer_out):
    lane = lax.broadcasted_iota(jnp.int32, (64, 128), 1)
    first = first_core()
    z_inner = jnp.zeros((64, 128), F32)
    z_outer = jnp.zeros((64, 128), F32)
    for xe in range(6):
        plane, z_tile = plane_of(xe, own, left, right, z_own)
        low, high = plane[:, 0:128], plane[:, 896:1024]
        inner_out[xe] = jnp.where(first, high, low)
        outer_out[xe] = jnp.where(first, low, high)
        z_wide = z_tile.astype(F32)
        low, high = z_wide[:, 0:1], z_wide[:, 7:8]
        z_inner = jnp.where(lane == xe, jnp.where(first, high, low), z_inner)
        z_outer = jnp.where(lane == xe, jnp.where(first, low, high), z_outer)
    inner_out[6] = z_inner.astype(BF16)
    outer_out[6] = z_outer.astype(BF16)


def cot_rows(n, py, own, left, right, z_own):
    xe, px = (n + 1) // 2, (n + 1) % 2
    if xe == 0 or xe == 5:
        part = left if xe == 0 else right
        rows = slice(py * 64, py * 64 + 64)
        return lambda y: part[rows, y * 128 : y * 128 + 128], part[rows, 1024:1152]
    rows = slice(px * 128 + py * 64, px * 128 + py * 64 + 64)
    return lambda y: own[xe - 1, rows, y * 128 : y * 128 + 128], z_own[xe - 1, rows, :]


def edge_cot_kernel(own, left, right, z_own, inner_out, outer_out):
    lane = lax.broadcasted_iota(jnp.int32, (64, 128), 1)
    first = first_core()
    z_inner = jnp.zeros((64, 128), F32)
    z_outer = jnp.zeros((64, 128), F32)
    for n in range(10):
        cells, z_tile = cot_rows(n, 0, own, left, right, z_own)
        low, z_low = cells(0), z_tile.astype(F32)[:, 0:1]
        cells, z_tile = cot_rows(n, 1, own, left, right, z_own)
        high, z_high = cells(7), z_tile.astype(F32)[:, 7:8]
        inner_out[n] = jnp.where(first, high, low)
        outer_out[n] = jnp.where(first, low, high)
        z_inner = jnp.where(lane == n, jnp.where(first, z_high, z_low), z_inner)
        z_outer = jnp.where(lane == n, jnp.where(first, z_low, z_high), z_outer)
    inner_out[10] = z_inner.astype(BF16)
    outer_out[10] = z_outer.astype(BF16)


def fill_windows(planes, own, left, right, z_own, windows, edges=None):
    for spot, xe in enumerate(planes):
        plane, z_tile = plane_of(xe, own, left, right, z_own)
        base = spot * 576
        for y in range(8):
            tile = plane[:, y * 128 : y * 128 + 128]
            column = z_tile[:, y : y + 1]
            three = (rolled(tile, column, True), tile, rolled(tile, column, False))
            for sz in range(3):
                for sy in range(3):
                    at = y - (sy - 1)
                    if 0 <= at < 8:
                        row = base + sy * 192 + sz * 64
                        windows[row : row + 64, at * 128 : at * 128 + 128] = three[sz]
        if edges is None:
            nothing = jnp.zeros((192, 128), BF16)
            windows[base : base + 192, 0:128] = nothing
            windows[base + 384 : base + 576, 896:1024] = nothing
        else:
            for edge, row, cells in ((0, base, slice(0, 128)), (1, base + 384, slice(896, 1024))):
                tile = low_and_high(*edges, xe)[edge]
                column = low_and_high(*edges, 6)[edge][:, xe : xe + 1]
                windows[row : row + 64, cells] = rolled(tile, column, True)
                windows[row + 64 : row + 128, cells] = tile
                windows[row + 128 : row + 192, cells] = rolled(tile, column, False)


def wgrad_main_kernel(own, left, right, z_own, cot, pay_out, windows, total):
    fill_windows(range(6), own, left, right, z_own, windows)
    for x in range(4):
        part = lax.dot_general(windows[x * 576 : x * 576 + 1728, :], cot[x], NT, preferred_element_type=F32)
        if x == 0:
            total[...] = part
        else:
            total[...] += part
    lane = lax.broadcasted_iota(jnp.int32, (64, 128), 1) // 32
    for px in range(2):
        for hx in range(2):
            for hy in range(2):
                for hz in range(2):
                    block = jnp.zeros((64, 128), F32)
                    for py in range(2):
                        for pz in range(2):
                            row = ((px - hx + 1) * 9 + (py - hy + 1) * 3 + (pz - hz + 1)) * 64
                            piece = total[row : row + 64, px * 128 : px * 128 + 128]
                            block = piece if py + pz == 0 else jnp.where(lane == 2 * py + pz, piece, block)
                    at = (px * 8 + hx * 4 + hy * 2 + hz) * 64
                    pay_out[at : at + 64, :] = block


def wgrad_edge_kernel(inner, outer, cot, pay, keep, give, edges):
    first = first_core()
    for xe in range(6):
        for edge in range(2):
            tile = low_and_high(inner, outer, xe)[edge]
            column = low_and_high(inner, outer, 6)[edge][:, xe : xe + 1]
            base = xe * 192
            edges[edge, base : base + 64, :] = rolled(tile, column, True)
            edges[edge, base + 64 : base + 128, :] = tile
            edges[edge, base + 128 : base + 192, :] = rolled(tile, column, False)
    sums = []
    for edge, cells in ((0, slice(0, 128)), (1, slice(896, 1024))):
        summed = None
        for x in range(4):
            part = lax.dot_general(
                edges[edge, x * 192 : x * 192 + 576, :], cot[x, :, cells], NT, preferred_element_type=F32
            )
            summed = part if summed is None else summed + part
        sums.append(summed)
    lane = lax.broadcasted_iota(jnp.int32, (64, 128), 1) // 32
    for hx in range(2):
        for hy in range(2):
            for hz in range(2):
                at = (hx * 4 + hy * 2 + hz) * 64
                blocks = []
                for px in range(2):
                    block = pay[px * 512 + at : px * 512 + at + 64, :]
                    for py in range(2):
                        if py - hy == 0:
                            continue
                        for pz in range(2):
                            row = ((px - hx + 1) * 3 + (pz - hz + 1)) * 64
                            piece = sums[0 if py - hy < 0 else 1][row : row + 64, px * 128 : px * 128 + 128]
                            block = jnp.where(lane == 2 * py + pz, block + piece, block)
                    blocks.append(block)
                keep[at : at + 64, :] = jnp.where(first, blocks[0], blocks[1])
                give[at : at + 64, :] = jnp.where(first, blocks[1], blocks[0])


def z_bit():
    chip = lax.rem(lax.axis_index("gy") // 2, 4)
    return lax.rem(chip, 2) ^ (chip // 2)


def finish_kernel(mine, beside, other, other_beside, out, *, factor):
    first, low = first_core(), z_bit() == 0
    for hx in range(2):
        for hy in range(2):
            for hz in range(2):
                at = (hy * 2 + hz) * 64
                own = jnp.where(low == (hx == 0), mine[at : at + 64, :], beside[at : at + 64, :])
                far = jnp.where(low == (hx == 0), other[at : at + 64, :], other_beside[at : at + 64, :])
                for px in range(2):
                    block = (jnp.where(first == (px == 0), own, far) * factor).T
                    for py in range(2):
                        for pz in range(2):
                            spot = (2 * py + pz) * 32
                            out[2 * hx + 1 - px, 2 * hy + 1 - py, 2 * hz + 1 - pz] = block[spot : spot + 32, :]


def up_kernel(own, left, right, z_own, inner, outer, weight, out, windows, matrix, *, start):
    taps = ((3, 1, None), (None, 2, 0))
    fill_windows(range(start, start + 4), own, left, right, z_own, windows, (inner, outer))
    for px in range(2):
        for py in range(2):
            for pz in range(2):
                pieces = []
                for kx in taps[px]:
                    for ky in taps[py]:
                        for kz in taps[pz]:
                            if kx is None or ky is None or kz is None:
                                pieces.append(jnp.zeros((32, 64), BF16))
                            else:
                                pieces.append(weight[kx, ky, kz])
                row = (px * 4 + py * 2 + pz) * 32
                matrix[row : row + 32, :] = jnp.concatenate(pieces, axis=1)
    for x in range(2):
        result = lax.dot_general(matrix[...], windows[x * 576 : x * 576 + 1728, :], NN, preferred_element_type=F32)
        for n in range(8):
            out[n, :, x] = result[n * 32 : n * 32 + 32].astype(BF16).reshape(32, 8, 128)


def igrad_kernel(own, left, right, z_own, inner, outer, weight, out, windows, matrix, *, start):
    for spot in range(6):
        n = 2 * start + spot
        for ky in range(4):
            py, sy = ((1, -1), (0, 0), (1, 0), (0, 1))[ky]
            cells_at, z_tile = cot_rows(n, py, own, left, right, z_own)
            base = spot * 512 + ky * 128
            for y in range(8):
                source = y + sy
                if 0 <= source < 8:
                    tile, column = cells_at(source), z_tile[:, source : source + 1]
                else:
                    edge = 0 if sy < 0 else 1
                    tile = low_and_high(inner, outer, n)[edge]
                    column = low_and_high(inner, outer, 10)[edge][:, n : n + 1]
                cells = slice(y * 128, y * 128 + 128)
                windows[base : base + 64, cells] = tile
                windows[base + 64 : base + 96, cells] = rolled(tile[0:32], column[0:32], False)
                windows[base + 96 : base + 128, cells] = rolled(tile[32:64], column[32:64], True)
    for kx in range(4):
        for ky in range(4):
            row = (kx * 4 + ky) * 128
            for place, kz in enumerate((1, 2, 3, 0)):
                matrix[row + place * 32 : row + place * 32 + 32, :] = weight[kx, ky, kz]
    turned = matrix[...].T
    for x in range(2):
        result = lax.dot_general(turned, windows[x * 1024 : x * 1024 + 2048, :], NN, preferred_element_type=F32)
        out[:, x] = result.astype(BF16).reshape(64, 8, 128)


def send(block, *flip):
    return lax.ppermute(block, AXES, xor_pairs(*flip))


def beside(block, flip, work):
    run, operands = work
    block, operands = lax.optimization_barrier((block, operands))
    got = send(block, *flip)
    return lax.optimization_barrier((block, got, run(*operands)))


def body(inputs, weight, cotangent):
    x_up, x_down = ring(4, 1), ring(4, -1)
    swap = [(0, 1), (1, 0)]
    weight_t = weight.transpose(0, 1, 2, 4, 3)

    own, z_face = call(prepare_in_kernel, (shaped((4, 64, 1024)), shaped((4, 64, 128))))(inputs)
    z_own = lax.ppermute(z_face, "gz", swap)
    cot, z_face = pl.pallas_call(
        prepare_cot_kernel,
        grid=(4,),
        out_shape=(shaped((4, 256, 1024)), shaped((4, 256, 128))),
        in_specs=[pl.BlockSpec((8, 32, 1, 8, 128), lambda x: (0, 0, x, 0, 0))],
        out_specs=(pl.BlockSpec((1, 256, 1024), lambda x: (x, 0, 0)), pl.BlockSpec((1, 256, 128), lambda x: (x, 0, 0))),
        compiler_params=PARAMS,
    )(cotangent.reshape(8, 32, 4, 8, 128))
    z_cot = lax.ppermute(z_face, "gz", swap)
    left = lax.ppermute(jnp.concatenate([own[3], z_own[3]], axis=1), "gx", x_up)
    right = lax.ppermute(jnp.concatenate([own[0], z_own[0]], axis=1), "gx", x_down)
    cot_left = lax.ppermute(jnp.concatenate([cot[3, 128:], z_cot[3, 128:]], axis=1), "gx", x_up)
    cot_right = lax.ppermute(jnp.concatenate([cot[0, :128], z_cot[0, :128]], axis=1), "gx", x_down)

    inner, outer = call(edge_in_kernel, (shaped((7, 64, 128)),) * 2)(own, left, right, z_own)
    outer = lax.ppermute(outer, "gy", OUTER)
    inner = lax.ppermute(inner, "gy", INNER)
    pay = call(
        wgrad_main_kernel,
        shaped((1024, 128), F32),
        [pltpu.VMEM((3456, 1024), BF16), pltpu.VMEM((1728, 256), F32)],
        flops=2 * 1728 * 256 * 4096,
    )(own, left, right, z_own, cot)
    keep, give = call(
        wgrad_edge_kernel, (shaped((512, 128), F32),) * 2, [pltpu.VMEM((2, 1152, 128), BF16)], flops=2 * 1152 * 256 * 512
    )(inner, outer, cot, pay)

    def up_part(start):
        return call(
            functools.partial(up_kernel, start=start),
            shaped((8, 32, 2, 8, 128)),
            [pltpu.VMEM((2304, 1024), BF16), pltpu.VMEM((256, 1728), BF16)],
            flops=2 * 1728 * 256 * 2048,
        ), (own, left, right, z_own, inner, outer, weight_t)

    def igrad_part(start):
        return call(
            functools.partial(igrad_kernel, start=start),
            shaped((64, 2, 8, 128)),
            [pltpu.VMEM((3072, 1024), BF16), pltpu.VMEM((2048, 64), BF16)],
            flops=2 * 2048 * 256 * 2048,
        ), (cot, cot_left, cot_right, z_cot, cot_inner, cot_outer, weight_t)

    block = keep + send(give, 0, 1, 0)
    half = block.shape[0] // 2
    low = z_bit() == 0
    keep, give = jnp.where(low, block[:half], block[half:]), jnp.where(low, block[half:], block[:half])
    edge_cot = call(edge_cot_kernel, (shaped((11, 64, 128)),) * 2), (cot, cot_left, cot_right, z_cot)
    _, got, (cot_inner, cot_outer) = beside(give, (0, 2, 0), edge_cot)
    block = keep + got
    cot_outer = lax.ppermute(cot_outer, "gy", OUTER)
    cot_inner = lax.ppermute(cot_inner, "gy", INNER)
    block, got, up_0 = beside(block, (0, 6, 0), up_part(0))
    block = block + got
    block, got, up_1 = beside(block, (1, 0, 0), up_part(2))
    block = block + got
    block, got, grad_0 = beside(block, (3, 0, 0), igrad_part(0))
    block = block + got
    block, got, grad_1 = beside(block, (0, 0, 1), igrad_part(2))
    block = block + got

    def join(a, b, c, d):
        return jnp.concatenate([a, b], axis=2), jnp.concatenate([c, d], axis=1)

    block, got, (up, grad) = beside(block, (0, 8, 1), (join, (up_0, up_1, grad_0, grad_1)))
    block = block + got
    near = send(block, 0, 2, 0)
    factor = 1.0 / math.sqrt(4 * 16 * 2 * inputs.shape[1] * inputs.shape[2] * inputs.shape[3])
    weight_grad = call(functools.partial(finish_kernel, factor=factor), shaped((4, 4, 4, 32, 64), F32))(
        block, near, send(block, 0, 1, 0), send(near, 0, 1, 0)
    )
    return up.reshape(2, 2, 2, 32, 4, 8, 128), grad, weight_grad.transpose(0, 1, 2, 4, 3)


def solution(mesh):
    placed = (P(None, "gx", "gy", "gz"), P(), P(None, None, None, None, "gx", "gy", "gz"))
    return jax.shard_map(
        body,
        mesh=mesh,
        in_specs=placed,
        out_specs=(P(None, None, None, None, "gx", "gy", "gz"), P(None, "gx", "gy", "gz"), P()),
        check_vma=False,
    )
```

time: 362 us -> 101 us (0.28); the launches traced: 357 us -> 101 us
  matrix products: 120 us -> 0 us
  waiting for transfers between devices: 131 us -> 11 us
  local copies, waits for them, and re-layouts: 57.8 us -> 4.75 us
  Pallas kernels: 0 us -> 46.9 us
  starting transfers between devices: 18.5 us -> 33.9 us
  between operations: 15.3 us -> 0.86 us
  other arithmetic: 14.5 us -> 3.51 us
    psum x1 -> x0, waiting for transfers between devices: 124 us -> none  [body(): total_grad = lax.psum(local_grad, ('gx', 'gy', 'gz'))]
    dot_general x192 -> x0, matrix products: 120 us -> none  [the longest x64 71.6 us: body(): jnp.einsum('io,oxyz->ixyz', weight[tap_x, tap_y, tap_z], window, preferre...]
    pallas_call x0 -> x11, Pallas kernels: none -> 46.9 us  [the longest x10 42.7 us: run(): pl.pallas_call(kernel, out_shape=out_shape, in_specs=[WHOLE] * len(operan...]
    unnamed x132 -> x38, local copies, waits for them, and re-layouts: 24.3 us -> 3.66 us
    slice x10 -> x0, local copies, waits for them, and re-layouts: 17.8 us -> none  [the longest x6 10.5 us: extended_2(): lax.slice_in_dim(cells, cells.shape[dim] - width, cells.shape[dim], axis=...]
    ppermute x12 -> x20, starting transfers between devices: 18.5 us -> 33.9 us  [the longest x10 20 us: send(): return lax.ppermute(block, AXES, xor_pairs(*flip))]
    ppermute x4 -> x0, local copies, waits for them, and re-layouts: 12.9 us -> none  [the longest x2 6.53 us: extended_2(): lax.ppermute(head, axis, [((i + 1) % count, i) for i in range(count)])]
    select_n x2 -> x1, other arithmetic: 11.5 us -> 0.02 us  [body(): jnp.where(low, block[half:], block[:half])]
  transfers between devices with their start and end apart: 13 -> 20, of which waited for: 6 -> 5; matrix products, arithmetic and copies ran while one was open for 19% -> 4% of each run, Pallas kernels for 0% -> 42%
where the time goes in v1:
time: 101 us
  Pallas kernels  46.9 us (46%)
  starting transfers between devices  33.9 us (34%)
  waiting for transfers between devices  11 us (11%)
  local copies, waits for them, and re-layouts  4.75 us (5%)
  other arithmetic  3.51 us (3%)
    pallas_call x10, Pallas kernels, run(): pl.pallas_call(kernel, out_shape=out_shape, in_specs=[WHOLE] * len(operan...  42.7 us
    ppermute x10, starting transfers between devices, send(): return lax.ppermute(block, AXES, xor_pairs(*flip))  20 us
    ppermute x1, waiting for transfers between devices, body(): lax.ppermute(jnp.concatenate([cot[0, :128], z_cot[0, :128]], axis=1), 'gx...  6.03 us
    pallas_call x1, Pallas kernels, body(): pl.pallas_call(prepare_cot_kernel, grid=(4,), out_shape=(shaped((4, 256,...  4.2 us
    unnamed x38, local copies, waits for them, and re-layouts  3.66 us
    ppermute x10, waiting for transfers between devices, send(): return lax.ppermute(block, AXES, xor_pairs(*flip))  3.24 us
    concatenate x2, other arithmetic, join(): return (jnp.concatenate([a, b], axis=2), jnp.concatenate([c, d], axis=1))  2.34 us
    ppermute x1, starting transfers between devices, body(): inner = lax.ppermute(inner, 'gy', INNER)  2.27 us
  transfers between devices with their start and end apart: 20, of which 5 were waited for; matrix products, arithmetic and copies ran while one was open for 4% of the time, Pallas kernels for 42%

profile of v1, /device:TPU:1, one launch (start us, length us, event | category | flops | bytes accessed | tf_op | source)
XLA Modules:
  0.0 100.9 jit_solution(12897221794269733983)
XLA Ops:
  0.6 2.1 %shard_map.58 = (bf16[4,64,1024]{2,1,0:T(8,128)(2,1)}, bf16[4,64,128]{2,1,0:T(8,128)(2,1)}) custom-call(bf16[64,4,8,128]{3,2,1,0:T(8,128)(2,1)} %raw.1), custom_call_target="tpu_custom_call" | custom-call | bytes 1114112 | tf_op jit(solution)/shard_map/pallas_call | solution.py:26
  2.8 2.0 %collective-permute-start = (bf16[4,64,128]{2,1,0:T(8,128)(2,1)}, bf16[4,64,128]{2,1,0:T(8,128)(2,1)S(1)}, u32[]{:S(2)}, u32[]{:S(2)}) collective-permute-start(bf16[4,64,128]{2,1,0:T(8,128)(2,1)} %get-tuple-element.75), channel_id=1, source_target_pairs={{0,1},{1,0},{2,3},{3,2},{4,5},{5,4},{6,7},{7,6},{8,9},{9,8},{10,11... | collective-permute-start | bytes 196616 | tf_op jit(solution)/shard_map/ppermute | solution.py:328
  4.8 4.2 %shard_map.60 = (bf16[4,256,1024]{2,1,0:T(8,128)(2,1)}, bf16[4,256,128]{2,1,0:T(8,128)(2,1)}) custom-call(bf16[8,32,4,8,128]{4,3,2,1,0:T(8,128)(2,1)} %bitcast.20), custom_call_target="tpu_custom_call" | custom-call | tf_op jit(solution)/shard_map/pallas_call | solution.py:329
  9.2 1.6 %collective-permute-start.1 = (bf16[64,1152]{1,0:T(8,128)(2,1)S(1)}, bf16[64,1152]{1,0:T(8,128)(2,1)S(1)}, u32[]{:S(2)}, u32[]{:S(2)}) collective-permute-start(bf16[64,1152]{1,0:T(8,128)(2,1)S(1)} %pad_maximum_fusion.4), channel_id=1, source_target_pairs={{0,32},{32,64},{64,96},{96,0},{1,33},{33,65},{65,97},{97,1},{2,34}... | collective-permute-start | bytes 442376 | tf_op jit(solution)/shard_map/ppermute | solution.py:338
  10.7 1.5 %collective-permute-start.2 = (bf16[64,1152]{1,0:T(8,128)(2,1)S(1)}, bf16[64,1152]{1,0:T(8,128)(2,1)S(1)}, u32[]{:S(2)}, u32[]{:S(2)}) collective-permute-start(bf16[64,1152]{1,0:T(8,128)(2,1)S(1)} %pad_maximum_fusion.5), channel_id=1, source_target_pairs={{0,96},{32,0},{64,32},{96,64},{1,97},{33,1},{65,33},{97,65},{2,98}... | collective-permute-start | bytes 442376 | tf_op jit(solution)/shard_map/ppermute | solution.py:339
  16.0 2.2 %shard_map.59 = (bf16[7,64,128]{2,1,0:T(8,128)(2,1)}, bf16[7,64,128]{2,1,0:T(8,128)(2,1)}) custom-call(bf16[4,64,1024]{2,1,0:T(8,128)(2,1)} %get-tuple-element.101.own, bf16[64,1152]{1,0:T(8,128)(2,1)} %copy-done.9, bf16[64,1152]{1,0:T(8,128)(2,1)} %copy-done.10, bf16[4,64,128]{2,1,0:T(8,128)(2,1)} %copy-done.11), custom_call_target="tpu_custom_call" | custom-call | bytes 1114112 | tf_op jit(solution)/shard_map/pallas_call | solution.py:26
  18.2 2.3 %collective-permute-start.3 = (bf16[7,64,128]{2,1,0:T(8,128)(2,1)}, bf16[7,64,128]{2,1,0:T(8,128)(2,1)S(1)}, u32[]{:S(2)}, u32[]{:S(2)}) collective-permute-start(bf16[7,64,128]{2,1,0:T(8,128)(2,1)} %get-tuple-element.76), channel_id=1, source_target_pairs={{0,2},{2,0},{4,6},{6,4},{8,10},{10,8},{12,14},{14,12},{16,18},{18,... | collective-permute-start | bytes 344072 | tf_op jit(solution)/shard_map/ppermute | solution.py:345
  20.5 1.6 %collective-permute-start.4 = (bf16[7,64,128]{2,1,0:T(8,128)(2,1)}, bf16[7,64,128]{2,1,0:T(8,128)(2,1)S(1)}, u32[]{:S(2)}, u32[]{:S(2)}) collective-permute-start(bf16[7,64,128]{2,1,0:T(8,128)(2,1)} %get-tuple-element.77), channel_id=1, source_target_pairs={{0,30},{2,4},{4,2},{6,8},{8,6},{10,12},{12,10},{14,16},{16,14},{18... | collective-permute-start | bytes 344072 | tf_op jit(solution)/shard_map/ppermute | solution.py:344
  22.0 6.9 %shard_map.61.pay = f32[1024,128]{1,0:T(8,128)} custom-call(bf16[4,64,1024]{2,1,0:T(8,128)(2,1)} %get-tuple-element.101.own, bf16[64,1152]{1,0:T(8,128)(2,1)} %copy-done.9, bf16[64,1152]{1,0:T(8,128)(2,1)} %copy-done.10, bf16[4,64,128]{2,1,0:T(8,128)(2,1)} %copy-done.11, bf16[4,256,1024]{2,1,0:T(8,128)(2,1)} %get-tuple-element.123.cot.own), custom_call_target="tpu_custom_call" | custom-call | flops 3623878656 | bytes 3506176 | tf_op jit(solution)/shard_map/pallas_call | solution.py:26
  31.5 3.4 %shard_map.62 = (f32[512,128]{1,0:T(8,128)}, f32[512,128]{1,0:T(8,128)}) custom-call(bf16[7,64,128]{2,1,0:T(8,128)(2,1)} %copy-done.15, bf16[7,64,128]{2,1,0:T(8,128)(2,1)} %copy-done.16, bf16[4,256,1024]{2,1,0:T(8,128)(2,1)} %get-tuple-element.123.cot.own, f32[1024,128]{1,0:T(8,128)} %shard_map.61.pay), custom_call_target="tpu_custom_call" | custom-call | flops 301989888 | bytes 3375104 | tf_op jit(solution)/shard_map/pallas_call | solution.py:26
  34.9 5.4 %collective-permute-start.5 = (f32[512,128]{1,0:T(8,128)}, f32[512,128]{1,0:T(8,128)S(1)}, u32[]{:S(2)}, u32[]{:S(2)}) collective-permute-start(f32[512,128]{1,0:T(8,128)} %get-tuple-element.80), channel_id=1, source_target_pairs={{0,2},{1,3},{2,0},{3,1},{4,6},{5,7},{6,4},{7,5},{8,10},{9,11},{10,... | collective-permute-start | bytes 786440 | tf_op jit(solution)/shard_map/ppermute | solution.py:312
  40.3 1.6 %collective-permute-start.8 = (bf16[128,1152]{1,0:T(8,128)(2,1)S(1)}, bf16[128,1152]{1,0:T(8,128)(2,1)S(1)}, u32[]{:S(2)}, u32[]{:S(2)}) collective-permute-start(bf16[128,1152]{1,0:T(8,128)(2,1)S(1)} %pad_maximum_fusion.3), channel_id=1, source_target_pairs={{0,96},{32,0},{64,32},{96,64},{1,97},{33,1},{65,33},{97,65},{2,98}... | collective-permute-start | bytes 884744 | tf_op jit(solution)/shard_map/ppermute | solution.py:341
  43.0 6.0 %collective-permute-done.8.right = bf16[128,1152]{1,0:T(8,128)(2,1)S(1)} collective-permute-done((bf16[128,1152]{1,0:T(8,128)(2,1)S(1)}, bf16[128,1152]{1,0:T(8,128)(2,1)S(1)}, u32[]{:S(2)}, u32[]{:S(2)}) %collective-permute-start.8) | collective-permute-done | bytes 294944 | tf_op jit(solution)/shard_map/ppermute | solution.py:341
  49.8 3.5 %shard_map.63 = (bf16[11,64,128]{2,1,0:T(8,128)(2,1)}, bf16[11,64,128]{2,1,0:T(8,128)(2,1)}) custom-call(bf16[4,256,1024]{2,1,0:T(8,128)(2,1)} %get-tuple-element.123.cot.own, bf16[128,1152]{1,0:T(8,128)(2,1)} %copy-done.5, bf16[128,1152]{1,0:T(8,128)(2,1)} %copy-done.6, bf16[4,256,128]{2,1,0:T(8,128)(2,1)} %copy-done.4), custom_call_target="tpu_custom_call" | custom-call | bytes 3309568 | tf_op jit(solution)/shard_map/pallas_call | solution.py:26
  53.4 1.8 %collective-permute-start.12 = (bf16[11,64,128]{2,1,0:T(8,128)(2,1)}, bf16[11,64,128]{2,1,0:T(8,128)(2,1)S(1)}, u32[]{:S(2)}, u32[]{:S(2)}) collective-permute-start(bf16[11,64,128]{2,1,0:T(8,128)(2,1)} %get-tuple-element.110), channel_id=1, source_target_pairs={{0,2},{2,0},{4,6},{6,4},{8,10},{10,8},{12,14},{14,12},{16,18},{18,... | collective-permute-start | bytes 540680 | tf_op jit(solution)/shard_map/ppermute | solution.py:380
  55.4 5.3 %shard_map.64 = bf16[8,32,2,8,128]{4,3,2,1,0:T(8,128)(2,1)} custom-call(bf16[4,64,1024]{2,1,0:T(8,128)(2,1)} %get-tuple-element.101.own, bf16[64,1152]{1,0:T(8,128)(2,1)} %copy-done.9, bf16[64,1152]{1,0:T(8,128)(2,1)} %copy-done.10, bf16[4,64,128]{2,1,0:T(8,128)(2,1)} %copy-done.11, bf16[7,64,128]{2,1,0:T(8,128)(2,1)} %copy-done.15, ...), custom_call_target="tpu_custom_call" | custom-call | flops 1811939328 | bytes 2424832 | tf_op jit(solution)/shard_map/pallas_call | solution.py:26
  61.7 5.2 %shard_map.65 = bf16[8,32,2,8,128]{4,3,2,1,0:T(8,128)(2,1)} custom-call(bf16[4,64,1024]{2,1,0:T(8,128)(2,1)} %get-tuple-element.101.own, bf16[64,1152]{1,0:T(8,128)(2,1)} %copy-done.9, bf16[64,1152]{1,0:T(8,128)(2,1)} %copy-done.10, bf16[4,64,128]{2,1,0:T(8,128)(2,1)} %copy-done.11, bf16[7,64,128]{2,1,0:T(8,128)(2,1)} %copy-done.15, ...), custom_call_target="tpu_custom_call" | custom-call | flops 1811939328 | bytes 2424832 | tf_op jit(solution)/shard_map/pallas_call | solution.py:26
  67.0 1.9 %collective-permute-start.14 = (f32[256,128]{1,0:T(8,128)S(1)}, f32[256,128]{1,0:T(8,128)S(1)}, u32[]{:S(2)}, u32[]{:S(2)}) collective-permute-start(f32[256,128]{1,0:T(8,128)S(1)} %add.26), channel_id=1, source_target_pairs={{0,96},{1,97},{2,98},{3,99},{4,100},{5,101},{6,102},{7,103},{8,104... | collective-permute-start | bytes 393224 | tf_op jit(solution)/shard_map/ppermute | solution.py:312
  69.0 5.7 %shard_map.66 = bf16[64,2,8,128]{3,2,1,0:T(8,128)(2,1)} custom-call(bf16[4,256,1024]{2,1,0:T(8,128)(2,1)} %get-tuple-element.123.cot.own, bf16[128,1152]{1,0:T(8,128)(2,1)} %copy-done.5, bf16[128,1152]{1,0:T(8,128)(2,1)} %copy-done.6, bf16[4,256,128]{2,1,0:T(8,128)(2,1)} %copy-done.4, bf16[11,64,128]{2,1,0:T(8,128)(2,1)} %copy-done.17, ...), custom_call_target="tpu_custom_call" | custom-call | flops 2147483648 | bytes 3833856 | tf_op jit(solution)/shard_map/pallas_call | solution.py:26
  75.1 5.9 %shard_map.67 = bf16[64,2,8,128]{3,2,1,0:T(8,128)(2,1)} custom-call(bf16[4,256,1024]{2,1,0:T(8,128)(2,1)} %get-tuple-element.123.cot.own, bf16[128,1152]{1,0:T(8,128)(2,1)} %copy-done.5, bf16[128,1152]{1,0:T(8,128)(2,1)} %copy-done.6, bf16[4,256,128]{2,1,0:T(8,128)(2,1)} %copy-done.4, bf16[11,64,128]{2,1,0:T(8,128)(2,1)} %copy-done.17, ...), custom_call_target="tpu_custom_call" | custom-call | flops 2147483648 | bytes 3833856 | tf_op jit(solution)/shard_map/pallas_call | solution.py:26
  84.0 2.2 %collective-permute-done.16 = f32[256,128]{1,0:T(8,128)S(1)} collective-permute-done((f32[256,128]{1,0:T(8,128)S(1)}, f32[256,128]{1,0:T(8,128)S(1)}, u32[]{:S(2)}, u32[]{:S(2)}) %collective-permute-start.16) | collective-permute-done | bytes 131104 | tf_op jit(solution)/shard_map/ppermute | solution.py:312
  87.6 4.3 %collective-permute-start.18 = (f32[256,128]{1,0:T(8,128)S(1)}, f32[256,128]{1,0:T(8,128)S(1)}, u32[]{:S(2)}, u32[]{:S(2)}) collective-permute-start(f32[256,128]{1,0:T(8,128)S(1)} %add.29.mine), channel_id=1, source_target_pairs={{0,2},{1,3},{2,0},{3,1},{4,6},{5,7},{6,4},{7,5},{8,10},{9,11},{10,... | collective-permute-start | bytes 393224 | tf_op jit(solution)/shard_map/ppermute | solution.py:312
  91.9 4.9 %collective-permute-start.19 = (f32[256,128]{1,0:T(8,128)S(1)}, f32[256,128]{1,0:T(8,128)S(1)}, u32[]{:S(2)}, u32[]{:S(2)}) collective-permute-start(f32[256,128]{1,0:T(8,128)S(1)} %collective-permute-done.17.beside), channel_id=1, source_target_pairs={{0,2},{1,3},{2,0},{3,1},{4,6},{5,7},{6,4},{7,5},{8,10},{9,11},{10,... | collective-permute-start | bytes 393224 | tf_op jit(solution)/shard_map/ppermute | solution.py:312
  98.5 2.4 %shard_map.68 = f32[4,4,4,32,64]{4,3,2,1,0:T(8,128)} custom-call(f32[256,128]{1,0:T(8,128)} %copy-done.3, f32[256,128]{1,0:T(8,128)} %copy-done.12, f32[256,128]{1,0:T(8,128)} %copy-done.13, f32[256,128]{1,0:T(8,128)} %copy-done.14), custom_call_target="tpu_custom_call" | custom-call | bytes 1048576 | tf_op jit(solution)/shard_map/pallas_call | solution.py:26
  (83 shorter events, 16.1 us)
Async XLA Ops:
  2.8 6.3 %collective-permute-start = (bf16[4,64,128]{2,1,0:T(8,128)(2,1)}, bf16[4,64,128]{2,1,0:T(8,128)(2,1)S(1)}, u32[]{:S(2)}, u32[]{:S(2)}) collective-permute-start(bf16[4,64,128]{2,1,0:T(8,128)(2,1)} %get-tuple-element.75), channel_id=1, source_target_pairs={{0,1},{1,0},{2,3},{3,2},{4,5},{5,4},{6,7},{7,6},{8,9},{9,8},{10,11... | collective-permute-start | bytes 196616 | tf_op jit(solution)/shard_map/ppermute | solution.py:328
  9.0 20.0 %collective-permute-start.6 = (bf16[4,256,128]{2,1,0:T(8,128)(2,1)}, bf16[4,256,128]{2,1,0:T(8,128)(2,1)S(1)}, u32[]{:S(2)}, u32[]{:S(2)}) collective-permute-start(bf16[4,256,128]{2,1,0:T(8,128)(2,1)} %get-tuple-element.81), channel_id=1, source_target_pairs={{0,1},{1,0},{2,3},{3,2},{4,5},{5,4},{6,7},{7,6},{8,9},{9,8},{10,11... | collective-permute-start | bytes 786440 | tf_op jit(solution)/shard_map/ppermute | solution.py:337
  9.2 5.5 %collective-permute-start.1 = (bf16[64,1152]{1,0:T(8,128)(2,1)S(1)}, bf16[64,1152]{1,0:T(8,128)(2,1)S(1)}, u32[]{:S(2)}, u32[]{:S(2)}) collective-permute-start(bf16[64,1152]{1,0:T(8,128)(2,1)S(1)} %pad_maximum_fusion.4), channel_id=1, source_target_pairs={{0,32},{32,64},{64,96},{96,0},{1,33},{33,65},{65,97},{97,1},{2,34}... | collective-permute-start | bytes 442376 | tf_op jit(solution)/shard_map/ppermute | solution.py:338
  10.7 4.4 %collective-permute-start.2 = (bf16[64,1152]{1,0:T(8,128)(2,1)S(1)}, bf16[64,1152]{1,0:T(8,128)(2,1)S(1)}, u32[]{:S(2)}, u32[]{:S(2)}) collective-permute-start(bf16[64,1152]{1,0:T(8,128)(2,1)S(1)} %pad_maximum_fusion.5), channel_id=1, source_target_pairs={{0,96},{32,0},{64,32},{96,64},{1,97},{33,1},{65,33},{97,65},{2,98}... | collective-permute-start | bytes 442376 | tf_op jit(solution)/shard_map/ppermute | solution.py:339
  18.2 12.0 %collective-permute-start.3 = (bf16[7,64,128]{2,1,0:T(8,128)(2,1)}, bf16[7,64,128]{2,1,0:T(8,128)(2,1)S(1)}, u32[]{:S(2)}, u32[]{:S(2)}) collective-permute-start(bf16[7,64,128]{2,1,0:T(8,128)(2,1)} %get-tuple-element.76), channel_id=1, source_target_pairs={{0,2},{2,0},{4,6},{6,4},{8,10},{10,8},{12,14},{14,12},{16,18},{18,... | collective-permute-start | bytes 344072 | tf_op jit(solution)/shard_map/ppermute | solution.py:345
  20.5 9.7 %collective-permute-start.4 = (bf16[7,64,128]{2,1,0:T(8,128)(2,1)}, bf16[7,64,128]{2,1,0:T(8,128)(2,1)S(1)}, u32[]{:S(2)}, u32[]{:S(2)}) collective-permute-start(bf16[7,64,128]{2,1,0:T(8,128)(2,1)} %get-tuple-element.77), channel_id=1, source_target_pairs={{0,30},{2,4},{4,2},{6,8},{8,6},{10,12},{12,10},{14,16},{16,14},{18... | collective-permute-start | bytes 344072 | tf_op jit(solution)/shard_map/ppermute | solution.py:344
  29.0 13.0 %copy-start.4 = (bf16[4,256,128]{2,1,0:T(8,128)(2,1)}, bf16[4,256,128]{2,1,0:T(8,128)(2,1)S(1)}, u32[]{:S(2)}) copy-start(bf16[4,256,128]{2,1,0:T(8,128)(2,1)S(1)} %collective-permute-done.6.z_own) | copy-start | bytes 786436
  29.0 14.0 %collective-permute-start.7 = (bf16[128,1152]{1,0:T(8,128)(2,1)S(1)}, bf16[128,1152]{1,0:T(8,128)(2,1)S(1)}, u32[]{:S(2)}, u32[]{:S(2)}) collective-permute-start(bf16[128,1152]{1,0:T(8,128)(2,1)S(1)} %pad_maximum_fusion.2), channel_id=1, source_target_pairs={{0,32},{32,64},{64,96},{96,0},{1,33},{33,65},{65,97},{97,1},{2,34}... | collective-permute-start | bytes 884744 | tf_op jit(solution)/shard_map/ppermute | solution.py:340
  34.9 7.1 %collective-permute-start.5 = (f32[512,128]{1,0:T(8,128)}, f32[512,128]{1,0:T(8,128)S(1)}, u32[]{:S(2)}, u32[]{:S(2)}) collective-permute-start(f32[512,128]{1,0:T(8,128)} %get-tuple-element.80), channel_id=1, source_target_pairs={{0,2},{1,3},{2,0},{3,1},{4,6},{5,7},{6,4},{7,5},{8,10},{9,11},{10,... | collective-permute-start | bytes 786440 | tf_op jit(solution)/shard_map/ppermute | solution.py:312
  40.3 8.7 %collective-permute-start.8 = (bf16[128,1152]{1,0:T(8,128)(2,1)S(1)}, bf16[128,1152]{1,0:T(8,128)(2,1)S(1)}, u32[]{:S(2)}, u32[]{:S(2)}) collective-permute-start(bf16[128,1152]{1,0:T(8,128)(2,1)S(1)} %pad_maximum_fusion.3), channel_id=1, source_target_pairs={{0,96},{32,0},{64,32},{96,64},{1,97},{33,1},{65,33},{97,65},{2,98}... | collective-permute-start | bytes 884744 | tf_op jit(solution)/shard_map/ppermute | solution.py:341
  49.0 4.2 %collective-permute-start.9 = (f32[256,128]{1,0:T(8,128)S(1)}, f32[256,128]{1,0:T(8,128)S(1)}, u32[]{:S(2)}, u32[]{:S(2)}) collective-permute-start(f32[256,128]{1,0:T(8,128)S(1)} %slice_select_fusion), channel_id=1, source_target_pairs={{0,4},{1,5},{2,6},{3,7},{4,0},{5,1},{6,2},{7,3},{8,12},{9,13},{10,... | collective-permute-start | bytes 393224 | tf_op jit(solution)/shard_map/ppermute | solution.py:312
  53.3 7.3 %collective-permute-start.10 = (f32[256,128]{1,0:T(8,128)S(1)}, f32[256,128]{1,0:T(8,128)S(1)}, u32[]{:S(2)}, u32[]{:S(2)}) collective-permute-start(f32[256,128]{1,0:T(8,128)S(1)} %select_add_fusion), channel_id=1, source_target_pairs={{0,12},{1,13},{2,14},{3,15},{4,8},{5,9},{6,10},{7,11},{8,4},{9,5},... | collective-permute-start | bytes 393224 | tf_op jit(solution)/shard_map/ppermute | solution.py:312
  53.4 13.6 %collective-permute-start.12 = (bf16[11,64,128]{2,1,0:T(8,128)(2,1)}, bf16[11,64,128]{2,1,0:T(8,128)(2,1)S(1)}, u32[]{:S(2)}, u32[]{:S(2)}) collective-permute-start(bf16[11,64,128]{2,1,0:T(8,128)(2,1)} %get-tuple-element.110), channel_id=1, source_target_pairs={{0,2},{2,0},{4,6},{6,4},{8,10},{10,8},{12,14},{14,12},{16,18},{18,... | collective-permute-start | bytes 540680 | tf_op jit(solution)/shard_map/ppermute | solution.py:380
  55.1 11.9 %collective-permute-start.13 = (bf16[11,64,128]{2,1,0:T(8,128)(2,1)}, bf16[11,64,128]{2,1,0:T(8,128)(2,1)S(1)}, u32[]{:S(2)}, u32[]{:S(2)}) collective-permute-start(bf16[11,64,128]{2,1,0:T(8,128)(2,1)} %get-tuple-element.111), channel_id=1, source_target_pairs={{0,30},{2,4},{4,2},{6,8},{8,6},{10,12},{12,10},{14,16},{16,14},{18... | collective-permute-start | bytes 540680 | tf_op jit(solution)/shard_map/ppermute | solution.py:379
  60.7 6.3 %collective-permute-start.11 = (f32[256,128]{1,0:T(8,128)S(1)}, f32[256,128]{1,0:T(8,128)S(1)}, u32[]{:S(2)}, u32[]{:S(2)}) collective-permute-start(f32[256,128]{1,0:T(8,128)S(1)} %add.25), channel_id=1, source_target_pairs={{0,32},{1,33},{2,34},{3,35},{4,36},{5,37},{6,38},{7,39},{8,40},{9,... | collective-permute-start | bytes 393224 | tf_op jit(solution)/shard_map/ppermute | solution.py:312
  67.0 7.6 %collective-permute-start.14 = (f32[256,128]{1,0:T(8,128)S(1)}, f32[256,128]{1,0:T(8,128)S(1)}, u32[]{:S(2)}, u32[]{:S(2)}) collective-permute-start(f32[256,128]{1,0:T(8,128)S(1)} %add.26), channel_id=1, source_target_pairs={{0,96},{1,97},{2,98},{3,99},{4,100},{5,101},{6,102},{7,103},{8,104... | collective-permute-start | bytes 393224 | tf_op jit(solution)/shard_map/ppermute | solution.py:312
  74.7 6.9 %copy-start.1 = (bf16[8,32,2,8,128]{4,3,2,1,0:T(8,128)(2,1)S(1)}, bf16[8,32,2,8,128]{4,3,2,1,0:T(8,128)(2,1)}, u32[]{:S(2)}) copy-start(bf16[8,32,2,8,128]{4,3,2,1,0:T(8,128)(2,1)} %shard_map.64) | copy-start | bytes 3145732
  74.7 6.9 %copy-start.2 = (bf16[8,32,2,8,128]{4,3,2,1,0:T(8,128)(2,1)S(1)}, bf16[8,32,2,8,128]{4,3,2,1,0:T(8,128)(2,1)}, u32[]{:S(2)}) copy-start(bf16[8,32,2,8,128]{4,3,2,1,0:T(8,128)(2,1)} %shard_map.65) | copy-start | bytes 3145732
  74.7 6.3 %collective-permute-start.15 = (f32[256,128]{1,0:T(8,128)S(1)}, f32[256,128]{1,0:T(8,128)S(1)}, u32[]{:S(2)}, u32[]{:S(2)}) collective-permute-start(f32[256,128]{1,0:T(8,128)S(1)} %add.27), channel_id=1, source_target_pairs={{0,1},{1,0},{2,3},{3,2},{4,5},{5,4},{6,7},{7,6},{8,9},{9,8},{10,11... | collective-permute-start | bytes 393224 | tf_op jit(solution)/shard_map/ppermute | solution.py:312
  81.1 5.1 %collective-permute-start.16 = (f32[256,128]{1,0:T(8,128)S(1)}, f32[256,128]{1,0:T(8,128)S(1)}, u32[]{:S(2)}, u32[]{:S(2)}) collective-permute-start(f32[256,128]{1,0:T(8,128)S(1)} %add.28), channel_id=1, source_target_pairs={{0,17},{1,16},{2,19},{3,18},{4,21},{5,20},{6,23},{7,22},{8,25},{9,... | collective-permute-start | bytes 393224 | tf_op jit(solution)/shard_map/ppermute | solution.py:312
  86.2 11.6 %copy-start.3 = (f32[256,128]{1,0:T(8,128)}, f32[256,128]{1,0:T(8,128)S(1)}, u32[]{:S(2)}) copy-start(f32[256,128]{1,0:T(8,128)S(1)} %add.29.mine) | copy-start | bytes 393220
  86.2 5.8 %collective-permute-start.17 = (f32[256,128]{1,0:T(8,128)S(1)}, f32[256,128]{1,0:T(8,128)S(1)}, u32[]{:S(2)}, u32[]{:S(2)}) collective-permute-start(f32[256,128]{1,0:T(8,128)S(1)} %add.29.mine), channel_id=1, source_target_pairs={{0,4},{1,5},{2,6},{3,7},{4,0},{5,1},{6,2},{7,3},{8,12},{9,13},{10,... | collective-permute-start | bytes 393224 | tf_op jit(solution)/shard_map/ppermute | solution.py:312
  87.6 9.2 %collective-permute-start.18 = (f32[256,128]{1,0:T(8,128)S(1)}, f32[256,128]{1,0:T(8,128)S(1)}, u32[]{:S(2)}, u32[]{:S(2)}) collective-permute-start(f32[256,128]{1,0:T(8,128)S(1)} %add.29.mine), channel_id=1, source_target_pairs={{0,2},{1,3},{2,0},{3,1},{4,6},{5,7},{6,4},{7,5},{8,10},{9,11},{10,... | collective-permute-start | bytes 393224 | tf_op jit(solution)/shard_map/ppermute | solution.py:312
  91.9 5.9 %collective-permute-start.19 = (f32[256,128]{1,0:T(8,128)S(1)}, f32[256,128]{1,0:T(8,128)S(1)}, u32[]{:S(2)}, u32[]{:S(2)}) collective-permute-start(f32[256,128]{1,0:T(8,128)S(1)} %collective-permute-done.17.beside), channel_id=1, source_target_pairs={{0,2},{1,3},{2,0},{3,1},{4,6},{5,7},{6,4},{7,5},{8,10},{9,11},{10,... | collective-permute-start | bytes 393224 | tf_op jit(solution)/shard_map/ppermute | solution.py:312
  (15 other events, 37.3 us)

commit v2 on v1

v2 whole, which is shorter than its diff:
```python
import functools
import math

import jax
import jax.numpy as jnp
from jax import lax
from jax.experimental import pallas as pl
from jax.experimental.pallas import tpu as pltpu
from jax.sharding import PartitionSpec as P

AXES = ("gx", "gy", "gz")
F32, BF16 = jnp.float32, jnp.bfloat16
NT = (((1,), (1,)), ((), ()))
NN = (((1,), (0,)), ((), ()))
PARAMS = pltpu.CompilerParams(vmem_limit_bytes=24 * 1024 * 1024)
WHOLE = pl.BlockSpec(memory_space=pltpu.VMEM)
FAR = pl.BlockSpec(memory_space=pltpu.HBM)


def shaped(shape, dtype=BF16):
    return pltpu.VMEM(shape, dtype)


def call(kernel, out_shape, scratch=(), flops=0, far=(), aliases=None):
    def run(*operands):
        moved = sum(math.prod(o.shape) * o.dtype.itemsize for o in (*operands, *jax.tree.leaves(out_shape)))
        return pl.pallas_call(
            kernel,
            out_shape=out_shape,
            in_specs=[FAR if n in far else WHOLE for n in range(len(operands))],
            out_specs=jax.tree.map(lambda o: FAR if isinstance(o, jax.ShapeDtypeStruct) else WHOLE, out_shape),
            scratch_shapes=list(scratch),
            compiler_params=PARAMS,
            input_output_aliases=aliases or {},
            cost_estimate=pl.CostEstimate(flops=flops, bytes_accessed=moved, transcendentals=0),
        )(*[pltpu.with_memory_space_constraint(o, pltpu.HBM if n in far else pltpu.VMEM) for n, o in enumerate(operands)])

    return run


def rolled(tile, column, before):
    lane = lax.broadcasted_iota(jnp.int32, tile.shape, 1)
    inside = lax.axis_index("gz") == (1 if before else 0)
    edge = jnp.where(inside, column.astype(F32), jnp.zeros(column.shape, F32))
    moved = pltpu.roll(tile, 1 if before else 127, 1).astype(F32)
    return jnp.where(lane == (0 if before else 127), edge, moved).astype(tile.dtype)


def plane_of(xe, own, left, right, low, high, z_all):
    if xe == 0 or xe == 5:
        plane, lane = (left, 1310) if xe == 0 else (right, 1280)
        return lambda ye: (plane[:, ye * 128 : ye * 128 + 128], plane[:, lane + ye : lane + ye + 1])

    def at(ye):
        column = z_all[:, xe * 10 - 10 + ye : xe * 10 - 9 + ye]
        if ye == 0 or ye == 9:
            return (low if ye == 0 else high)[xe - 1], column
        return own[xe - 1, :, ye * 128 - 128 : ye * 128], column

    return at


def xor_pairs(fx, fy, fz):
    pairs = []
    for gx in range(4):
        for gy in range(16):
            for gz in range(2):
                pairs.append(((gx * 16 + gy) * 2 + gz, ((gx ^ fx) * 16 + (gy ^ fy)) * 2 + (gz ^ fz)))
    return pairs


def ring(count, step):
    return [(i, (i + step) % count) for i in range(count)]


OUTER = [(i, (i - 1) % 16 if i % 2 == 0 else (i + 1) % 16) for i in range(16)]
INNER = [(i, i ^ 1) for i in range(16)]


def first_core():
    return lax.rem(lax.axis_index("gy"), 2) == 0


def low_and_high(inner, outer, n):
    a, b, first = inner[n], outer[n], first_core()
    return jnp.where(first, b, a), jnp.where(first, a, b)


def side_picker(x):
    cell = lax.broadcasted_iota(jnp.int32, (1024, 128), 0)
    lane = lax.broadcasted_iota(jnp.int32, (1024, 128), 1)
    side = jnp.where(lax.axis_index("gz") == 0, 127, 0)
    return (cell == (lane - 10 * x - 1) * 128 + side).astype(F32).astype(BF16)


def prepare_in_kernel(raw, own, z_face, inner, outer, arrived, sems):
    copies = [pltpu.make_async_copy(raw.at[16 * n : 16 * n + 16], arrived.at[16 * n : 16 * n + 16], sems.at[n]) for n in range(4)]
    for copy in copies:
        copy.start()
    for copy in copies:
        copy.wait()
    faces = jnp.zeros((64, 128), F32)
    for x in range(4):
        plane = arrived[:, x].reshape(64, 1024)
        own[x] = plane
        low, high = plane[:, 0:128], plane[:, 896:1024]
        inner[x] = jnp.where(first_core(), high, low)
        outer[x] = jnp.where(first_core(), low, high)
        faces += jnp.dot(plane, side_picker(x), preferred_element_type=F32)
    z_face[...] = faces.astype(BF16)


def prepare_cot_kernel(raw, cot, z_face, inner, outer, arrived, sems):
    copies = [pltpu.make_async_copy(raw.at[n], arrived.at[n], sems.at[n]) for n in range(8)]
    for copy in copies:
        copy.start()
    for n in range(8):
        copies[n].wait()
        for x in range(4):
            cot[x, n * 32 : n * 32 + 32, :] = arrived[n, :, x].reshape(32, 1024)
    faces = jnp.zeros((256, 128), F32)
    for x in range(4):
        faces += jnp.dot(cot[x], side_picker(x), preferred_element_type=F32)
        for px in range(2):
            row = px * 128
            low, high = cot[x, row : row + 64, 0:128], cot[x, row + 64 : row + 128, 896:1024]
            inner[x, px * 64 : px * 64 + 64, :] = jnp.where(first_core(), high, low)
            outer[x, px * 64 : px * 64 + 64, :] = jnp.where(first_core(), low, high)
    odd = lax.axis_index("gz") == 0
    for n in range(4):
        even_rows, odd_rows = faces[n * 64 : n * 64 + 32], faces[n * 64 + 32 : n * 64 + 64]
        z_face[n * 32 : n * 32 + 32, :] = jnp.where(odd, odd_rows, even_rows).astype(BF16)


def side_in_kernel(own, z_own, inner, outer, up, down, low, high, z_all):
    lane = lax.broadcasted_iota(jnp.int32, (64, 128), 1)
    z_low, z_high = (tile.astype(F32) for tile in low_and_high(inner, outer, slice(256, 320)))
    every = z_own[...].astype(F32)
    for x in range(4):
        low[x], high[x] = low_and_high(inner, outer, slice(x * 64, x * 64 + 64))
        every = jnp.where(lane == x * 10, z_low[:, x * 10 + 8 : x * 10 + 9], every)
        every = jnp.where(lane == x * 10 + 9, z_high[:, x * 10 + 1 : x * 10 + 2], every)
    z_all[...] = every.astype(BF16)
    for x, out in ((0, down), (3, up)):
        out[:, 0:128] = low[x]
        out[:, 128:1152] = own[x]
        out[:, 1152:1280] = high[x]
        out[:, 1280:1408] = z_all[...]


def side_cot_kernel(cot, z_face, inner, outer, up, down, low, high, z_out):
    lane = lax.broadcasted_iota(jnp.int32, (32, 128), 1)
    odd = lax.axis_index("gz") == 0
    for x in range(4):
        low[x], high[x] = low_and_high(inner, outer, slice(320 + x * 128, 448 + x * 128))
    for px in range(2):
        for py, side, spot in ((0, high, 9), (1, low, 0)):
            rows = slice((px * 2 + py) * 32, (px * 2 + py) * 32 + 32)
            face = z_face[rows, :].astype(F32)
            for x in range(4):
                even_rows, odd_rows = side[x, px * 64 : px * 64 + 32, :], side[x, px * 64 + 32 : px * 64 + 64, :]
                column = jnp.where(odd, odd_rows[:, 127:128].astype(F32), even_rows[:, 0:1].astype(F32))
                face = jnp.where(lane == x * 10 + spot, column, face)
            z_out[rows, :] = face.astype(BF16)
    nothing = jnp.zeros((64, 128), BF16)
    for x, px, out in ((0, 0, down), (3, 1, up)):
        out[0:64, 0:128] = nothing
        out[64:128, 0:128] = low[x, px * 64 : px * 64 + 64, :]
        out[:, 128:1152] = cot[x, px * 128 : px * 128 + 128, :]
        out[0:64, 1152:1280] = high[x, px * 64 : px * 64 + 64, :]
        out[64:128, 1152:1280] = nothing


def cot_plane_of(n, py, own, left, right, low, high, z_all):
    xe, px = (n + 1) // 2, (n + 1) % 2
    if xe == 0 or xe == 5:
        part, lane = (left, 1310) if xe == 0 else (right, 1280)
        rows, halo = slice(py * 64, py * 64 + 64), slice(py * 32, py * 32 + 32)
        return lambda ye: (part[rows, ye * 128 : ye * 128 + 128], part[halo, lane + ye : lane + ye + 1])

    def at(ye):
        row = (px * 2 + py) * 32
        column = z_all[row : row + 32, xe * 10 - 10 + ye : xe * 10 - 9 + ye]
        if ye == 0 or ye == 9:
            return (low if ye == 0 else high)[xe - 1, px * 64 : px * 64 + 64, :], column
        row = px * 128 + py * 64
        return own[xe - 1, row : row + 64, ye * 128 - 128 : ye * 128], column

    return at


def fill_windows(planes, block, windows):
    for spot, xe in enumerate(planes):
        plane = plane_of(xe, *block)
        for ye in range(10):
            tile, column = plane(ye)
            three = (rolled(tile, column, True), tile, rolled(tile, column, False))
            for sy in range(3):
                at = ye - sy
                if 0 <= at < 8:
                    for sz in range(3):
                        row = spot * 576 + sy * 192 + sz * 64
                        windows[row : row + 64, at * 128 : at * 128 + 128] = three[sz]


def wgrad_main_kernel(own, low, high, z_all, cot, pay_out, windows, total):
    fill_windows(range(1, 5), (own, None, None, low, high, z_all), windows)
    for x in (1, 0, 2, 3):
        first, last = max(x - 1, 0), min(x + 1, 3)
        part = lax.dot_general(windows[first * 576 : last * 576 + 576, :], cot[x], NT, preferred_element_type=F32)
        if x == 1:
            total[...] = part
        else:
            row = (first - x + 1) * 576
            total[row : row + part.shape[0], :] += part
    lane = lax.broadcasted_iota(jnp.int32, (64, 128), 1) // 32
    for px in range(2):
        for hx in range(2):
            for hy in range(2):
                for hz in range(2):
                    block = jnp.zeros((64, 128), F32)
                    for py in range(2):
                        for pz in range(2):
                            row = ((px - hx + 1) * 9 + (py - hy + 1) * 3 + (pz - hz + 1)) * 64
                            piece = total[row : row + 64, px * 128 : px * 128 + 128]
                            block = piece if py + pz == 0 else jnp.where(lane == 2 * py + pz, piece, block)
                    at = (px * 8 + hx * 4 + hy * 2 + hz) * 64
                    pay_out[at : at + 64, :] = block


def wgrad_edge_kernel(left, right, cot, pay, keep, give, windows):
    first = first_core()
    fill_windows((0, 5), (None, left, right, None, None, None), windows)
    sums = []
    for px, x in ((0, 0), (1, 3)):
        taps = cot[x, px * 128 : px * 128 + 128, :]
        sums.append(lax.dot_general(windows[px * 576 : px * 576 + 576, :], taps, NT, preferred_element_type=F32))
    lane = lax.broadcasted_iota(jnp.int32, (64, 128), 1) // 32
    for hx in range(2):
        for hy in range(2):
            for hz in range(2):
                at = (hx * 4 + hy * 2 + hz) * 64
                blocks = [pay[at : at + 64, :], pay[512 + at : 512 + at + 64, :]]
                px = 1 - hx
                beyond = jnp.zeros((64, 128), F32)
                for py in range(2):
                    for pz in range(2):
                        row = ((py - hy + 1) * 3 + (pz - hz + 1)) * 64
                        beyond = jnp.where(lane == 2 * py + pz, sums[px][row : row + 64, :], beyond)
                blocks[px] = blocks[px] + beyond
                keep[at : at + 64, :] = jnp.where(first, blocks[0], blocks[1])
                give[at : at + 64, :] = jnp.where(first, blocks[1], blocks[0])


def x_chip():
    return (lax.axis_index("gy") // 8) * 2 + lax.axis_index("gz")


def split_kernel(keep, got, mine, one, two, three):
    for k, out in enumerate((mine, one, two, three)):
        rows = pl.ds(pl.multiple_of((x_chip() ^ k) * 128, 128), 128)
        out[...] = keep[rows, :] + got[rows, :]


def finish_kernel(*refs, factor):
    pieces, (out, taps, sems) = refs[:8], refs[8:]
    copies = []
    core = lax.rem(lax.axis_index("gy"), 2)
    for n in range(8):
        quarter = x_chip() ^ (n % 4)
        px = core if n < 4 else 1 - core
        kx = 2 * (quarter // 2) + 1 - px
        for hz in range(2):
            block = (pieces[n][hz * 64 : hz * 64 + 64, :] * factor).T
            for py in range(2):
                for pz in range(2):
                    spot = (2 * py + pz) * 32
                    taps[kx, 2 * lax.rem(quarter, 2) + 1 - py, 2 * hz + 1 - pz] = block[spot : spot + 32, :]
        two = pl.ds(2 * lax.rem(quarter, 2), 2)
        copies.append(pltpu.make_async_copy(taps.at[kx, two], out.at[kx, two], sems.at[n]))
        copies[-1].start()
    for copy in copies:
        copy.wait()


def up_kernel(own, left, right, low, high, z_all, weight, *rest, start):
    out, windows, matrix, planes, sems = rest[-5:]
    taps = ((3, 1, None), (None, 2, 0))
    fill_windows(range(start, start + 4), (own, left, right, low, high, z_all), windows)
    for px in range(2):
        for py in range(2):
            for pz in range(2):
                pieces = []
                for kx in taps[px]:
                    for ky in taps[py]:
                        for kz in taps[pz]:
                            if kx is None or ky is None or kz is None:
                                pieces.append(jnp.zeros((32, 64), BF16))
                            else:
                                pieces.append(weight[kx, ky, kz])
                row = (px * 4 + py * 2 + pz) * 32
                matrix[row : row + 32, :] = jnp.concatenate(pieces, axis=1)
    copies = []
    for x in range(2):
        result = lax.dot_general(matrix[...], windows[x * 576 : x * 576 + 1728, :], NN, preferred_element_type=F32)
        for n in range(8):
            planes[x, n] = result[n * 32 : n * 32 + 32].reshape(32, 8, 128).astype(BF16)
        copies.append(pltpu.make_async_copy(planes.at[x], out.at[:, :, start + x], sems.at[x]))
        copies[-1].start()
    for copy in copies:
        copy.wait()


def igrad_kernel(own, left, right, low, high, z_all, weight, *rest, start):
    out, windows, matrix, planes, sems = rest[-5:]
    for spot in range(6):
        n = 2 * start + spot
        for ky in range(4):
            py, sy = ((1, -1), (0, 0), (1, 0), (0, 1))[ky]
            plane = cot_plane_of(n, py, own, left, right, low, high, z_all)
            base = spot * 512 + ky * 128
            for y in range(8):
                tile, column = plane(y + sy + 1)
                cells = slice(y * 128, y * 128 + 128)
                windows[base : base + 64, cells] = tile
                windows[base + 64 : base + 96, cells] = rolled(tile[0:32], column, False)
                windows[base + 96 : base + 128, cells] = rolled(tile[32:64], column, True)
    for kx in range(4):
        for ky in range(4):
            row = (kx * 4 + ky) * 128
            for place, kz in enumerate((1, 2, 3, 0)):
                matrix[row + place * 32 : row + place * 32 + 32, :] = weight[kx, ky, kz]
    turned = matrix[...].T
    copies = []
    for x in range(2):
        result = lax.dot_general(turned, windows[x * 1024 : x * 1024 + 2048, :], NN, preferred_element_type=F32)
        planes[x] = result.reshape(64, 8, 128).astype(BF16)
        copies.append(pltpu.make_async_copy(planes.at[x], out.at[:, start + x], sems.at[x]))
        copies[-1].start()
    for copy in copies:
        copy.wait()


def send(block, *flip):
    return lax.ppermute(block, AXES, xor_pairs(*flip))


def beside(block, flip, run, operands):
    block, last = lax.optimization_barrier((block, operands[-1]))
    got = send(block, *flip)
    return lax.optimization_barrier((block, got, run(*operands[:-1], last)))


def body(inputs, weight, cotangent):
    x_up, x_down = ring(4, 1), ring(4, -1)
    swap = [(0, 1), (1, 0)]
    weight_t = weight.transpose(0, 1, 2, 4, 3)

    own, z_face, inner, outer = call(
        prepare_in_kernel,
        (shaped((4, 64, 1024)), shaped((64, 128)), shaped((4, 64, 128)), shaped((4, 64, 128))),
        [pltpu.VMEM((64, 4, 8, 128), BF16), pltpu.SemaphoreType.DMA((4,))],
        far=(0,),
    )(inputs)
    z_own = lax.ppermute(z_face, "gz", swap)
    cot, z_face, inner_cot, outer_cot = call(
        prepare_cot_kernel,
        (shaped((4, 256, 1024)), shaped((128, 128)), shaped((4, 128, 128)), shaped((4, 128, 128))),
        [pltpu.VMEM((8, 32, 4, 8, 128), BF16), pltpu.SemaphoreType.DMA((8,))],
        far=(0,),
    )(cotangent.reshape(8, 32, 4, 8, 128))
    rows = lambda *parts: jnp.concatenate([part.reshape(-1, 128) for part in parts])
    outer = lax.ppermute(rows(outer, z_own, outer_cot), "gy", OUTER)
    inner = lax.ppermute(rows(inner, z_own, inner_cot), "gy", INNER)
    face = shaped((4, 64, 128))
    left, right, low, high, z_all = call(
        side_in_kernel, (shaped((64, 1408)), shaped((64, 1408)), face, face, shaped((64, 128)))
    )(own, z_own, inner, outer)
    left, right, z_face = lax.optimization_barrier((left, right, z_face))
    left, right = lax.ppermute(left, "gx", x_up), lax.ppermute(right, "gx", x_down)
    face = shaped((4, 128, 128))
    cot_left, cot_right, low_cot, high_cot, z_face = call(
        side_cot_kernel, (shaped((128, 1280)), shaped((128, 1280)), face, face, shaped((128, 128)))
    )(cot, z_face, inner, outer)
    z_cot = lax.ppermute(z_face, "gz", swap)
    pay = call(
        wgrad_main_kernel,
        shaped((1024, 128), F32),
        [pltpu.VMEM((2304, 1024), BF16), pltpu.VMEM((1728, 256), F32)],
        flops=2 * 1728 * 256 * 4096,
    )(own, low, high, z_all, cot)
    keep, give = call(
        wgrad_edge_kernel, (shaped((512, 128), F32),) * 2, [pltpu.VMEM((1152, 1024), BF16)], flops=2 * 1152 * 128 * 1024
    )(left, right, cot, pay)
    z_even, z_odd = jnp.tile(z_cot[:64], (2, 1)), jnp.tile(z_cot[64:], (2, 1))
    cot_left, cot_right = jnp.concatenate([cot_left, z_odd], axis=1), jnp.concatenate([cot_right, z_even], axis=1)
    keep, give, cot_left, cot_right = lax.optimization_barrier((keep, give, cot_left, cot_right))
    cot_left = lax.ppermute(cot_left, "gx", x_up)
    cot_right = lax.ppermute(cot_right, "gx", x_down)

    up_shape = jax.ShapeDtypeStruct((8, 32, 4, 8, 128), BF16)
    grad_shape = jax.ShapeDtypeStruct((64, 4, 8, 128), BF16)

    def up_part(start, *into):
        return call(
            functools.partial(up_kernel, start=start),
            up_shape,
            [
                pltpu.VMEM((2304, 1024), BF16),
                pltpu.VMEM((256, 1728), BF16),
                pltpu.VMEM((2, 8, 32, 8, 128), BF16),
                pltpu.SemaphoreType.DMA((2,)),
            ],
            2 * 1728 * 256 * 2048,
            (7,),
            {7: 0} if into else None,
        ), (own, left, right, low, high, z_all, weight_t, *into)

    def igrad_part(start, *into):
        return call(
            functools.partial(igrad_kernel, start=start),
            grad_shape,
            [
                pltpu.VMEM((3072, 1024), BF16),
                pltpu.VMEM((2048, 64), BF16),
                pltpu.VMEM((2, 64, 8, 128), BF16),
                pltpu.SemaphoreType.DMA((2,)),
            ],
            2 * 2048 * 256 * 2048,
            (7,),
            {7: 0} if into else None,
        ), (cot, cot_left, cot_right, low_cot, high_cot, z_cot, weight_t, *into)

    block, one, two, three = call(split_kernel, (shaped((128, 128), F32),) * 4)(keep, send(give, 0, 1, 0))
    along_x = ((0, 0, 1), (0, 8, 0), (0, 8, 1))
    run, operands = up_part(0)
    one, two, three, last = lax.optimization_barrier((one, two, three, operands[-1]))
    got = [send(part, *flip) for part, flip in zip((one, two, three), along_x)]
    block, got, up_0 = lax.optimization_barrier((block, got, run(*operands[:-1], last)))
    block = (block + got[0]) + (got[1] + got[2])
    run, operands = up_part(2, up_0)
    block, got, up = beside(block, (0, 2, 0), run, operands)
    block = block + got
    run, operands = igrad_part(0)
    block, got, grad_0 = beside(block, (0, 6, 0), run, operands)
    block = block + got
    run, operands = igrad_part(2, grad_0)
    block, got, grad = beside(block, (1, 0, 0), run, operands)
    block = block + got
    block = block + send(block, 3, 0, 0)
    mine = [block] + [send(block, *flip) for flip in along_x]
    other = [send(part, 0, 1, 0) for part in mine]
    factor = 1.0 / math.sqrt(4 * 16 * 2 * inputs.shape[1] * inputs.shape[2] * inputs.shape[3])
    weight_grad = call(
        functools.partial(finish_kernel, factor=factor),
        jax.ShapeDtypeStruct((4, 4, 4, 32, 64), F32),
        [pltpu.VMEM((4, 4, 4, 32, 64), F32), pltpu.SemaphoreType.DMA((8,))],
    )(
        *mine, *other
    )
    return up.reshape(2, 2, 2, 32, 4, 8, 128), grad, weight_grad.transpose(0, 1, 2, 4, 3)


def solution(mesh):
    placed = (P(None, "gx", "gy", "gz"), P(), P(None, None, None, None, "gx", "gy", "gz"))
    return jax.shard_map(
        body,
        mesh=mesh,
        in_specs=placed,
        out_specs=(P(None, None, None, None, "gx", "gy", "gz"), P(None, "gx", "gy", "gz"), P()),
        check_vma=False,
    )
```

time: 101 us -> 69.9 us (0.69)
  Pallas kernels: 46.9 us -> 24.7 us
  local copies, waits for them, and re-layouts: 4.75 us -> 0.02 us
  waiting for transfers between devices: 11 us -> 6.79 us
  other arithmetic: 3.51 us -> 0.15 us
  starting transfers between devices: 33.9 us -> 37 us
    pallas_call x11 -> x12, Pallas kernels: 46.9 us -> 24.7 us  [run(): pl.pallas_call(kernel, out_shape=out_shape, in_specs=[FAR if n in far els...]
    ppermute x8 -> x6, waiting for transfers between devices: 7.8 us -> 1.1 us  [the longest x1 1.09 us: body(): inner = lax.ppermute(rows(inner, z_own, inner_cot), 'gy', INNER)]
    unnamed x38 -> x2, local copies, waits for them, and re-layouts: 3.66 us -> 0.01 us
    ppermute x10 -> x15, starting transfers between devices: 20 us -> 22.9 us  [send(): return lax.ppermute(block, AXES, xor_pairs(*flip))]
    ppermute x10 -> x15, waiting for transfers between devices: 3.24 us -> 5.68 us  [send(): return lax.ppermute(block, AXES, xor_pairs(*flip))]
    concatenate x6 -> x2, other arithmetic: 2.42 us -> 0.09 us  [the longest x1 0.06 us: body(): jnp.concatenate([cot_left, z_odd], axis=1)]
    squeeze x4 -> x0, local copies, waits for them, and re-layouts: 1.09 us -> none  [the longest x1 1.06 us: body(): cot[0, :128]]
    ppermute x8 -> x6, starting transfers between devices: 11.7 us -> 12 us  [the longest x1 3.84 us: body(): inner = lax.ppermute(rows(inner, z_own, inner_cot), 'gy', INNER)]
  transfers between devices with their start and end apart: 20 -> 23, of which waited for: 5 -> 5; matrix products, arithmetic and copies ran while one was open for 4% -> 0% of each run, Pallas kernels for 42% -> 30%
where the time goes in v2:
time: 69.9 us; the launch traced here: 69.8 us
  starting transfers between devices  37 us (53%)
  Pallas kernels  24.7 us (35%)
  waiting for transfers between devices  6.79 us (10%)
  between operations  1.06 us (2%)
    pallas_call x12, Pallas kernels, run(): pl.pallas_call(kernel, out_shape=out_shape, in_specs=[FAR if n in far els...  24.7 us
    ppermute x15, starting transfers between devices, send(): return lax.ppermute(block, AXES, xor_pairs(*flip))  22.9 us
    ppermute x15, waiting for transfers between devices, send(): return lax.ppermute(block, AXES, xor_pairs(*flip))  5.68 us
    ppermute x1, starting transfers between devices, body(): inner = lax.ppermute(rows(inner, z_own, inner_cot), 'gy', INNER)  3.84 us
    ppermute x1, starting transfers between devices, body(): cot_right = lax.ppermute(cot_right, 'gx', x_down)  2.59 us
    ppermute x1, starting transfers between devices, body(): outer = lax.ppermute(rows(outer, z_own, outer_cot), 'gy', OUTER)  2.56 us
    ppermute x1, starting transfers between devices, body(): z_own = lax.ppermute(z_face, 'gz', swap)  2.12 us
    ppermute x1, starting transfers between devices, body(): lax.ppermute(right, 'gx', x_down)  1.52 us
  transfers between devices with their start and end apart: 23, of which 5 were waited for; matrix products, arithmetic and copies ran while one was open for 0% of the time, Pallas kernels for 30%

profile of v2, /device:TPU:1, one launch (start us, length us, event | category | flops | bytes accessed | tf_op | source)
XLA Modules:
  0.0 69.8 jit_solution(12854077655036226838)
XLA Ops:
  0.6 1.6 %shard_map.58 = (bf16[4,64,1024]{2,1,0:T(8,128)(2,1)S(1)}, bf16[64,128]{1,0:T(8,128)(2,1)S(1)}, bf16[4,64,128]{2,1,0:T(8,128)(2,1)S(1)}, bf16[4,64,128]{2,1,0:T(8,128)(2,1)S(1)}) custom-call(bf16[64,4,8,128]{3,2,1,0:T(8,128)(2,1)} %raw.1), custom_call_target="tpu_custom_call" | custom-call | bytes 1196032 | tf_op jit(solution)/shard_map/pallas_call | solution.py:27
  2.2 2.1 %collective-permute-start = (bf16[64,128]{1,0:T(8,128)(2,1)S(1)}, bf16[64,128]{1,0:T(8,128)(2,1)S(1)}, u32[]{:S(2)}, u32[]{:S(2)}) collective-permute-start(bf16[64,128]{1,0:T(8,128)(2,1)S(1)} %get-tuple-element.59), channel_id=1, source_target_pairs={{0,1},{1,0},{2,3},{3,2},{4,5},{5,4},{6,7},{7,6},{8,9},{9,8},{10,11... | collective-permute-start | bytes 49160 | tf_op jit(solution)/shard_map/ppermute | solution.py:365
  4.4 2.5 %shard_map.59 = (bf16[4,256,1024]{2,1,0:T(8,128)(2,1)S(1)}, bf16[128,128]{1,0:T(8,128)(2,1)S(1)}, bf16[4,128,128]{2,1,0:T(8,128)(2,1)S(1)}, bf16[4,128,128]{2,1,0:T(8,128)(2,1)S(1)}) custom-call(bf16[8,32,4,8,128]{4,3,2,1,0:T(8,128)(2,1)} %bitcast.18), custom_call_target="tpu_custom_call" | custom-call | bytes 4489216 | tf_op jit(solution)/shard_map/pallas_call | solution.py:27
  6.9 2.6 %collective-permute-start.2 = (bf16[832,128]{1,0:T(8,128)(2,1)S(1)}, bf16[832,128]{1,0:T(8,128)(2,1)S(1)}, u32[]{:S(2)}, u32[]{:S(2)}) collective-permute-start(bf16[832,128]{1,0:T(8,128)(2,1)S(1)} %get-tuple-element.115), channel_id=1, source_target_pairs={{0,30},{2,4},{4,2},{6,8},{8,6},{10,12},{12,10},{14,16},{16,14},{18... | collective-permute-start | bytes 638984 | tf_op jit(solution)/shard_map/ppermute | solution.py:373
  9.5 3.8 %collective-permute-start.1 = (bf16[832,128]{1,0:T(8,128)(2,1)S(1)}, bf16[832,128]{1,0:T(8,128)(2,1)S(1)}, u32[]{:S(2)}, u32[]{:S(2)}) collective-permute-start(bf16[832,128]{1,0:T(8,128)(2,1)S(1)} %get-tuple-element.116), channel_id=1, source_target_pairs={{0,2},{2,0},{4,6},{6,4},{8,10},{10,8},{12,14},{14,12},{16,18},{18,... | collective-permute-start | bytes 638984 | tf_op jit(solution)/shard_map/ppermute | solution.py:374
  13.3 1.1 %collective-permute-done.1.inner = bf16[832,128]{1,0:T(8,128)(2,1)S(1)} collective-permute-done((bf16[832,128]{1,0:T(8,128)(2,1)S(1)}, bf16[832,128]{1,0:T(8,128)(2,1)S(1)}, u32[]{:S(2)}, u32[]{:S(2)}) %collective-permute-start.1) | collective-permute-done | bytes 213024 | tf_op jit(solution)/shard_map/ppermute | solution.py:374
  14.6 1.4 %collective-permute-start.3 = (bf16[64,1408]{1,0:T(8,128)(2,1)S(1)}, bf16[64,1408]{1,0:T(8,128)(2,1)S(1)}, u32[]{:S(2)}, u32[]{:S(2)}) collective-permute-start(bf16[64,1408]{1,0:T(8,128)(2,1)S(1)} %get-tuple-element.67), channel_id=1, source_target_pairs={{0,32},{32,64},{64,96},{96,0},{1,33},{33,65},{65,97},{97,1},{2,34}... | collective-permute-start | bytes 540680 | tf_op jit(solution)/shard_map/ppermute | solution.py:380
  15.9 1.5 %collective-permute-start.4 = (bf16[64,1408]{1,0:T(8,128)(2,1)S(1)}, bf16[64,1408]{1,0:T(8,128)(2,1)S(1)}, u32[]{:S(2)}, u32[]{:S(2)}) collective-permute-start(bf16[64,1408]{1,0:T(8,128)(2,1)S(1)} %get-tuple-element.68), channel_id=1, source_target_pairs={{0,96},{32,0},{64,32},{96,64},{1,97},{33,1},{65,33},{97,65},{2,98}... | collective-permute-start | bytes 540680 | tf_op jit(solution)/shard_map/ppermute | solution.py:380
  17.8 3.5 %shard_map.61.pay = f32[1024,128]{1,0:T(8,128)S(1)} custom-call(bf16[4,64,1024]{2,1,0:T(8,128)(2,1)S(1)} %get-tuple-element.58.own, bf16[4,64,128]{2,1,0:T(8,128)(2,1)S(1)} %get-tuple-element.70.low, bf16[4,64,128]{2,1,0:T(8,128)(2,1)S(1)} %get-tuple-element.71.high, bf16[64,128]{1,0:T(8,128)(2,1)S(1)} %get-tuple-element.72.z_all, ...), custom_call_target="tpu_custom_call" | custom-call | flops 3623878656 | bytes 3293184 | tf_op jit(solution)/shard_map/pallas_call | solution.py:27
  22.5 4.1 %collective-permute-start.6 = (f32[512,128]{1,0:T(8,128)S(1)}, f32[512,128]{1,0:T(8,128)S(1)}, u32[]{:S(2)}, u32[]{:S(2)}) collective-permute-start(f32[512,128]{1,0:T(8,128)S(1)} %get-tuple-element.80), channel_id=1, source_target_pairs={{0,2},{1,3},{2,0},{3,1},{4,6},{5,7},{6,4},{7,5},{8,10},{9,11},{10,... | collective-permute-start | bytes 786440 | tf_op jit(solution)/shard_map/ppermute | solution.py:345
  26.7 2.6 %collective-permute-start.13 = (bf16[128,1408]{1,0:T(8,128)(2,1)S(1)}, bf16[128,1408]{1,0:T(8,128)(2,1)S(1)}, u32[]{:S(2)}, u32[]{:S(2)}) collective-permute-start(bf16[128,1408]{1,0:T(8,128)(2,1)S(1)} %get-tuple-element.101), channel_id=1, source_target_pairs={{0,96},{32,0},{64,32},{96,64},{1,97},{33,1},{65,33},{97,65},{2,98}... | collective-permute-start | bytes 1081352 | tf_op jit(solution)/shard_map/ppermute | solution.py:399
  30.0 2.4 %collective-permute-start.8 = (f32[128,128]{1,0:T(8,128)S(1)}, f32[128,128]{1,0:T(8,128)S(1)}, u32[]{:S(2)}, u32[]{:S(2)}) collective-permute-start(f32[128,128]{1,0:T(8,128)S(1)} %get-tuple-element.86), channel_id=1, source_target_pairs={{0,16},{1,17},{2,18},{3,19},{4,20},{5,21},{6,22},{7,23},{8,24},{9,... | collective-permute-start | bytes 196616 | tf_op jit(solution)/shard_map/ppermute | solution.py:345
  33.3 3.4 %shard_map.65.rest_0_ = bf16[8,32,4,8,128]{4,3,2,1,0:T(8,128)(2,1)} custom-call(bf16[4,64,1024]{2,1,0:T(8,128)(2,1)S(1)} %get-tuple-element.58.own, bf16[64,1408]{1,0:T(8,128)(2,1)S(1)} %collective-permute-done.3.left, bf16[64,1408]{1,0:T(8,128)(2,1)S(1)} %collective-permute-done.4.right, bf16[4,64,128]{2,1,0:T(8,128)(2,1)S(1)} %get-tuple-element.70.low, ...), custom_call_target="tpu_custom_call" | custom-call | flops 1811939328 | bytes 3391488 | tf_op jit(solution)/shard_map/pallas_call | solution.py:27
  37.3 3.4 %shard_map.66 = bf16[8,32,4,8,128]{4,3,2,1,0:T(8,128)(2,1)} custom-call(bf16[4,64,1024]{2,1,0:T(8,128)(2,1)S(1)} %get-tuple-element.58.own, bf16[64,1408]{1,0:T(8,128)(2,1)S(1)} %collective-permute-done.3.left, bf16[64,1408]{1,0:T(8,128)(2,1)S(1)} %collective-permute-done.4.right, ...), custom_call_target="tpu_custom_call", output_to_operand_aliasing={{}: (7, {})} | custom-call | flops 1811939328 | bytes 5488640 | tf_op jit(solution)/shard_map/pallas_call | solution.py:27
  40.7 2.4 %collective-permute-start.11 = (f32[128,128]{1,0:T(8,128)S(1)}, f32[128,128]{1,0:T(8,128)S(1)}, u32[]{:S(2)}, u32[]{:S(2)}) collective-permute-start(f32[128,128]{1,0:T(8,128)S(1)} %add.24), channel_id=1, source_target_pairs={{0,12},{1,13},{2,14},{3,15},{4,8},{5,9},{6,10},{7,11},{8,4},{9,5},... | collective-permute-start | bytes 196616 | tf_op jit(solution)/shard_map/ppermute | solution.py:345
  43.1 3.9 %shard_map.67.rest_0_ = bf16[64,4,8,128]{3,2,1,0:T(8,128)(2,1)} custom-call(bf16[4,256,1024]{2,1,0:T(8,128)(2,1)S(1)} %get-tuple-element.69.cot.own, bf16[128,1408]{1,0:T(8,128)(2,1)S(1)} %collective-permute-done.12.left, bf16[128,1408]{1,0:T(8,128)(2,1)S(1)} %collective-permute-done.13.right, bf16[4,128,128]{2,1,0:T(8,128)(2,1)S(1)} %get-tuple-element.102.low, ...), custom_call_target="tpu_custom_call" | custom-call | flops 2147483648 | bytes 3899392 | tf_op jit(solution)/shard_map/pallas_call | solution.py:27
  47.1 3.9 %shard_map.68 = bf16[64,4,8,128]{3,2,1,0:T(8,128)(2,1)} custom-call(bf16[4,256,1024]{2,1,0:T(8,128)(2,1)S(1)} %get-tuple-element.69.cot.own, bf16[128,1408]{1,0:T(8,128)(2,1)S(1)} %collective-permute-done.12.left, bf16[128,1408]{1,0:T(8,128)(2,1)S(1)} %collective-permute-done.13.right, ...), custom_call_target="tpu_custom_call", output_to_operand_aliasing={{}: (7, {})} | custom-call | flops 2147483648 | bytes 4423680 | tf_op jit(solution)/shard_map/pallas_call | solution.py:27
  51.4 4.0 %collective-permute-done.15 = f32[128,128]{1,0:T(8,128)S(1)} collective-permute-done((f32[128,128]{1,0:T(8,128)S(1)}, f32[128,128]{1,0:T(8,128)S(1)}, u32[]{:S(2)}, u32[]{:S(2)}) %collective-permute-start.15) | collective-permute-done | bytes 65568 | tf_op jit(solution)/shard_map/ppermute | solution.py:345
  55.4 1.3 %collective-permute-start.18 = (f32[128,128]{1,0:T(8,128)S(1)}, f32[128,128]{1,0:T(8,128)S(1)}, u32[]{:S(2)}, u32[]{:S(2)}) collective-permute-start(f32[128,128]{1,0:T(8,128)S(1)} %add.27.refs_0_), channel_id=1, source_target_pairs={{0,17},{1,16},{2,19},{3,18},{4,21},{5,20},{6,23},{7,22},{8,25},{9,... | collective-permute-start | bytes 196616 | tf_op jit(solution)/shard_map/ppermute | solution.py:345
  56.7 2.0 %collective-permute-start.16 = (f32[128,128]{1,0:T(8,128)S(1)}, f32[128,128]{1,0:T(8,128)S(1)}, u32[]{:S(2)}, u32[]{:S(2)}) collective-permute-start(f32[128,128]{1,0:T(8,128)S(1)} %add.27.refs_0_), channel_id=1, source_target_pairs={{0,1},{1,0},{2,3},{3,2},{4,5},{5,4},{6,7},{7,6},{8,9},{9,8},{10,11... | collective-permute-start | bytes 196616 | tf_op jit(solution)/shard_map/ppermute | solution.py:345
  58.8 5.6 %collective-permute-start.19 = (f32[128,128]{1,0:T(8,128)S(1)}, f32[128,128]{1,0:T(8,128)S(1)}, u32[]{:S(2)}, u32[]{:S(2)}) collective-permute-start(f32[128,128]{1,0:T(8,128)S(1)} %add.27.refs_0_), channel_id=1, source_target_pairs={{0,2},{1,3},{2,0},{3,1},{4,6},{5,7},{6,4},{7,5},{8,10},{9,11},{10,... | collective-permute-start | bytes 196616 | tf_op jit(solution)/shard_map/ppermute | solution.py:345
  64.3 1.4 %collective-permute-start.22 = (f32[128,128]{1,0:T(8,128)S(1)}, f32[128,128]{1,0:T(8,128)S(1)}, u32[]{:S(2)}, u32[]{:S(2)}) collective-permute-start(f32[128,128]{1,0:T(8,128)S(1)} %collective-permute-done.18.refs_3_), channel_id=1, source_target_pairs={{0,2},{1,3},{2,0},{3,1},{4,6},{5,7},{6,4},{7,5},{8,10},{9,11},{10,... | collective-permute-start | bytes 196616 | tf_op jit(solution)/shard_map/ppermute | solution.py:345
  65.7 1.5 %collective-permute-start.21 = (f32[128,128]{1,0:T(8,128)S(1)}, f32[128,128]{1,0:T(8,128)S(1)}, u32[]{:S(2)}, u32[]{:S(2)}) collective-permute-start(f32[128,128]{1,0:T(8,128)S(1)} %collective-permute-done.17.refs_2_), channel_id=1, source_target_pairs={{0,2},{1,3},{2,0},{3,1},{4,6},{5,7},{6,4},{7,5},{8,10},{9,11},{10,... | collective-permute-start | bytes 196616 | tf_op jit(solution)/shard_map/ppermute | solution.py:345
  68.5 1.1 %shard_map.69 = f32[4,4,4,32,64]{4,3,2,1,0:T(8,128)} custom-call(f32[128,128]{1,0:T(8,128)S(1)} %add.27.refs_0_, f32[128,128]{1,0:T(8,128)S(1)} %collective-permute-done.16.refs_1_, f32[128,128]{1,0:T(8,128)S(1)} %collective-permute-done.17.refs_2_, f32[128,128]{1,0:T(8,128)S(1)} %collective-permute-done.18.refs_3_, ...), custom_call_target="tpu_custom_call" | custom-call | bytes 1048576 | tf_op jit(solution)/shard_map/pallas_call | solution.py:27
  (46 shorter events, 5.6 us)
Async XLA Ops:
  2.2 4.6 %collective-permute-start = (bf16[64,128]{1,0:T(8,128)(2,1)S(1)}, bf16[64,128]{1,0:T(8,128)(2,1)S(1)}, u32[]{:S(2)}, u32[]{:S(2)}) collective-permute-start(bf16[64,128]{1,0:T(8,128)(2,1)S(1)} %get-tuple-element.59), channel_id=1, source_target_pairs={{0,1},{1,0},{2,3},{3,2},{4,5},{5,4},{6,7},{7,6},{8,9},{9,8},{10,11... | collective-permute-start | bytes 49160 | tf_op jit(solution)/shard_map/ppermute | solution.py:365
  6.9 6.4 %collective-permute-start.2 = (bf16[832,128]{1,0:T(8,128)(2,1)S(1)}, bf16[832,128]{1,0:T(8,128)(2,1)S(1)}, u32[]{:S(2)}, u32[]{:S(2)}) collective-permute-start(bf16[832,128]{1,0:T(8,128)(2,1)S(1)} %get-tuple-element.115), channel_id=1, source_target_pairs={{0,30},{2,4},{4,2},{6,8},{8,6},{10,12},{12,10},{14,16},{16,14},{18... | collective-permute-start | bytes 638984 | tf_op jit(solution)/shard_map/ppermute | solution.py:373
  9.5 4.9 %collective-permute-start.1 = (bf16[832,128]{1,0:T(8,128)(2,1)S(1)}, bf16[832,128]{1,0:T(8,128)(2,1)S(1)}, u32[]{:S(2)}, u32[]{:S(2)}) collective-permute-start(bf16[832,128]{1,0:T(8,128)(2,1)S(1)} %get-tuple-element.116), channel_id=1, source_target_pairs={{0,2},{2,0},{4,6},{6,4},{8,10},{10,8},{12,14},{14,12},{16,18},{18,... | collective-permute-start | bytes 638984 | tf_op jit(solution)/shard_map/ppermute | solution.py:374
  14.6 6.9 %collective-permute-start.3 = (bf16[64,1408]{1,0:T(8,128)(2,1)S(1)}, bf16[64,1408]{1,0:T(8,128)(2,1)S(1)}, u32[]{:S(2)}, u32[]{:S(2)}) collective-permute-start(bf16[64,1408]{1,0:T(8,128)(2,1)S(1)} %get-tuple-element.67), channel_id=1, source_target_pairs={{0,32},{32,64},{64,96},{96,0},{1,33},{33,65},{65,97},{97,1},{2,34}... | collective-permute-start | bytes 540680 | tf_op jit(solution)/shard_map/ppermute | solution.py:380
  15.9 5.5 %collective-permute-start.4 = (bf16[64,1408]{1,0:T(8,128)(2,1)S(1)}, bf16[64,1408]{1,0:T(8,128)(2,1)S(1)}, u32[]{:S(2)}, u32[]{:S(2)}) collective-permute-start(bf16[64,1408]{1,0:T(8,128)(2,1)S(1)} %get-tuple-element.68), channel_id=1, source_target_pairs={{0,96},{32,0},{64,32},{96,64},{1,97},{33,1},{65,33},{97,65},{2,98}... | collective-permute-start | bytes 540680 | tf_op jit(solution)/shard_map/ppermute | solution.py:380
  17.7 3.6 %collective-permute-start.5 = (bf16[128,128]{1,0:T(8,128)(2,1)S(1)}, bf16[128,128]{1,0:T(8,128)(2,1)S(1)}, u32[]{:S(2)}, u32[]{:S(2)}) collective-permute-start(bf16[128,128]{1,0:T(8,128)(2,1)S(1)} %get-tuple-element.77), channel_id=1, source_target_pairs={{0,1},{1,0},{2,3},{3,2},{4,5},{5,4},{6,7},{7,6},{8,9},{9,8},{10,11... | collective-permute-start | bytes 98312 | tf_op jit(solution)/shard_map/ppermute | solution.py:385
  21.4 11.8 %copy-start = (bf16[4,4,4,64,32]{3,4,2,1,0:T(8,128)(2,1)S(1)}, bf16[4,4,4,64,32]{3,4,2,1,0:T(8,128)(2,1)}, u32[]{:S(2)}) copy-start(bf16[4,4,4,64,32]{3,4,2,1,0:T(8,128)(2,1)} %param.4) | copy-start | bytes 786436
  22.5 6.8 %collective-permute-start.6 = (f32[512,128]{1,0:T(8,128)S(1)}, f32[512,128]{1,0:T(8,128)S(1)}, u32[]{:S(2)}, u32[]{:S(2)}) collective-permute-start(f32[512,128]{1,0:T(8,128)S(1)} %get-tuple-element.80), channel_id=1, source_target_pairs={{0,2},{1,3},{2,0},{3,1},{4,6},{5,7},{6,4},{7,5},{8,10},{9,11},{10,... | collective-permute-start | bytes 786440 | tf_op jit(solution)/shard_map/ppermute | solution.py:345
  26.6 16.5 %collective-permute-start.12 = (bf16[128,1408]{1,0:T(8,128)(2,1)S(1)}, bf16[128,1408]{1,0:T(8,128)(2,1)S(1)}, u32[]{:S(2)}, u32[]{:S(2)}) collective-permute-start(bf16[128,1408]{1,0:T(8,128)(2,1)S(1)} %get-tuple-element.100), channel_id=1, source_target_pairs={{0,32},{32,64},{64,96},{96,0},{1,33},{33,65},{65,97},{97,1},{2,34}... | collective-permute-start | bytes 1081352 | tf_op jit(solution)/shard_map/ppermute | solution.py:398
  26.7 16.4 %collective-permute-start.13 = (bf16[128,1408]{1,0:T(8,128)(2,1)S(1)}, bf16[128,1408]{1,0:T(8,128)(2,1)S(1)}, u32[]{:S(2)}, u32[]{:S(2)}) collective-permute-start(bf16[128,1408]{1,0:T(8,128)(2,1)S(1)} %get-tuple-element.101), channel_id=1, source_target_pairs={{0,96},{32,0},{64,32},{96,64},{1,97},{33,1},{65,33},{97,65},{2,98}... | collective-permute-start | bytes 1081352 | tf_op jit(solution)/shard_map/ppermute | solution.py:399
  29.3 7.4 %collective-permute-start.7 = (f32[128,128]{1,0:T(8,128)S(1)}, f32[128,128]{1,0:T(8,128)S(1)}, u32[]{:S(2)}, u32[]{:S(2)}) collective-permute-start(f32[128,128]{1,0:T(8,128)S(1)} %get-tuple-element.85), channel_id=1, source_target_pairs={{0,1},{1,0},{2,3},{3,2},{4,5},{5,4},{6,7},{7,6},{8,9},{9,8},{10,11... | collective-permute-start | bytes 196616 | tf_op jit(solution)/shard_map/ppermute | solution.py:345
  30.0 6.7 %collective-permute-start.8 = (f32[128,128]{1,0:T(8,128)S(1)}, f32[128,128]{1,0:T(8,128)S(1)}, u32[]{:S(2)}, u32[]{:S(2)}) collective-permute-start(f32[128,128]{1,0:T(8,128)S(1)} %get-tuple-element.86), channel_id=1, source_target_pairs={{0,16},{1,17},{2,18},{3,19},{4,20},{5,21},{6,22},{7,23},{8,24},{9,... | collective-permute-start | bytes 196616 | tf_op jit(solution)/shard_map/ppermute | solution.py:345
  32.4 4.8 %collective-permute-start.9 = (f32[128,128]{1,0:T(8,128)S(1)}, f32[128,128]{1,0:T(8,128)S(1)}, u32[]{:S(2)}, u32[]{:S(2)}) collective-permute-start(f32[128,128]{1,0:T(8,128)S(1)} %get-tuple-element.87), channel_id=1, source_target_pairs={{0,17},{1,16},{2,19},{3,18},{4,21},{5,20},{6,23},{7,22},{8,25},{9,... | collective-permute-start | bytes 196616 | tf_op jit(solution)/shard_map/ppermute | solution.py:345
  37.2 3.5 %collective-permute-start.10 = (f32[128,128]{1,0:T(8,128)S(1)}, f32[128,128]{1,0:T(8,128)S(1)}, u32[]{:S(2)}, u32[]{:S(2)}) collective-permute-start(f32[128,128]{1,0:T(8,128)S(1)} %add_add_fusion), channel_id=1, source_target_pairs={{0,4},{1,5},{2,6},{3,7},{4,0},{5,1},{6,2},{7,3},{8,12},{9,13},{10,... | collective-permute-start | bytes 196616 | tf_op jit(solution)/shard_map/ppermute | solution.py:345
  40.7 6.3 %collective-permute-start.11 = (f32[128,128]{1,0:T(8,128)S(1)}, f32[128,128]{1,0:T(8,128)S(1)}, u32[]{:S(2)}, u32[]{:S(2)}) collective-permute-start(f32[128,128]{1,0:T(8,128)S(1)} %add.24), channel_id=1, source_target_pairs={{0,12},{1,13},{2,14},{3,15},{4,8},{5,9},{6,10},{7,11},{8,4},{9,5},... | collective-permute-start | bytes 196616 | tf_op jit(solution)/shard_map/ppermute | solution.py:345
  47.0 4.0 %collective-permute-start.14 = (f32[128,128]{1,0:T(8,128)S(1)}, f32[128,128]{1,0:T(8,128)S(1)}, u32[]{:S(2)}, u32[]{:S(2)}) collective-permute-start(f32[128,128]{1,0:T(8,128)S(1)} %add.25), channel_id=1, source_target_pairs={{0,32},{1,33},{2,34},{3,35},{4,36},{5,37},{6,38},{7,39},{8,40},{9,... | collective-permute-start | bytes 196616 | tf_op jit(solution)/shard_map/ppermute | solution.py:345
  51.0 4.4 %collective-permute-start.15 = (f32[128,128]{1,0:T(8,128)S(1)}, f32[128,128]{1,0:T(8,128)S(1)}, u32[]{:S(2)}, u32[]{:S(2)}) collective-permute-start(f32[128,128]{1,0:T(8,128)S(1)} %add.26), channel_id=1, source_target_pairs={{0,96},{1,97},{2,98},{3,99},{4,100},{5,101},{6,102},{7,103},{8,104... | collective-permute-start | bytes 196616 | tf_op jit(solution)/shard_map/ppermute | solution.py:345
  55.4 8.9 %collective-permute-start.18 = (f32[128,128]{1,0:T(8,128)S(1)}, f32[128,128]{1,0:T(8,128)S(1)}, u32[]{:S(2)}, u32[]{:S(2)}) collective-permute-start(f32[128,128]{1,0:T(8,128)S(1)} %add.27.refs_0_), channel_id=1, source_target_pairs={{0,17},{1,16},{2,19},{3,18},{4,21},{5,20},{6,23},{7,22},{8,25},{9,... | collective-permute-start | bytes 196616 | tf_op jit(solution)/shard_map/ppermute | solution.py:345
  56.7 9.0 %collective-permute-start.17 = (f32[128,128]{1,0:T(8,128)S(1)}, f32[128,128]{1,0:T(8,128)S(1)}, u32[]{:S(2)}, u32[]{:S(2)}) collective-permute-start(f32[128,128]{1,0:T(8,128)S(1)} %add.27.refs_0_), channel_id=1, source_target_pairs={{0,16},{1,17},{2,18},{3,19},{4,20},{5,21},{6,22},{7,23},{8,24},{9,... | collective-permute-start | bytes 196616 | tf_op jit(solution)/shard_map/ppermute | solution.py:345
  56.7 10.5 %collective-permute-start.16 = (f32[128,128]{1,0:T(8,128)S(1)}, f32[128,128]{1,0:T(8,128)S(1)}, u32[]{:S(2)}, u32[]{:S(2)}) collective-permute-start(f32[128,128]{1,0:T(8,128)S(1)} %add.27.refs_0_), channel_id=1, source_target_pairs={{0,1},{1,0},{2,3},{3,2},{4,5},{5,4},{6,7},{7,6},{8,9},{9,8},{10,11... | collective-permute-start | bytes 196616 | tf_op jit(solution)/shard_map/ppermute | solution.py:345
  58.8 8.5 %collective-permute-start.19 = (f32[128,128]{1,0:T(8,128)S(1)}, f32[128,128]{1,0:T(8,128)S(1)}, u32[]{:S(2)}, u32[]{:S(2)}) collective-permute-start(f32[128,128]{1,0:T(8,128)S(1)} %add.27.refs_0_), channel_id=1, source_target_pairs={{0,2},{1,3},{2,0},{3,1},{4,6},{5,7},{6,4},{7,5},{8,10},{9,11},{10,... | collective-permute-start | bytes 196616 | tf_op jit(solution)/shard_map/ppermute | solution.py:345
  64.3 2.9 %collective-permute-start.22 = (f32[128,128]{1,0:T(8,128)S(1)}, f32[128,128]{1,0:T(8,128)S(1)}, u32[]{:S(2)}, u32[]{:S(2)}) collective-permute-start(f32[128,128]{1,0:T(8,128)S(1)} %collective-permute-done.18.refs_3_), channel_id=1, source_target_pairs={{0,2},{1,3},{2,0},{3,1},{4,6},{5,7},{6,4},{7,5},{8,10},{9,11},{10,... | collective-permute-start | bytes 196616 | tf_op jit(solution)/shard_map/ppermute | solution.py:345
  65.7 2.4 %collective-permute-start.21 = (f32[128,128]{1,0:T(8,128)S(1)}, f32[128,128]{1,0:T(8,128)S(1)}, u32[]{:S(2)}, u32[]{:S(2)}) collective-permute-start(f32[128,128]{1,0:T(8,128)S(1)} %collective-permute-done.17.refs_2_), channel_id=1, source_target_pairs={{0,2},{1,3},{2,0},{3,1},{4,6},{5,7},{6,4},{7,5},{8,10},{9,11},{10,... | collective-permute-start | bytes 196616 | tf_op jit(solution)/shard_map/ppermute | solution.py:345
  67.2 1.3 %collective-permute-start.20 = (f32[128,128]{1,0:T(8,128)S(1)}, f32[128,128]{1,0:T(8,128)S(1)}, u32[]{:S(2)}, u32[]{:S(2)}) collective-permute-start(f32[128,128]{1,0:T(8,128)S(1)} %collective-permute-done.16.refs_1_), channel_id=1, source_target_pairs={{0,2},{1,3},{2,0},{3,1},{4,6},{5,7},{6,4},{7,5},{8,10},{9,11},{10,... | collective-permute-start | bytes 196616 | tf_op jit(solution)/shard_map/ppermute | solution.py:345

commit v3 on v2

--- a/solution.py
+++ b/solution.py
@@ -21,7 +21,7 @@
     return pltpu.VMEM(shape, dtype)
 
 
-def call(kernel, out_shape, scratch=(), flops=0, far=(), aliases=None):
+def call(kernel, out_shape, scratch=(), flops=0, far=()):
     def run(*operands):
         moved = sum(math.prod(o.shape) * o.dtype.itemsize for o in (*operands, *jax.tree.leaves(out_shape)))
         return pl.pallas_call(
@@ -31,7 +31,6 @@
             out_specs=jax.tree.map(lambda o: FAR if isinstance(o, jax.ShapeDtypeStruct) else WHOLE, out_shape),
             scratch_shapes=list(scratch),
             compiler_params=PARAMS,
-            input_output_aliases=aliases or {},
             cost_estimate=pl.CostEstimate(flops=flops, bytes_accessed=moved, transcendentals=0),
         )(*[pltpu.with_memory_space_constraint(o, pltpu.HBM if n in far else pltpu.VMEM) for n, o in enumerate(operands)])
 
@@ -97,12 +96,13 @@
     copies = [pltpu.make_async_copy(raw.at[16 * n : 16 * n + 16], arrived.at[16 * n : 16 * n + 16], sems.at[n]) for n in range(4)]
     for copy in copies:
         copy.start()
-    for copy in copies:
-        copy.wait()
+    for n in range(4):
+        copies[n].wait()
+        for x in range(4):
+            own[x, 16 * n : 16 * n + 16, :] = arrived[16 * n : 16 * n + 16, x].reshape(16, 1024)
     faces = jnp.zeros((64, 128), F32)
     for x in range(4):
-        plane = arrived[:, x].reshape(64, 1024)
-        own[x] = plane
+        plane = own[x]
         low, high = plane[:, 0:128], plane[:, 896:1024]
         inner[x] = jnp.where(first_core(), high, low)
         outer[x] = jnp.where(first_core(), low, high)
@@ -148,7 +148,7 @@
         out[:, 1280:1408] = z_all[...]
 
 
-def side_cot_kernel(cot, z_face, inner, outer, up, down, low, high, z_out):
+def side_cot_kernel(z_face, inner, outer, low, high, z_out):
     lane = lax.broadcasted_iota(jnp.int32, (32, 128), 1)
     odd = lax.axis_index("gz") == 0
     for x in range(4):
@@ -162,6 +162,9 @@
                 column = jnp.where(odd, odd_rows[:, 127:128].astype(F32), even_rows[:, 0:1].astype(F32))
                 face = jnp.where(lane == x * 10 + spot, column, face)
             z_out[rows, :] = face.astype(BF16)
+
+
+def sides_cot_kernel(cot, low, high, z_all, up, down):
     nothing = jnp.zeros((64, 128), BF16)
     for x, px, out in ((0, 0, down), (3, 1, up)):
         out[0:64, 0:128] = nothing
@@ -169,6 +172,8 @@
         out[:, 128:1152] = cot[x, px * 128 : px * 128 + 128, :]
         out[0:64, 1152:1280] = high[x, px * 64 : px * 64 + 64, :]
         out[64:128, 1152:1280] = nothing
+        out[0:64, 1280:1408] = z_all[px * 64 : px * 64 + 64, :]
+        out[64:128, 1280:1408] = nothing
 
 
 def cot_plane_of(n, py, own, left, right, low, high, z_all):
@@ -283,10 +288,8 @@
         copy.wait()
 
 
-def up_kernel(own, left, right, low, high, z_all, weight, *rest, start):
-    out, windows, matrix, planes, sems = rest[-5:]
+def weights_kernel(weight, for_up, for_grad, turned):
     taps = ((3, 1, None), (None, 2, 0))
-    fill_windows(range(start, start + 4), (own, left, right, low, high, z_all), windows)
     for px in range(2):
         for py in range(2):
             for pz in range(2):
@@ -299,43 +302,47 @@
                             else:
                                 pieces.append(weight[kx, ky, kz])
                 row = (px * 4 + py * 2 + pz) * 32
-                matrix[row : row + 32, :] = jnp.concatenate(pieces, axis=1)
+                for_up[row : row + 32, :] = jnp.concatenate(pieces, axis=1)
+    for kx in range(4):
+        for ky in range(4):
+            row = (kx * 4 + ky) * 128
+            for place, kz in enumerate((1, 2, 3, 0)):
+                turned[row + place * 32 : row + place * 32 + 32, :] = weight[kx, ky, kz]
+    for_grad[...] = turned[...].T
+
+
+def up_kernel(own, left, right, low, high, z_all, matrix, out, windows, planes, sems):
+    fill_windows(range(6), (own, left, right, low, high, z_all), windows)
     copies = []
-    for x in range(2):
+    for x in range(4):
         result = lax.dot_general(matrix[...], windows[x * 576 : x * 576 + 1728, :], NN, preferred_element_type=F32)
         for n in range(8):
-            planes[x, n] = result[n * 32 : n * 32 + 32].reshape(32, 8, 128).astype(BF16)
-        copies.append(pltpu.make_async_copy(planes.at[x], out.at[:, :, start + x], sems.at[x]))
-        copies[-1].start()
+            part = result[n * 32 : n * 32 + 32].astype(BF16)
+            part = jnp.stack([part[:, y * 128 : y * 128 + 128] for y in range(8)], 0)
+            planes[x, n] = jnp.swapaxes(part, 0, 1)
+            copies.append(pltpu.make_async_copy(planes.at[x, n], out.at[n, :, x], sems.at[x, n]))
+            copies[-1].start()
     for copy in copies:
         copy.wait()
 
 
-def igrad_kernel(own, left, right, low, high, z_all, weight, *rest, start):
-    out, windows, matrix, planes, sems = rest[-5:]
-    for spot in range(6):
-        n = 2 * start + spot
+def igrad_kernel(own, left, right, low, high, z_all, matrix, out, windows, planes, sems):
+    for n in range(10):
         for ky in range(4):
             py, sy = ((1, -1), (0, 0), (1, 0), (0, 1))[ky]
             plane = cot_plane_of(n, py, own, left, right, low, high, z_all)
-            base = spot * 512 + ky * 128
+            base = n * 512 + ky * 128
             for y in range(8):
                 tile, column = plane(y + sy + 1)
                 cells = slice(y * 128, y * 128 + 128)
                 windows[base : base + 64, cells] = tile
                 windows[base + 64 : base + 96, cells] = rolled(tile[0:32], column, False)
                 windows[base + 96 : base + 128, cells] = rolled(tile[32:64], column, True)
-    for kx in range(4):
-        for ky in range(4):
-            row = (kx * 4 + ky) * 128
-            for place, kz in enumerate((1, 2, 3, 0)):
-                matrix[row + place * 32 : row + place * 32 + 32, :] = weight[kx, ky, kz]
-    turned = matrix[...].T
     copies = []
-    for x in range(2):
-        result = lax.dot_general(turned, windows[x * 1024 : x * 1024 + 2048, :], NN, preferred_element_type=F32)
+    for x in range(4):
+        result = lax.dot_general(matrix[...], windows[x * 1024 : x * 1024 + 2048, :], NN, preferred_element_type=F32)
         planes[x] = result.reshape(64, 8, 128).astype(BF16)
-        copies.append(pltpu.make_async_copy(planes.at[x], out.at[:, start + x], sems.at[x]))
+        copies.append(pltpu.make_async_copy(planes.at[x], out.at[:, x], sems.at[x]))
         copies[-1].start()
     for copy in copies:
         copy.wait()
@@ -345,10 +352,11 @@
     return lax.ppermute(block, AXES, xor_pairs(*flip))
 
 
-def beside(block, flip, run, operands):
-    block, last = lax.optimization_barrier((block, operands[-1]))
-    got = send(block, *flip)
-    return lax.optimization_barrier((block, got, run(*operands[:-1], last)))
+def beside(parts, flips, *works):
+    parts, last = lax.optimization_barrier((parts, [operands[-1] for _, operands in works]))
+    got = [send(part, *flip) for part, flip in zip(parts, flips)]
+    done = [run(*operands[:-1], carry) for (run, operands), carry in zip(works, last)]
+    return lax.optimization_barrier((parts, got, done))
 
 
 def body(inputs, weight, cotangent):
@@ -370,8 +378,13 @@
         far=(0,),
     )(cotangent.reshape(8, 32, 4, 8, 128))
     rows = lambda *parts: jnp.concatenate([part.reshape(-1, 128) for part in parts])
+    z_own, weight_t = lax.optimization_barrier((z_own, weight_t))
+    for_up, for_grad = call(
+        weights_kernel, (shaped((256, 1728)), shaped((64, 2048))), [pltpu.VMEM((2048, 64), BF16)], far=()
+    )(weight_t)
     outer = lax.ppermute(rows(outer, z_own, outer_cot), "gy", OUTER)
     inner = lax.ppermute(rows(inner, z_own, inner_cot), "gy", INNER)
+    inner, outer, for_up, for_grad = lax.optimization_barrier((inner, outer, for_up, for_grad))
     face = shaped((4, 64, 128))
     left, right, low, high, z_all = call(
         side_in_kernel, (shaped((64, 1408)), shaped((64, 1408)), face, face, shaped((64, 128)))
@@ -379,9 +392,7 @@
     left, right, z_face = lax.optimization_barrier((left, right, z_face))
     left, right = lax.ppermute(left, "gx", x_up), lax.ppermute(right, "gx", x_down)
     face = shaped((4, 128, 128))
-    cot_left, cot_right, low_cot, high_cot, z_face = call(
-        side_cot_kernel, (shaped((128, 1280)), shaped((128, 1280)), face, face, shaped((128, 128)))
-    )(cot, z_face, inner, outer)
+    low_cot, high_cot, z_face = call(side_cot_kernel, (face, face, shaped((128, 128))))(z_face, inner, outer)
     z_cot = lax.ppermute(z_face, "gz", swap)
     pay = call(
         wgrad_main_kernel,
@@ -389,65 +400,38 @@
         [pltpu.VMEM((2304, 1024), BF16), pltpu.VMEM((1728, 256), F32)],
         flops=2 * 1728 * 256 * 4096,
     )(own, low, high, z_all, cot)
+    left, right, z_cot = lax.optimization_barrier((left, right, z_cot))
     keep, give = call(
         wgrad_edge_kernel, (shaped((512, 128), F32),) * 2, [pltpu.VMEM((1152, 1024), BF16)], flops=2 * 1152 * 128 * 1024
     )(left, right, cot, pay)
-    z_even, z_odd = jnp.tile(z_cot[:64], (2, 1)), jnp.tile(z_cot[64:], (2, 1))
-    cot_left, cot_right = jnp.concatenate([cot_left, z_odd], axis=1), jnp.concatenate([cot_right, z_even], axis=1)
-    keep, give, cot_left, cot_right = lax.optimization_barrier((keep, give, cot_left, cot_right))
-    cot_left = lax.ppermute(cot_left, "gx", x_up)
-    cot_right = lax.ppermute(cot_right, "gx", x_down)
-
-    up_shape = jax.ShapeDtypeStruct((8, 32, 4, 8, 128), BF16)
-    grad_shape = jax.ShapeDtypeStruct((64, 4, 8, 128), BF16)
-
-    def up_part(start, *into):
-        return call(
-            functools.partial(up_kernel, start=start),
-            up_shape,
-            [
-                pltpu.VMEM((2304, 1024), BF16),
-                pltpu.VMEM((256, 1728), BF16),
-                pltpu.VMEM((2, 8, 32, 8, 128), BF16),
-                pltpu.SemaphoreType.DMA((2,)),
-            ],
-            2 * 1728 * 256 * 2048,
-            (7,),
-            {7: 0} if into else None,
-        ), (own, left, right, low, high, z_all, weight_t, *into)
-
-    def igrad_part(start, *into):
-        return call(
-            functools.partial(igrad_kernel, start=start),
-            grad_shape,
-            [
-                pltpu.VMEM((3072, 1024), BF16),
-                pltpu.VMEM((2048, 64), BF16),
-                pltpu.VMEM((2, 64, 8, 128), BF16),
-                pltpu.SemaphoreType.DMA((2,)),
-            ],
-            2 * 2048 * 256 * 2048,
-            (7,),
-            {7: 0} if into else None,
-        ), (cot, cot_left, cot_right, low_cot, high_cot, z_cot, weight_t, *into)
+    up_work = call(
+        up_kernel,
+        jax.ShapeDtypeStruct((8, 32, 4, 8, 128), BF16),
+        [pltpu.VMEM((3456, 1024), BF16), pltpu.VMEM((4, 8, 32, 8, 128), BF16), pltpu.SemaphoreType.DMA((4, 8))],
+        flops=2 * 1728 * 256 * 4096,
+    ), (own, left, right, low, high, z_all, for_up)
+    grad_work = call(
+        igrad_kernel,
+        jax.ShapeDtypeStruct((64, 4, 8, 128), BF16),
+        [pltpu.VMEM((5120, 1024), BF16), pltpu.VMEM((4, 64, 8, 128), BF16), pltpu.SemaphoreType.DMA((4,))],
+        flops=2 * 2048 * 256 * 4096,
+    )
 
     block, one, two, three = call(split_kernel, (shaped((128, 128), F32),) * 4)(keep, send(give, 0, 1, 0))
     along_x = ((0, 0, 1), (0, 8, 0), (0, 8, 1))
-    run, operands = up_part(0)
-    one, two, three, last = lax.optimization_barrier((one, two, three, operands[-1]))
+    (one, two, three), last = lax.optimization_barrier(((one, two, three), z_cot))
     got = [send(part, *flip) for part, flip in zip((one, two, three), along_x)]
-    block, got, up_0 = lax.optimization_barrier((block, got, run(*operands[:-1], last)))
+    cot_left, cot_right = call(sides_cot_kernel, (shaped((128, 1408)), shaped((128, 1408))), flops=2 * 1728 * 256 * 2048)(
+        cot, low_cot, high_cot, last
+    )
+    cot_left, cot_right = lax.ppermute(cot_left, "gx", x_up), lax.ppermute(cot_right, "gx", x_down)
     block = (block + got[0]) + (got[1] + got[2])
-    run, operands = up_part(2, up_0)
-    block, got, up = beside(block, (0, 2, 0), run, operands)
-    block = block + got
-    run, operands = igrad_part(0)
-    block, got, grad_0 = beside(block, (0, 6, 0), run, operands)
-    block = block + got
-    run, operands = igrad_part(2, grad_0)
-    block, got, grad = beside(block, (1, 0, 0), run, operands)
-    block = block + got
-    block = block + send(block, 3, 0, 0)
+    along_y, along_z = ((1, 0, 0), (2, 0, 0), (3, 0, 0)), ((0, 2, 0), (0, 4, 0), (0, 6, 0))
+    (block, *_), got, (up,) = beside([block] * 3, along_z, up_work)
+    block = (block + got[0]) + (got[1] + got[2])
+    grad_work = grad_work, (cot, cot_left, cot_right, low_cot, high_cot, z_cot, for_grad)
+    (block, *_), got, (grad,) = beside([block] * 3, along_y, grad_work)
+    block = (block + got[0]) + (got[1] + got[2])
     mine = [block] + [send(block, *flip) for flip in along_x]
     other = [send(part, 0, 1, 0) for part in mine]
     factor = 1.0 / math.sqrt(4 * 16 * 2 * inputs.shape[1] * inputs.shape[2] * inputs.shape[3])

time: 69.9 us -> 67.6 us (0.967)
  starting transfers between devices: 37 us -> 41.1 us
  Pallas kernels: 24.7 us -> 21.3 us
  waiting for transfers between devices: 6.79 us -> 3.96 us
    ppermute x15 -> x17, starting transfers between devices: 22.9 us -> 26.9 us  [send(): return lax.ppermute(block, AXES, xor_pairs(*flip))]
    pallas_call x12, Pallas kernels: 24.7 us -> 21.3 us  [run(): pl.pallas_call(kernel, out_shape=out_shape, in_specs=[FAR if n in far els...]
    ppermute x15 -> x17, waiting for transfers between devices: 5.68 us -> 3.13 us  [send(): return lax.ppermute(block, AXES, xor_pairs(*flip))]
  transfers between devices with their start and end apart: 23 -> 25, of which waited for: 5 -> 5; matrix products, arithmetic and copies ran while one was open for 0% -> 0% of each run, Pallas kernels for 30% -> 25%
where the time goes in v3:
time: 67.6 us; the launch traced here: 67.5 us
  starting transfers between devices  41.1 us (61%)
  Pallas kernels  21.3 us (32%)
  waiting for transfers between devices  3.96 us (6%)
  between operations  1.02 us (2%)
    ppermute x17, starting transfers between devices, send(): return lax.ppermute(block, AXES, xor_pairs(*flip))  26.9 us
    pallas_call x12, Pallas kernels, run(): pl.pallas_call(kernel, out_shape=out_shape, in_specs=[FAR if n in far els...  21.3 us
    ppermute x1, starting transfers between devices, body(): inner = lax.ppermute(rows(inner, z_own, inner_cot), 'gy', INNER)  3.84 us
    ppermute x17, waiting for transfers between devices, send(): return lax.ppermute(block, AXES, xor_pairs(*flip))  3.13 us
    ppermute x1, starting transfers between devices, body(): outer = lax.ppermute(rows(outer, z_own, outer_cot), 'gy', OUTER)  2.56 us
    ppermute x1, starting transfers between devices, body(): z_own = lax.ppermute(z_face, 'gz', swap)  2.12 us
    ppermute x1, starting transfers between devices, body(): lax.ppermute(right, 'gx', x_down)  1.52 us
    ppermute x1, starting transfers between devices, body(): lax.ppermute(cot_right, 'gx', x_down)  1.38 us
  transfers between devices with their start and end apart: 25, of which 5 were waited for; matrix products, arithmetic and copies ran while one was open for 0% of the time, Pallas kernels for 25%

profile of v3, /device:TPU:1, one launch (start us, length us, event | category | flops | bytes accessed | tf_op | source)
XLA Modules:
  0.0 67.5 jit_solution(11173557425363896712)
XLA Ops:
  0.6 1.6 %shard_map.58 = (bf16[4,64,1024]{2,1,0:T(8,128)(2,1)S(1)}, bf16[64,128]{1,0:T(8,128)(2,1)S(1)}, bf16[4,64,128]{2,1,0:T(8,128)(2,1)S(1)}, bf16[4,64,128]{2,1,0:T(8,128)(2,1)S(1)}) custom-call(bf16[64,4,8,128]{3,2,1,0:T(8,128)(2,1)} %raw.1), custom_call_target="tpu_custom_call" | custom-call | bytes 1196032 | tf_op jit(solution)/shard_map/pallas_call | solution.py:27
  2.3 2.1 %collective-permute-start = (bf16[64,128]{1,0:T(8,128)(2,1)S(1)}, bf16[64,128]{1,0:T(8,128)(2,1)S(1)}, u32[]{:S(2)}, u32[]{:S(2)}) collective-permute-start(bf16[64,128]{1,0:T(8,128)(2,1)S(1)} %get-tuple-element.64), channel_id=1, source_target_pairs={{0,1},{1,0},{2,3},{3,2},{4,5},{5,4},{6,7},{7,6},{8,9},{9,8},{10,11... | collective-permute-start | bytes 49160 | tf_op jit(solution)/shard_map/ppermute | solution.py:373
  4.4 2.5 %shard_map.59 = (bf16[4,256,1024]{2,1,0:T(8,128)(2,1)S(1)}, bf16[128,128]{1,0:T(8,128)(2,1)S(1)}, bf16[4,128,128]{2,1,0:T(8,128)(2,1)S(1)}, bf16[4,128,128]{2,1,0:T(8,128)(2,1)S(1)}) custom-call(bf16[8,32,4,8,128]{4,3,2,1,0:T(8,128)(2,1)} %bitcast.13), custom_call_target="tpu_custom_call" | custom-call | bytes 4489216 | tf_op jit(solution)/shard_map/pallas_call | solution.py:27
  7.0 2.6 %collective-permute-start.2 = (bf16[832,128]{1,0:T(8,128)(2,1)S(1)}, bf16[832,128]{1,0:T(8,128)(2,1)S(1)}, u32[]{:S(2)}, u32[]{:S(2)}) collective-permute-start(bf16[832,128]{1,0:T(8,128)(2,1)S(1)} %get-tuple-element.123), channel_id=1, source_target_pairs={{0,30},{2,4},{4,2},{6,8},{8,6},{10,12},{12,10},{14,16},{16,14},{18... | collective-permute-start | bytes 638984 | tf_op jit(solution)/shard_map/ppermute | solution.py:385
  9.5 3.8 %collective-permute-start.1 = (bf16[832,128]{1,0:T(8,128)(2,1)S(1)}, bf16[832,128]{1,0:T(8,128)(2,1)S(1)}, u32[]{:S(2)}, u32[]{:S(2)}) collective-permute-start(bf16[832,128]{1,0:T(8,128)(2,1)S(1)} %get-tuple-element.124), channel_id=1, source_target_pairs={{0,2},{2,0},{4,6},{6,4},{8,10},{10,8},{12,14},{14,12},{16,18},{18,... | collective-permute-start | bytes 638984 | tf_op jit(solution)/shard_map/ppermute | solution.py:386
  14.9 1.4 %collective-permute-start.3 = (bf16[64,1408]{1,0:T(8,128)(2,1)S(1)}, bf16[64,1408]{1,0:T(8,128)(2,1)S(1)}, u32[]{:S(2)}, u32[]{:S(2)}) collective-permute-start(bf16[64,1408]{1,0:T(8,128)(2,1)S(1)} %get-tuple-element.78), channel_id=1, source_target_pairs={{0,32},{32,64},{64,96},{96,0},{1,33},{33,65},{65,97},{97,1},{2,34}... | collective-permute-start | bytes 540680 | tf_op jit(solution)/shard_map/ppermute | solution.py:393
  16.3 1.5 %collective-permute-start.4 = (bf16[64,1408]{1,0:T(8,128)(2,1)S(1)}, bf16[64,1408]{1,0:T(8,128)(2,1)S(1)}, u32[]{:S(2)}, u32[]{:S(2)}) collective-permute-start(bf16[64,1408]{1,0:T(8,128)(2,1)S(1)} %get-tuple-element.79), channel_id=1, source_target_pairs={{0,96},{32,0},{64,32},{96,64},{1,97},{33,1},{65,33},{97,65},{2,98}... | collective-permute-start | bytes 540680 | tf_op jit(solution)/shard_map/ppermute | solution.py:393
  17.8 3.5 %shard_map.63.pay = f32[1024,128]{1,0:T(8,128)S(1)} custom-call(bf16[4,64,1024]{2,1,0:T(8,128)(2,1)S(1)} %get-tuple-element.63.own, bf16[4,64,128]{2,1,0:T(8,128)(2,1)S(1)} %get-tuple-element.85.low, bf16[4,64,128]{2,1,0:T(8,128)(2,1)S(1)} %get-tuple-element.86.high, bf16[64,128]{1,0:T(8,128)(2,1)S(1)} %get-tuple-element.87.z_all, ...), custom_call_target="tpu_custom_call" | custom-call | flops 3623878656 | bytes 3293184 | tf_op jit(solution)/shard_map/pallas_call | solution.py:27
  22.4 4.3 %collective-permute-start.6 = (f32[512,128]{1,0:T(8,128)S(1)}, f32[512,128]{1,0:T(8,128)S(1)}, u32[]{:S(2)}, u32[]{:S(2)}) collective-permute-start(f32[512,128]{1,0:T(8,128)S(1)} %get-tuple-element.89), channel_id=1, source_target_pairs={{0,2},{1,3},{2,0},{3,1},{4,6},{5,7},{6,4},{7,5},{8,10},{9,11},{10,... | collective-permute-start | bytes 786440 | tf_op jit(solution)/shard_map/ppermute | solution.py:352
  26.7 1.2 %collective-permute-done.6.got = f32[512,128]{1,0:T(8,128)S(1)} collective-permute-done((f32[512,128]{1,0:T(8,128)S(1)}, f32[512,128]{1,0:T(8,128)S(1)}, u32[]{:S(2)}, u32[]{:S(2)}) %collective-permute-start.6) | collective-permute-done | bytes 262176 | tf_op jit(solution)/shard_map/ppermute | solution.py:352
  28.7 2.3 %collective-permute-start.8 = (f32[128,128]{1,0:T(8,128)S(1)}, f32[128,128]{1,0:T(8,128)S(1)}, u32[]{:S(2)}, u32[]{:S(2)}) collective-permute-start(f32[128,128]{1,0:T(8,128)S(1)} %get-tuple-element.96), channel_id=1, source_target_pairs={{0,16},{1,17},{2,18},{3,19},{4,20},{5,21},{6,22},{7,23},{8,24},{9,... | collective-permute-start | bytes 196616 | tf_op jit(solution)/shard_map/ppermute | solution.py:352
  31.9 1.4 %collective-permute-start.16 = (bf16[128,1408]{1,0:T(8,128)(2,1)S(1)}, bf16[128,1408]{1,0:T(8,128)(2,1)S(1)}, u32[]{:S(2)}, u32[]{:S(2)}) collective-permute-start(bf16[128,1408]{1,0:T(8,128)(2,1)S(1)} %get-tuple-element.115), channel_id=1, source_target_pairs={{0,32},{32,64},{64,96},{96,0},{1,33},{33,65},{65,97},{97,1},{2,34}... | collective-permute-start | bytes 1081352 | tf_op jit(solution)/shard_map/ppermute | solution.py:427
  33.3 1.4 %collective-permute-start.17 = (bf16[128,1408]{1,0:T(8,128)(2,1)S(1)}, bf16[128,1408]{1,0:T(8,128)(2,1)S(1)}, u32[]{:S(2)}, u32[]{:S(2)}) collective-permute-start(bf16[128,1408]{1,0:T(8,128)(2,1)S(1)} %get-tuple-element.116), channel_id=1, source_target_pairs={{0,96},{32,0},{64,32},{96,64},{1,97},{33,1},{65,33},{97,65},{2,98}... | collective-permute-start | bytes 1081352 | tf_op jit(solution)/shard_map/ppermute | solution.py:427
  35.6 3.6 %collective-permute-start.11 = (f32[128,128]{1,0:T(8,128)S(1)}, f32[128,128]{1,0:T(8,128)S(1)}, u32[]{:S(2)}, u32[]{:S(2)}) collective-permute-start(f32[128,128]{1,0:T(8,128)S(1)} %add_add_fusion.2), channel_id=1, source_target_pairs={{0,8},{1,9},{2,10},{3,11},{4,12},{5,13},{6,14},{7,15},{8,0},{9,1},... | collective-permute-start | bytes 196616 | tf_op jit(solution)/shard_map/ppermute | solution.py:352
  39.4 5.5 %shard_map.66 = bf16[8,32,4,8,128]{4,3,2,1,0:T(8,128)(2,1)} custom-call(bf16[4,64,1024]{2,1,0:T(8,128)(2,1)S(1)} %get-tuple-element.63.own, bf16[64,1408]{1,0:T(8,128)(2,1)S(1)} %collective-permute-done.3.left, bf16[64,1408]{1,0:T(8,128)(2,1)S(1)} %collective-permute-done.4.right, bf16[4,64,128]{2,1,0:T(8,128)(2,1)S(1)} %get-tuple-element.85.low, ...), custom_call_target="tpu_custom_call" | custom-call | flops 3623878656 | bytes 4014080 | tf_op jit(solution)/shard_map/pallas_call | solution.py:27
  45.0 1.4 %collective-permute-start.13 = (f32[128,128]{1,0:T(8,128)S(1)}, f32[128,128]{1,0:T(8,128)S(1)}, u32[]{:S(2)}, u32[]{:S(2)}) collective-permute-start(f32[128,128]{1,0:T(8,128)S(1)} %add_add_fusion.1), channel_id=1, source_target_pairs={{0,32},{1,33},{2,34},{3,35},{4,36},{5,37},{6,38},{7,39},{8,40},{9,... | collective-permute-start | bytes 196616 | tf_op jit(solution)/shard_map/ppermute | solution.py:352
  46.3 2.5 %collective-permute-start.14 = (f32[128,128]{1,0:T(8,128)S(1)}, f32[128,128]{1,0:T(8,128)S(1)}, u32[]{:S(2)}, u32[]{:S(2)}) collective-permute-start(f32[128,128]{1,0:T(8,128)S(1)} %add_add_fusion.1), channel_id=1, source_target_pairs={{0,64},{1,65},{2,66},{3,67},{4,68},{5,69},{6,70},{7,71},{8,72},{9,... | collective-permute-start | bytes 196616 | tf_op jit(solution)/shard_map/ppermute | solution.py:352
  48.9 5.3 %shard_map.68 = bf16[64,4,8,128]{3,2,1,0:T(8,128)(2,1)} custom-call(bf16[4,256,1024]{2,1,0:T(8,128)(2,1)S(1)} %get-tuple-element.84.cot.own, bf16[128,1408]{1,0:T(8,128)(2,1)S(1)} %collective-permute-done.16.left, bf16[128,1408]{1,0:T(8,128)(2,1)S(1)} %collective-permute-done.17.right, bf16[4,128,128]{2,1,0:T(8,128)(2,1)S(1)} %get-tuple-element.112.low, ...), custom_call_target="tpu_custom_call" | custom-call | flops 4294967296 | bytes 3899392 | tf_op jit(solution)/shard_map/pallas_call | solution.py:27
  54.3 1.5 %collective-permute-start.20 = (f32[128,128]{1,0:T(8,128)S(1)}, f32[128,128]{1,0:T(8,128)S(1)}, u32[]{:S(2)}, u32[]{:S(2)}) collective-permute-start(f32[128,128]{1,0:T(8,128)S(1)} %add_add_fusion.refs_0_), channel_id=1, source_target_pairs={{0,17},{1,16},{2,19},{3,18},{4,21},{5,20},{6,23},{7,22},{8,25},{9,... | collective-permute-start | bytes 196616 | tf_op jit(solution)/shard_map/ppermute | solution.py:352
  55.8 1.2 %collective-permute-start.19 = (f32[128,128]{1,0:T(8,128)S(1)}, f32[128,128]{1,0:T(8,128)S(1)}, u32[]{:S(2)}, u32[]{:S(2)}) collective-permute-start(f32[128,128]{1,0:T(8,128)S(1)} %add_add_fusion.refs_0_), channel_id=1, source_target_pairs={{0,16},{1,17},{2,18},{3,19},{4,20},{5,21},{6,22},{7,23},{8,24},{9,... | collective-permute-start | bytes 196616 | tf_op jit(solution)/shard_map/ppermute | solution.py:352
  57.6 4.5 %collective-permute-start.21 = (f32[128,128]{1,0:T(8,128)S(1)}, f32[128,128]{1,0:T(8,128)S(1)}, u32[]{:S(2)}, u32[]{:S(2)}) collective-permute-start(f32[128,128]{1,0:T(8,128)S(1)} %add_add_fusion.refs_0_), channel_id=1, source_target_pairs={{0,2},{1,3},{2,0},{3,1},{4,6},{5,7},{6,4},{7,5},{8,10},{9,11},{10,... | collective-permute-start | bytes 196616 | tf_op jit(solution)/shard_map/ppermute | solution.py:352
  62.1 1.4 %collective-permute-start.24 = (f32[128,128]{1,0:T(8,128)S(1)}, f32[128,128]{1,0:T(8,128)S(1)}, u32[]{:S(2)}, u32[]{:S(2)}) collective-permute-start(f32[128,128]{1,0:T(8,128)S(1)} %collective-permute-done.20.refs_3_), channel_id=1, source_target_pairs={{0,2},{1,3},{2,0},{3,1},{4,6},{5,7},{6,4},{7,5},{8,10},{9,11},{10,... | collective-permute-start | bytes 196616 | tf_op jit(solution)/shard_map/ppermute | solution.py:352
  63.5 1.4 %collective-permute-start.23 = (f32[128,128]{1,0:T(8,128)S(1)}, f32[128,128]{1,0:T(8,128)S(1)}, u32[]{:S(2)}, u32[]{:S(2)}) collective-permute-start(f32[128,128]{1,0:T(8,128)S(1)} %collective-permute-done.19.refs_2_), channel_id=1, source_target_pairs={{0,2},{1,3},{2,0},{3,1},{4,6},{5,7},{6,4},{7,5},{8,10},{9,11},{10,... | collective-permute-start | bytes 196616 | tf_op jit(solution)/shard_map/ppermute | solution.py:352
  66.2 1.1 %shard_map.69 = f32[4,4,4,32,64]{4,3,2,1,0:T(8,128)} custom-call(f32[128,128]{1,0:T(8,128)S(1)} %add_add_fusion.refs_0_, f32[128,128]{1,0:T(8,128)S(1)} %collective-permute-done.18.refs_1_, f32[128,128]{1,0:T(8,128)S(1)} %collective-permute-done.19.refs_2_, f32[128,128]{1,0:T(8,128)S(1)} %collective-permute-done.20.refs_3_, ...), custom_call_target="tpu_custom_call" | custom-call | bytes 1048576 | tf_op jit(solution)/shard_map/pallas_call | solution.py:27
  (44 shorter events, 7.5 us)
Async XLA Ops:
  2.3 4.6 %collective-permute-start = (bf16[64,128]{1,0:T(8,128)(2,1)S(1)}, bf16[64,128]{1,0:T(8,128)(2,1)S(1)}, u32[]{:S(2)}, u32[]{:S(2)}) collective-permute-start(bf16[64,128]{1,0:T(8,128)(2,1)S(1)} %get-tuple-element.64), channel_id=1, source_target_pairs={{0,1},{1,0},{2,3},{3,2},{4,5},{5,4},{6,7},{7,6},{8,9},{9,8},{10,11... | collective-permute-start | bytes 49160 | tf_op jit(solution)/shard_map/ppermute | solution.py:373
  7.0 6.7 %collective-permute-start.2 = (bf16[832,128]{1,0:T(8,128)(2,1)S(1)}, bf16[832,128]{1,0:T(8,128)(2,1)S(1)}, u32[]{:S(2)}, u32[]{:S(2)}) collective-permute-start(bf16[832,128]{1,0:T(8,128)(2,1)S(1)} %get-tuple-element.123), channel_id=1, source_target_pairs={{0,30},{2,4},{4,2},{6,8},{8,6},{10,12},{12,10},{14,16},{16,14},{18... | collective-permute-start | bytes 638984 | tf_op jit(solution)/shard_map/ppermute | solution.py:385
  9.5 4.9 %collective-permute-start.1 = (bf16[832,128]{1,0:T(8,128)(2,1)S(1)}, bf16[832,128]{1,0:T(8,128)(2,1)S(1)}, u32[]{:S(2)}, u32[]{:S(2)}) collective-permute-start(bf16[832,128]{1,0:T(8,128)(2,1)S(1)} %get-tuple-element.124), channel_id=1, source_target_pairs={{0,2},{2,0},{4,6},{6,4},{8,10},{10,8},{12,14},{14,12},{16,18},{18,... | collective-permute-start | bytes 638984 | tf_op jit(solution)/shard_map/ppermute | solution.py:386
  14.8 6.5 %collective-permute-start.5 = (bf16[128,128]{1,0:T(8,128)(2,1)S(1)}, bf16[128,128]{1,0:T(8,128)(2,1)S(1)}, u32[]{:S(2)}, u32[]{:S(2)}) collective-permute-start(bf16[128,128]{1,0:T(8,128)(2,1)S(1)} %get-tuple-element.81), channel_id=1, source_target_pairs={{0,1},{1,0},{2,3},{3,2},{4,5},{5,4},{6,7},{7,6},{8,9},{9,8},{10,11... | collective-permute-start | bytes 98312 | tf_op jit(solution)/shard_map/ppermute | solution.py:396
  14.9 6.4 %collective-permute-start.3 = (bf16[64,1408]{1,0:T(8,128)(2,1)S(1)}, bf16[64,1408]{1,0:T(8,128)(2,1)S(1)}, u32[]{:S(2)}, u32[]{:S(2)}) collective-permute-start(bf16[64,1408]{1,0:T(8,128)(2,1)S(1)} %get-tuple-element.78), channel_id=1, source_target_pairs={{0,32},{32,64},{64,96},{96,0},{1,33},{33,65},{65,97},{97,1},{2,34}... | collective-permute-start | bytes 540680 | tf_op jit(solution)/shard_map/ppermute | solution.py:393
  16.3 5.1 %collective-permute-start.4 = (bf16[64,1408]{1,0:T(8,128)(2,1)S(1)}, bf16[64,1408]{1,0:T(8,128)(2,1)S(1)}, u32[]{:S(2)}, u32[]{:S(2)}) collective-permute-start(bf16[64,1408]{1,0:T(8,128)(2,1)S(1)} %get-tuple-element.79), channel_id=1, source_target_pairs={{0,96},{32,0},{64,32},{96,64},{1,97},{33,1},{65,33},{97,65},{2,98}... | collective-permute-start | bytes 540680 | tf_op jit(solution)/shard_map/ppermute | solution.py:393
  22.4 5.5 %collective-permute-start.6 = (f32[512,128]{1,0:T(8,128)S(1)}, f32[512,128]{1,0:T(8,128)S(1)}, u32[]{:S(2)}, u32[]{:S(2)}) collective-permute-start(f32[512,128]{1,0:T(8,128)S(1)} %get-tuple-element.89), channel_id=1, source_target_pairs={{0,2},{1,3},{2,0},{3,1},{4,6},{5,7},{6,4},{7,5},{8,10},{9,11},{10,... | collective-permute-start | bytes 786440 | tf_op jit(solution)/shard_map/ppermute | solution.py:352
  27.9 6.8 %collective-permute-start.7 = (f32[128,128]{1,0:T(8,128)S(1)}, f32[128,128]{1,0:T(8,128)S(1)}, u32[]{:S(2)}, u32[]{:S(2)}) collective-permute-start(f32[128,128]{1,0:T(8,128)S(1)} %get-tuple-element.95), channel_id=1, source_target_pairs={{0,1},{1,0},{2,3},{3,2},{4,5},{5,4},{6,7},{7,6},{8,9},{9,8},{10,11... | collective-permute-start | bytes 196616 | tf_op jit(solution)/shard_map/ppermute | solution.py:352
  28.7 5.9 %collective-permute-start.8 = (f32[128,128]{1,0:T(8,128)S(1)}, f32[128,128]{1,0:T(8,128)S(1)}, u32[]{:S(2)}, u32[]{:S(2)}) collective-permute-start(f32[128,128]{1,0:T(8,128)S(1)} %get-tuple-element.96), channel_id=1, source_target_pairs={{0,16},{1,17},{2,18},{3,19},{4,20},{5,21},{6,22},{7,23},{8,24},{9,... | collective-permute-start | bytes 196616 | tf_op jit(solution)/shard_map/ppermute | solution.py:352
  31.0 4.5 %collective-permute-start.9 = (f32[128,128]{1,0:T(8,128)S(1)}, f32[128,128]{1,0:T(8,128)S(1)}, u32[]{:S(2)}, u32[]{:S(2)}) collective-permute-start(f32[128,128]{1,0:T(8,128)S(1)} %get-tuple-element.97), channel_id=1, source_target_pairs={{0,17},{1,16},{2,19},{3,18},{4,21},{5,20},{6,23},{7,22},{8,25},{9,... | collective-permute-start | bytes 196616 | tf_op jit(solution)/shard_map/ppermute | solution.py:352
  31.9 17.0 %collective-permute-start.16 = (bf16[128,1408]{1,0:T(8,128)(2,1)S(1)}, bf16[128,1408]{1,0:T(8,128)(2,1)S(1)}, u32[]{:S(2)}, u32[]{:S(2)}) collective-permute-start(bf16[128,1408]{1,0:T(8,128)(2,1)S(1)} %get-tuple-element.115), channel_id=1, source_target_pairs={{0,32},{32,64},{64,96},{96,0},{1,33},{33,65},{65,97},{97,1},{2,34}... | collective-permute-start | bytes 1081352 | tf_op jit(solution)/shard_map/ppermute | solution.py:427
  33.3 15.6 %collective-permute-start.17 = (bf16[128,1408]{1,0:T(8,128)(2,1)S(1)}, bf16[128,1408]{1,0:T(8,128)(2,1)S(1)}, u32[]{:S(2)}, u32[]{:S(2)}) collective-permute-start(bf16[128,1408]{1,0:T(8,128)(2,1)S(1)} %get-tuple-element.116), channel_id=1, source_target_pairs={{0,96},{32,0},{64,32},{96,64},{1,97},{33,1},{65,33},{97,65},{2,98}... | collective-permute-start | bytes 1081352 | tf_op jit(solution)/shard_map/ppermute | solution.py:427
  35.5 9.4 %collective-permute-start.10 = (f32[128,128]{1,0:T(8,128)S(1)}, f32[128,128]{1,0:T(8,128)S(1)}, u32[]{:S(2)}, u32[]{:S(2)}) collective-permute-start(f32[128,128]{1,0:T(8,128)S(1)} %add_add_fusion.2), channel_id=1, source_target_pairs={{0,4},{1,5},{2,6},{3,7},{4,0},{5,1},{6,2},{7,3},{8,12},{9,13},{10,... | collective-permute-start | bytes 196616 | tf_op jit(solution)/shard_map/ppermute | solution.py:352
  35.6 9.4 %collective-permute-start.11 = (f32[128,128]{1,0:T(8,128)S(1)}, f32[128,128]{1,0:T(8,128)S(1)}, u32[]{:S(2)}, u32[]{:S(2)}) collective-permute-start(f32[128,128]{1,0:T(8,128)S(1)} %add_add_fusion.2), channel_id=1, source_target_pairs={{0,8},{1,9},{2,10},{3,11},{4,12},{5,13},{6,14},{7,15},{8,0},{9,1},... | collective-permute-start | bytes 196616 | tf_op jit(solution)/shard_map/ppermute | solution.py:352
  39.2 5.7 %collective-permute-start.12 = (f32[128,128]{1,0:T(8,128)S(1)}, f32[128,128]{1,0:T(8,128)S(1)}, u32[]{:S(2)}, u32[]{:S(2)}) collective-permute-start(f32[128,128]{1,0:T(8,128)S(1)} %add_add_fusion.2), channel_id=1, source_target_pairs={{0,12},{1,13},{2,14},{3,15},{4,8},{5,9},{6,10},{7,11},{8,4},{9,5},... | collective-permute-start | bytes 196616 | tf_op jit(solution)/shard_map/ppermute | solution.py:352
  45.0 9.3 %collective-permute-start.13 = (f32[128,128]{1,0:T(8,128)S(1)}, f32[128,128]{1,0:T(8,128)S(1)}, u32[]{:S(2)}, u32[]{:S(2)}) collective-permute-start(f32[128,128]{1,0:T(8,128)S(1)} %add_add_fusion.1), channel_id=1, source_target_pairs={{0,32},{1,33},{2,34},{3,35},{4,36},{5,37},{6,38},{7,39},{8,40},{9,... | collective-permute-start | bytes 196616 | tf_op jit(solution)/shard_map/ppermute | solution.py:352
  46.3 7.9 %collective-permute-start.14 = (f32[128,128]{1,0:T(8,128)S(1)}, f32[128,128]{1,0:T(8,128)S(1)}, u32[]{:S(2)}, u32[]{:S(2)}) collective-permute-start(f32[128,128]{1,0:T(8,128)S(1)} %add_add_fusion.1), channel_id=1, source_target_pairs={{0,64},{1,65},{2,66},{3,67},{4,68},{5,69},{6,70},{7,71},{8,72},{9,... | collective-permute-start | bytes 196616 | tf_op jit(solution)/shard_map/ppermute | solution.py:352
  48.8 5.5 %collective-permute-start.15 = (f32[128,128]{1,0:T(8,128)S(1)}, f32[128,128]{1,0:T(8,128)S(1)}, u32[]{:S(2)}, u32[]{:S(2)}) collective-permute-start(f32[128,128]{1,0:T(8,128)S(1)} %add_add_fusion.1), channel_id=1, source_target_pairs={{0,96},{1,97},{2,98},{3,99},{4,100},{5,101},{6,102},{7,103},{8,104... | collective-permute-start | bytes 196616 | tf_op jit(solution)/shard_map/ppermute | solution.py:352
  54.3 7.8 %collective-permute-start.20 = (f32[128,128]{1,0:T(8,128)S(1)}, f32[128,128]{1,0:T(8,128)S(1)}, u32[]{:S(2)}, u32[]{:S(2)}) collective-permute-start(f32[128,128]{1,0:T(8,128)S(1)} %add_add_fusion.refs_0_), channel_id=1, source_target_pairs={{0,17},{1,16},{2,19},{3,18},{4,21},{5,20},{6,23},{7,22},{8,25},{9,... | collective-permute-start | bytes 196616 | tf_op jit(solution)/shard_map/ppermute | solution.py:352
  55.8 7.7 %collective-permute-start.19 = (f32[128,128]{1,0:T(8,128)S(1)}, f32[128,128]{1,0:T(8,128)S(1)}, u32[]{:S(2)}, u32[]{:S(2)}) collective-permute-start(f32[128,128]{1,0:T(8,128)S(1)} %add_add_fusion.refs_0_), channel_id=1, source_target_pairs={{0,16},{1,17},{2,18},{3,19},{4,20},{5,21},{6,22},{7,23},{8,24},{9,... | collective-permute-start | bytes 196616 | tf_op jit(solution)/shard_map/ppermute | solution.py:352
  57.0 7.9 %collective-permute-start.18 = (f32[128,128]{1,0:T(8,128)S(1)}, f32[128,128]{1,0:T(8,128)S(1)}, u32[]{:S(2)}, u32[]{:S(2)}) collective-permute-start(f32[128,128]{1,0:T(8,128)S(1)} %add_add_fusion.refs_0_), channel_id=1, source_target_pairs={{0,1},{1,0},{2,3},{3,2},{4,5},{5,4},{6,7},{7,6},{8,9},{9,8},{10,11... | collective-permute-start | bytes 196616 | tf_op jit(solution)/shard_map/ppermute | solution.py:352
  57.6 7.4 %collective-permute-start.21 = (f32[128,128]{1,0:T(8,128)S(1)}, f32[128,128]{1,0:T(8,128)S(1)}, u32[]{:S(2)}, u32[]{:S(2)}) collective-permute-start(f32[128,128]{1,0:T(8,128)S(1)} %add_add_fusion.refs_0_), channel_id=1, source_target_pairs={{0,2},{1,3},{2,0},{3,1},{4,6},{5,7},{6,4},{7,5},{8,10},{9,11},{10,... | collective-permute-start | bytes 196616 | tf_op jit(solution)/shard_map/ppermute | solution.py:352
  62.1 2.9 %collective-permute-start.24 = (f32[128,128]{1,0:T(8,128)S(1)}, f32[128,128]{1,0:T(8,128)S(1)}, u32[]{:S(2)}, u32[]{:S(2)}) collective-permute-start(f32[128,128]{1,0:T(8,128)S(1)} %collective-permute-done.20.refs_3_), channel_id=1, source_target_pairs={{0,2},{1,3},{2,0},{3,1},{4,6},{5,7},{6,4},{7,5},{8,10},{9,11},{10,... | collective-permute-start | bytes 196616 | tf_op jit(solution)/shard_map/ppermute | solution.py:352
  63.5 2.3 %collective-permute-start.23 = (f32[128,128]{1,0:T(8,128)S(1)}, f32[128,128]{1,0:T(8,128)S(1)}, u32[]{:S(2)}, u32[]{:S(2)}) collective-permute-start(f32[128,128]{1,0:T(8,128)S(1)} %collective-permute-done.19.refs_2_), channel_id=1, source_target_pairs={{0,2},{1,3},{2,0},{3,1},{4,6},{5,7},{6,4},{7,5},{8,10},{9,11},{10,... | collective-permute-start | bytes 196616 | tf_op jit(solution)/shard_map/ppermute | solution.py:352
  (2 other events, 14.0 us)

commit v4 on v3

--- a/solution.py
+++ b/solution.py
@@ -21,7 +21,7 @@
     return pltpu.VMEM(shape, dtype)
 
 
-def call(kernel, out_shape, scratch=(), flops=0, far=()):
+def call(kernel, out_shape, scratch=(), flops=0, far=(), aliases=None):
     def run(*operands):
         moved = sum(math.prod(o.shape) * o.dtype.itemsize for o in (*operands, *jax.tree.leaves(out_shape)))
         return pl.pallas_call(
@@ -31,6 +31,7 @@
             out_specs=jax.tree.map(lambda o: FAR if isinstance(o, jax.ShapeDtypeStruct) else WHOLE, out_shape),
             scratch_shapes=list(scratch),
             compiler_params=PARAMS,
+            input_output_aliases=aliases or {},
             cost_estimate=pl.CostEstimate(flops=flops, bytes_accessed=moved, transcendentals=0),
         )(*[pltpu.with_memory_space_constraint(o, pltpu.HBM if n in far else pltpu.VMEM) for n, o in enumerate(operands)])
 
@@ -194,10 +195,13 @@
     return at
 
 
-def fill_windows(planes, block, windows):
+def fill_windows(planes, block, windows, y_halo=True):
     for spot, xe in enumerate(planes):
         plane = plane_of(xe, *block)
-        for ye in range(10):
+        if not y_halo:
+            windows[spot * 576 : spot * 576 + 192, 0:128] = jnp.zeros((192, 128), BF16)
+            windows[spot * 576 + 384 : spot * 576 + 576, 896:1024] = jnp.zeros((192, 128), BF16)
+        for ye in range(10) if y_halo else range(1, 9):
             tile, column = plane(ye)
             three = (rolled(tile, column, True), tile, rolled(tile, column, False))
             for sy in range(3):
@@ -208,8 +212,8 @@
                         windows[row : row + 64, at * 128 : at * 128 + 128] = three[sz]
 
 
-def wgrad_main_kernel(own, low, high, z_all, cot, pay_out, windows, total):
-    fill_windows(range(1, 5), (own, None, None, low, high, z_all), windows)
+def wgrad_main_kernel(own, z_own, cot, pay_out, windows, total):
+    fill_windows(range(1, 5), (own, None, None, None, None, z_own), windows, False)
     for x in (1, 0, 2, 3):
         first, last = max(x - 1, 0), min(x + 1, 3)
         part = lax.dot_general(windows[first * 576 : last * 576 + 576, :], cot[x], NT, preferred_element_type=F32)
@@ -230,6 +234,39 @@
                             piece = total[row : row + 64, px * 128 : px * 128 + 128]
                             block = piece if py + pz == 0 else jnp.where(lane == 2 * py + pz, piece, block)
                     at = (px * 8 + hx * 4 + hy * 2 + hz) * 64
+                    pay_out[at : at + 64, :] = block
+
+
+def wgrad_y_kernel(low, high, z_all, cot, pay, pay_out, windows, totals):
+    for edge, (side, ye) in enumerate(((low, 0), (high, 9))):
+        for x in range(4):
+            tile, column = side[x], z_all[:, x * 10 + ye : x * 10 + ye + 1]
+            windows[x * 192 : x * 192 + 64, :] = rolled(tile, column, True)
+            windows[x * 192 + 64 : x * 192 + 128, :] = tile
+            windows[x * 192 + 128 : x * 192 + 192, :] = rolled(tile, column, False)
+        cells = slice(0, 128) if edge == 0 else slice(896, 1024)
+        for x in (1, 0, 2, 3):
+            first, last = max(x - 1, 0), min(x + 1, 3)
+            part = lax.dot_general(
+                windows[first * 192 : last * 192 + 192, :], cot[x, :, cells], NT, preferred_element_type=F32
+            )
+            row = (first - x + 1) * 192
+            if x == 1:
+                totals[edge] = part
+            else:
+                totals[edge, row : row + part.shape[0], :] += part
+    lane = lax.broadcasted_iota(jnp.int32, (64, 128), 1) // 32
+    for px in range(2):
+        for hx in range(2):
+            for hy in range(2):
+                for hz in range(2):
+                    at = (px * 8 + hx * 4 + hy * 2 + hz) * 64
+                    block = pay[at : at + 64, :]
+                    py = 1 - hy
+                    for pz in range(2):
+                        row = ((px - hx + 1) * 3 + (pz - hz + 1)) * 64
+                        piece = totals[0 if py - hy < 0 else 1, row : row + 64, px * 128 : px * 128 + 128]
+                        block = jnp.where(lane == 2 * py + pz, block + piece, block)
                     pay_out[at : at + 64, :] = block
 
 
@@ -311,16 +348,25 @@
     for_grad[...] = turned[...].T
 
 
-def up_kernel(own, left, right, low, high, z_all, matrix, out, windows, planes, sems):
-    fill_windows(range(6), (own, left, right, low, high, z_all), windows)
+def up_inside_kernel(own, low, high, z_all, *rest):
+    up_planes((1, 2), 1, (own, None, None, low, high, z_all), *rest)
+
+
+def up_outside_kernel(own, left, right, low, high, z_all, inside, *rest):
+    up_planes((0, 3), 0, (own, left, right, low, high, z_all), *rest)
+
+
+def up_planes(wanted, start, block, matrix, out, windows, planes, sems):
+    fill_windows(range(start, 6 - start), block, windows)
     copies = []
-    for x in range(4):
-        result = lax.dot_general(matrix[...], windows[x * 576 : x * 576 + 1728, :], NN, preferred_element_type=F32)
+    for spot, x in enumerate(wanted):
+        row = (x - start) * 576
+        result = lax.dot_general(matrix[...], windows[row : row + 1728, :], NN, preferred_element_type=F32)
         for n in range(8):
             part = result[n * 32 : n * 32 + 32].astype(BF16)
             part = jnp.stack([part[:, y * 128 : y * 128 + 128] for y in range(8)], 0)
-            planes[x, n] = jnp.swapaxes(part, 0, 1)
-            copies.append(pltpu.make_async_copy(planes.at[x, n], out.at[n, :, x], sems.at[x, n]))
+            planes[spot, n] = jnp.swapaxes(part, 0, 1)
+            copies.append(pltpu.make_async_copy(planes.at[spot, n], out.at[n, :, x], sems.at[spot, n]))
             copies[-1].start()
     for copy in copies:
         copy.wait()
@@ -378,38 +424,51 @@
         far=(0,),
     )(cotangent.reshape(8, 32, 4, 8, 128))
     rows = lambda *parts: jnp.concatenate([part.reshape(-1, 128) for part in parts])
-    z_own, weight_t = lax.optimization_barrier((z_own, weight_t))
-    for_up, for_grad = call(
-        weights_kernel, (shaped((256, 1728)), shaped((64, 2048))), [pltpu.VMEM((2048, 64), BF16)], far=()
-    )(weight_t)
     outer = lax.ppermute(rows(outer, z_own, outer_cot), "gy", OUTER)
     inner = lax.ppermute(rows(inner, z_own, inner_cot), "gy", INNER)
-    inner, outer, for_up, for_grad = lax.optimization_barrier((inner, outer, for_up, for_grad))
-    face = shaped((4, 64, 128))
-    left, right, low, high, z_all = call(
-        side_in_kernel, (shaped((64, 1408)), shaped((64, 1408)), face, face, shaped((64, 128)))
-    )(own, z_own, inner, outer)
-    left, right, z_face = lax.optimization_barrier((left, right, z_face))
-    left, right = lax.ppermute(left, "gx", x_up), lax.ppermute(right, "gx", x_down)
-    face = shaped((4, 128, 128))
-    low_cot, high_cot, z_face = call(side_cot_kernel, (face, face, shaped((128, 128))))(z_face, inner, outer)
-    z_cot = lax.ppermute(z_face, "gz", swap)
     pay = call(
         wgrad_main_kernel,
         shaped((1024, 128), F32),
         [pltpu.VMEM((2304, 1024), BF16), pltpu.VMEM((1728, 256), F32)],
         flops=2 * 1728 * 256 * 4096,
-    )(own, low, high, z_all, cot)
-    left, right, z_cot = lax.optimization_barrier((left, right, z_cot))
+    )(own, z_own, cot)
+    pay, weight_t = lax.optimization_barrier((pay, weight_t))
+    for_up, for_grad = call(
+        weights_kernel, (shaped((256, 1728)), shaped((64, 2048))), [pltpu.VMEM((2048, 64), BF16)]
+    )(weight_t)
+    inner, outer, for_up, for_grad, pay = lax.optimization_barrier((inner, outer, for_up, for_grad, pay))
+    face = shaped((4, 64, 128))
+    left, right, low, high, z_all = call(
+        side_in_kernel, (shaped((64, 1408)), shaped((64, 1408)), face, face, shaped((64, 128)))
+    )(own, z_own, inner, outer)
+    left, right = lax.ppermute(left, "gx", x_up), lax.ppermute(right, "gx", x_down)
+    pay = call(
+        wgrad_y_kernel,
+        shaped((1024, 128), F32),
+        [pltpu.VMEM((768, 128), BF16), pltpu.VMEM((2, 576, 256), F32)],
+        flops=2 * 1152 * 256 * 512,
+    )(low, high, z_all, cot, pay)
+    face = shaped((4, 128, 128))
+    pay, z_face = lax.optimization_barrier((pay, z_face))
+    low_cot, high_cot, z_face = call(side_cot_kernel, (face, face, shaped((128, 128))))(z_face, inner, outer)
+    z_cot = lax.ppermute(z_face, "gz", swap)
+    up_shape = jax.ShapeDtypeStruct((8, 32, 4, 8, 128), BF16)
+    up_scratch = [pltpu.VMEM((2, 8, 32, 8, 128), BF16), pltpu.SemaphoreType.DMA((2, 8))]
+    inside = call(up_inside_kernel, up_shape, [pltpu.VMEM((2304, 1024), BF16), *up_scratch], flops=2 * 1728 * 256 * 2048)(
+        own, low, high, z_all, for_up
+    )
+    left, right, z_cot, inside, pay = lax.optimization_barrier((left, right, z_cot, inside, pay))
     keep, give = call(
         wgrad_edge_kernel, (shaped((512, 128), F32),) * 2, [pltpu.VMEM((1152, 1024), BF16)], flops=2 * 1152 * 128 * 1024
     )(left, right, cot, pay)
     up_work = call(
-        up_kernel,
-        jax.ShapeDtypeStruct((8, 32, 4, 8, 128), BF16),
-        [pltpu.VMEM((3456, 1024), BF16), pltpu.VMEM((4, 8, 32, 8, 128), BF16), pltpu.SemaphoreType.DMA((4, 8))],
-        flops=2 * 1728 * 256 * 4096,
-    ), (own, left, right, low, high, z_all, for_up)
+        up_outside_kernel,
+        up_shape,
+        [pltpu.VMEM((3456, 1024), BF16), *up_scratch],
+        2 * 1728 * 256 * 2048,
+        (6,),
+        {6: 0},
+    ), (own, left, right, low, high, z_all, inside, for_up)
     grad_work = call(
         igrad_kernel,
         jax.ShapeDtypeStruct((64, 4, 8, 128), BF16),

time: 67.6 us -> 67.4 us (level)
  starting transfers between devices: 41.1 us -> 38.1 us
  Pallas kernels: 21.3 us -> 23.3 us
  waiting for transfers between devices: 3.96 us -> 4.77 us
    ppermute x17, starting transfers between devices: 26.9 us -> 23.8 us  [send(): return lax.ppermute(block, AXES, xor_pairs(*flip))]
    pallas_call x12 -> x14, Pallas kernels: 21.3 us -> 23.3 us  [run(): pl.pallas_call(kernel, out_shape=out_shape, in_specs=[FAR if n in far els...]
    ppermute x17, waiting for transfers between devices: 3.13 us -> 4.5 us  [send(): return lax.ppermute(block, AXES, xor_pairs(*flip))]
    ppermute x1, waiting for transfers between devices: 0.82 us -> 0.01 us  [body(): inner = lax.ppermute(rows(inner, z_own, inner_cot), 'gy', INNER)]
  transfers between devices with their start and end apart: 25 -> 25, of which waited for: 5 -> 6; matrix products, arithmetic and copies ran while one was open for 0% -> 0% of each run, Pallas kernels for 25% -> 29%
where the time goes in v4:
time: 67.4 us; the launch traced here: 67.2 us
  starting transfers between devices  38.1 us (57%)
  Pallas kernels  23.3 us (35%)
  waiting for transfers between devices  4.77 us (7%)
  between operations  1.02 us (2%)
    ppermute x17, starting transfers between devices, send(): return lax.ppermute(block, AXES, xor_pairs(*flip))  23.8 us
    pallas_call x14, Pallas kernels, run(): pl.pallas_call(kernel, out_shape=out_shape, in_specs=[FAR if n in far els...  23.3 us
    ppermute x17, waiting for transfers between devices, send(): return lax.ppermute(block, AXES, xor_pairs(*flip))  4.5 us
    ppermute x1, starting transfers between devices, body(): inner = lax.ppermute(rows(inner, z_own, inner_cot), 'gy', INNER)  3.84 us
    ppermute x1, starting transfers between devices, body(): outer = lax.ppermute(rows(outer, z_own, outer_cot), 'gy', OUTER)  2.56 us
    ppermute x1, starting transfers between devices, body(): z_own = lax.ppermute(z_face, 'gz', swap)  2.12 us
    ppermute x1, starting transfers between devices, body(): lax.ppermute(cot_right, 'gx', x_down)  1.75 us
    ppermute x1, starting transfers between devices, body(): lax.ppermute(right, 'gx', x_down)  1.52 us
  transfers between devices with their start and end apart: 25, of which 6 were waited for; matrix products, arithmetic and copies ran while one was open for 0% of the time, Pallas kernels for 29%

profile of v4, /device:TPU:1, one launch (start us, length us, event | category | flops | bytes accessed | tf_op | source)
XLA Modules:
  0.0 67.2 jit_solution(9074797637297171017)
XLA Ops:
  0.6 1.6 %shard_map.58 = (bf16[4,64,1024]{2,1,0:T(8,128)(2,1)S(1)}, bf16[64,128]{1,0:T(8,128)(2,1)S(1)}, bf16[4,64,128]{2,1,0:T(8,128)(2,1)S(1)}, bf16[4,64,128]{2,1,0:T(8,128)(2,1)S(1)}) custom-call(bf16[64,4,8,128]{3,2,1,0:T(8,128)(2,1)} %raw.1), custom_call_target="tpu_custom_call" | custom-call | bytes 1196032 | tf_op jit(solution)/shard_map/pallas_call | solution.py:27
  2.2 2.1 %collective-permute-start = (bf16[64,128]{1,0:T(8,128)(2,1)S(1)}, bf16[64,128]{1,0:T(8,128)(2,1)S(1)}, u32[]{:S(2)}, u32[]{:S(2)}) collective-permute-start(bf16[64,128]{1,0:T(8,128)(2,1)S(1)} %get-tuple-element.66), channel_id=1, source_target_pairs={{0,1},{1,0},{2,3},{3,2},{4,5},{5,4},{6,7},{7,6},{8,9},{9,8},{10,11... | collective-permute-start | bytes 49160 | tf_op jit(solution)/shard_map/ppermute | solution.py:419
  4.3 2.5 %shard_map.59 = (bf16[4,256,1024]{2,1,0:T(8,128)(2,1)S(1)}, bf16[128,128]{1,0:T(8,128)(2,1)S(1)}, bf16[4,128,128]{2,1,0:T(8,128)(2,1)S(1)}, bf16[4,128,128]{2,1,0:T(8,128)(2,1)S(1)}) custom-call(bf16[8,32,4,8,128]{4,3,2,1,0:T(8,128)(2,1)} %bitcast.13), custom_call_target="tpu_custom_call" | custom-call | bytes 4489216 | tf_op jit(solution)/shard_map/pallas_call | solution.py:27
  6.9 2.6 %collective-permute-start.2 = (bf16[832,128]{1,0:T(8,128)(2,1)S(1)}, bf16[832,128]{1,0:T(8,128)(2,1)S(1)}, u32[]{:S(2)}, u32[]{:S(2)}) collective-permute-start(bf16[832,128]{1,0:T(8,128)(2,1)S(1)} %get-tuple-element.127), channel_id=1, source_target_pairs={{0,30},{2,4},{4,2},{6,8},{8,6},{10,12},{12,10},{14,16},{16,14},{18... | collective-permute-start | bytes 638984 | tf_op jit(solution)/shard_map/ppermute | solution.py:427
  9.5 3.8 %collective-permute-start.1 = (bf16[832,128]{1,0:T(8,128)(2,1)S(1)}, bf16[832,128]{1,0:T(8,128)(2,1)S(1)}, u32[]{:S(2)}, u32[]{:S(2)}) collective-permute-start(bf16[832,128]{1,0:T(8,128)(2,1)S(1)} %get-tuple-element.128), channel_id=1, source_target_pairs={{0,2},{2,0},{4,6},{6,4},{8,10},{10,8},{12,14},{14,12},{16,18},{18,... | collective-permute-start | bytes 638984 | tf_op jit(solution)/shard_map/ppermute | solution.py:428
  13.3 3.5 %shard_map.60.pay = f32[1024,128]{1,0:T(8,128)S(1)} custom-call(bf16[4,64,1024]{2,1,0:T(8,128)(2,1)S(1)} %get-tuple-element.65.own, bf16[64,128]{1,0:T(8,128)(2,1)S(1)} %collective-permute-done.z_own, bf16[4,256,1024]{2,1,0:T(8,128)(2,1)S(1)} %get-tuple-element.71.cot.own), custom_call_target="tpu_custom_call" | custom-call | flops 3623878656 | bytes 3162112 | tf_op jit(solution)/shard_map/pallas_call | solution.py:27
  17.2 1.4 %collective-permute-start.3 = (bf16[64,1408]{1,0:T(8,128)(2,1)S(1)}, bf16[64,1408]{1,0:T(8,128)(2,1)S(1)}, u32[]{:S(2)}, u32[]{:S(2)}) collective-permute-start(bf16[64,1408]{1,0:T(8,128)(2,1)S(1)} %get-tuple-element.78), channel_id=1, source_target_pairs={{0,32},{32,64},{64,96},{96,0},{1,33},{33,65},{65,97},{97,1},{2,34}... | collective-permute-start | bytes 540680 | tf_op jit(solution)/shard_map/ppermute | solution.py:444
  18.6 1.5 %collective-permute-start.4 = (bf16[64,1408]{1,0:T(8,128)(2,1)S(1)}, bf16[64,1408]{1,0:T(8,128)(2,1)S(1)}, u32[]{:S(2)}, u32[]{:S(2)}) collective-permute-start(bf16[64,1408]{1,0:T(8,128)(2,1)S(1)} %get-tuple-element.79), channel_id=1, source_target_pairs={{0,96},{32,0},{64,32},{96,64},{1,97},{33,1},{65,33},{97,65},{2,98}... | collective-permute-start | bytes 540680 | tf_op jit(solution)/shard_map/ppermute | solution.py:444
  21.3 3.3 %shard_map.65.inside = bf16[8,32,4,8,128]{4,3,2,1,0:T(8,128)(2,1)} custom-call(bf16[4,64,1024]{2,1,0:T(8,128)(2,1)S(1)} %get-tuple-element.65.own, bf16[4,64,128]{2,1,0:T(8,128)(2,1)S(1)} %get-tuple-element.80.low, bf16[4,64,128]{2,1,0:T(8,128)(2,1)S(1)} %get-tuple-element.81.high, bf16[64,128]{1,0:T(8,128)(2,1)S(1)} %get-tuple-element.82.z_all, ...), custom_call_target="tpu_custom_call" | custom-call | flops 1811939328 | bytes 3653632 | tf_op jit(solution)/shard_map/pallas_call | solution.py:27
  25.9 1.2 %collective-permute-start.6 = (f32[512,128]{1,0:T(8,128)S(1)}, f32[512,128]{1,0:T(8,128)S(1)}, u32[]{:S(2)}, u32[]{:S(2)}) collective-permute-start(f32[512,128]{1,0:T(8,128)S(1)} %get-tuple-element.93), channel_id=1, source_target_pairs={{0,2},{1,3},{2,0},{3,1},{4,6},{5,7},{6,4},{7,5},{8,10},{9,11},{10,... | collective-permute-start | bytes 786440 | tf_op jit(solution)/shard_map/ppermute | solution.py:398
  27.0 1.2 %collective-permute-done.6.got = f32[512,128]{1,0:T(8,128)S(1)} collective-permute-done((f32[512,128]{1,0:T(8,128)S(1)}, f32[512,128]{1,0:T(8,128)S(1)}, u32[]{:S(2)}, u32[]{:S(2)}) %collective-permute-start.6) | collective-permute-done | bytes 262176 | tf_op jit(solution)/shard_map/ppermute | solution.py:398
  29.3 2.2 %collective-permute-start.8 = (f32[128,128]{1,0:T(8,128)S(1)}, f32[128,128]{1,0:T(8,128)S(1)}, u32[]{:S(2)}, u32[]{:S(2)}) collective-permute-start(f32[128,128]{1,0:T(8,128)S(1)} %get-tuple-element.100), channel_id=1, source_target_pairs={{0,16},{1,17},{2,18},{3,19},{4,20},{5,21},{6,22},{7,23},{8,24},{9,... | collective-permute-start | bytes 196616 | tf_op jit(solution)/shard_map/ppermute | solution.py:398
  33.4 1.7 %collective-permute-start.17 = (bf16[128,1408]{1,0:T(8,128)(2,1)S(1)}, bf16[128,1408]{1,0:T(8,128)(2,1)S(1)}, u32[]{:S(2)}, u32[]{:S(2)}) collective-permute-start(bf16[128,1408]{1,0:T(8,128)(2,1)S(1)} %get-tuple-element.120), channel_id=1, source_target_pairs={{0,96},{32,0},{64,32},{96,64},{1,97},{33,1},{65,33},{97,65},{2,98}... | collective-permute-start | bytes 1081352 | tf_op jit(solution)/shard_map/ppermute | solution.py:486
  36.2 3.5 %collective-permute-start.11 = (f32[128,128]{1,0:T(8,128)S(1)}, f32[128,128]{1,0:T(8,128)S(1)}, u32[]{:S(2)}, u32[]{:S(2)}) collective-permute-start(f32[128,128]{1,0:T(8,128)S(1)} %add_add_fusion.2), channel_id=1, source_target_pairs={{0,8},{1,9},{2,10},{3,11},{4,12},{5,13},{6,14},{7,15},{8,0},{9,1},... | collective-permute-start | bytes 196616 | tf_op jit(solution)/shard_map/ppermute | solution.py:398
  40.0 3.4 %shard_map.68 = bf16[8,32,4,8,128]{4,3,2,1,0:T(8,128)(2,1)} custom-call(bf16[4,64,1024]{2,1,0:T(8,128)(2,1)S(1)} %get-tuple-element.65.own, bf16[64,1408]{1,0:T(8,128)(2,1)S(1)} %collective-permute-done.3.left, bf16[64,1408]{1,0:T(8,128)(2,1)S(1)} %collective-permute-done.4.right, ...), custom_call_target="tpu_custom_call", output_to_operand_aliasing={{}: (6, {})} | custom-call | flops 1811939328 | bytes 6111232 | tf_op jit(solution)/shard_map/pallas_call | solution.py:27
  43.5 1.3 %collective-permute-done.12 = f32[128,128]{1,0:T(8,128)S(1)} collective-permute-done((f32[128,128]{1,0:T(8,128)S(1)}, f32[128,128]{1,0:T(8,128)S(1)}, u32[]{:S(2)}, u32[]{:S(2)}) %collective-permute-start.12) | collective-permute-done | bytes 65568 | tf_op jit(solution)/shard_map/ppermute | solution.py:398
  44.9 2.8 %collective-permute-start.14 = (f32[128,128]{1,0:T(8,128)S(1)}, f32[128,128]{1,0:T(8,128)S(1)}, u32[]{:S(2)}, u32[]{:S(2)}) collective-permute-start(f32[128,128]{1,0:T(8,128)S(1)} %add_add_fusion.1), channel_id=1, source_target_pairs={{0,64},{1,65},{2,66},{3,67},{4,68},{5,69},{6,70},{7,71},{8,72},{9,... | collective-permute-start | bytes 196616 | tf_op jit(solution)/shard_map/ppermute | solution.py:398
  48.7 5.3 %shard_map.70 = bf16[64,4,8,128]{3,2,1,0:T(8,128)(2,1)} custom-call(bf16[4,256,1024]{2,1,0:T(8,128)(2,1)S(1)} %get-tuple-element.71.cot.own, bf16[128,1408]{1,0:T(8,128)(2,1)S(1)} %collective-permute-done.16.left, bf16[128,1408]{1,0:T(8,128)(2,1)S(1)} %collective-permute-done.17.right, bf16[4,128,128]{2,1,0:T(8,128)(2,1)S(1)} %get-tuple-element.116.low, ...), custom_call_target="tpu_custom_call" | custom-call | flops 4294967296 | bytes 3899392 | tf_op jit(solution)/shard_map/pallas_call | solution.py:27
  54.1 1.3 %collective-permute-start.20 = (f32[128,128]{1,0:T(8,128)S(1)}, f32[128,128]{1,0:T(8,128)S(1)}, u32[]{:S(2)}, u32[]{:S(2)}) collective-permute-start(f32[128,128]{1,0:T(8,128)S(1)} %add_add_fusion.refs_0_), channel_id=1, source_target_pairs={{0,17},{1,16},{2,19},{3,18},{4,21},{5,20},{6,23},{7,22},{8,25},{9,... | collective-permute-start | bytes 196616 | tf_op jit(solution)/shard_map/ppermute | solution.py:398
  55.8 1.7 %collective-permute-start.18 = (f32[128,128]{1,0:T(8,128)S(1)}, f32[128,128]{1,0:T(8,128)S(1)}, u32[]{:S(2)}, u32[]{:S(2)}) collective-permute-start(f32[128,128]{1,0:T(8,128)S(1)} %add_add_fusion.refs_0_), channel_id=1, source_target_pairs={{0,1},{1,0},{2,3},{3,2},{4,5},{5,4},{6,7},{7,6},{8,9},{9,8},{10,11... | collective-permute-start | bytes 196616 | tf_op jit(solution)/shard_map/ppermute | solution.py:398
  57.4 4.4 %collective-permute-start.21 = (f32[128,128]{1,0:T(8,128)S(1)}, f32[128,128]{1,0:T(8,128)S(1)}, u32[]{:S(2)}, u32[]{:S(2)}) collective-permute-start(f32[128,128]{1,0:T(8,128)S(1)} %add_add_fusion.refs_0_), channel_id=1, source_target_pairs={{0,2},{1,3},{2,0},{3,1},{4,6},{5,7},{6,4},{7,5},{8,10},{9,11},{10,... | collective-permute-start | bytes 196616 | tf_op jit(solution)/shard_map/ppermute | solution.py:398
  61.9 1.4 %collective-permute-start.24 = (f32[128,128]{1,0:T(8,128)S(1)}, f32[128,128]{1,0:T(8,128)S(1)}, u32[]{:S(2)}, u32[]{:S(2)}) collective-permute-start(f32[128,128]{1,0:T(8,128)S(1)} %collective-permute-done.20.refs_3_), channel_id=1, source_target_pairs={{0,2},{1,3},{2,0},{3,1},{4,6},{5,7},{6,4},{7,5},{8,10},{9,11},{10,... | collective-permute-start | bytes 196616 | tf_op jit(solution)/shard_map/ppermute | solution.py:398
  63.2 1.4 %collective-permute-start.23 = (f32[128,128]{1,0:T(8,128)S(1)}, f32[128,128]{1,0:T(8,128)S(1)}, u32[]{:S(2)}, u32[]{:S(2)}) collective-permute-start(f32[128,128]{1,0:T(8,128)S(1)} %collective-permute-done.19.refs_2_), channel_id=1, source_target_pairs={{0,2},{1,3},{2,0},{3,1},{4,6},{5,7},{6,4},{7,5},{8,10},{9,11},{10,... | collective-permute-start | bytes 196616 | tf_op jit(solution)/shard_map/ppermute | solution.py:398
  65.9 1.1 %shard_map.71 = f32[4,4,4,32,64]{4,3,2,1,0:T(8,128)} custom-call(f32[128,128]{1,0:T(8,128)S(1)} %add_add_fusion.refs_0_, f32[128,128]{1,0:T(8,128)S(1)} %collective-permute-done.18.refs_1_, f32[128,128]{1,0:T(8,128)S(1)} %collective-permute-done.19.refs_2_, f32[128,128]{1,0:T(8,128)S(1)} %collective-permute-done.20.refs_3_, ...), custom_call_target="tpu_custom_call" | custom-call | bytes 1048576 | tf_op jit(solution)/shard_map/pallas_call | solution.py:27
  (46 shorter events, 9.9 us)
Async XLA Ops:
  2.2 4.6 %collective-permute-start = (bf16[64,128]{1,0:T(8,128)(2,1)S(1)}, bf16[64,128]{1,0:T(8,128)(2,1)S(1)}, u32[]{:S(2)}, u32[]{:S(2)}) collective-permute-start(bf16[64,128]{1,0:T(8,128)(2,1)S(1)} %get-tuple-element.66), channel_id=1, source_target_pairs={{0,1},{1,0},{2,3},{3,2},{4,5},{5,4},{6,7},{7,6},{8,9},{9,8},{10,11... | collective-permute-start | bytes 49160 | tf_op jit(solution)/shard_map/ppermute | solution.py:419
  6.9 10.2 %collective-permute-start.2 = (bf16[832,128]{1,0:T(8,128)(2,1)S(1)}, bf16[832,128]{1,0:T(8,128)(2,1)S(1)}, u32[]{:S(2)}, u32[]{:S(2)}) collective-permute-start(bf16[832,128]{1,0:T(8,128)(2,1)S(1)} %get-tuple-element.127), channel_id=1, source_target_pairs={{0,30},{2,4},{4,2},{6,8},{8,6},{10,12},{12,10},{14,16},{16,14},{18... | collective-permute-start | bytes 638984 | tf_op jit(solution)/shard_map/ppermute | solution.py:427
  9.5 7.6 %collective-permute-start.1 = (bf16[832,128]{1,0:T(8,128)(2,1)S(1)}, bf16[832,128]{1,0:T(8,128)(2,1)S(1)}, u32[]{:S(2)}, u32[]{:S(2)}) collective-permute-start(bf16[832,128]{1,0:T(8,128)(2,1)S(1)} %get-tuple-element.128), channel_id=1, source_target_pairs={{0,2},{2,0},{4,6},{6,4},{8,10},{10,8},{12,14},{14,12},{16,18},{18,... | collective-permute-start | bytes 638984 | tf_op jit(solution)/shard_map/ppermute | solution.py:428
  17.2 7.6 %collective-permute-start.3 = (bf16[64,1408]{1,0:T(8,128)(2,1)S(1)}, bf16[64,1408]{1,0:T(8,128)(2,1)S(1)}, u32[]{:S(2)}, u32[]{:S(2)}) collective-permute-start(bf16[64,1408]{1,0:T(8,128)(2,1)S(1)} %get-tuple-element.78), channel_id=1, source_target_pairs={{0,32},{32,64},{64,96},{96,0},{1,33},{33,65},{65,97},{97,1},{2,34}... | collective-permute-start | bytes 540680 | tf_op jit(solution)/shard_map/ppermute | solution.py:444
  18.6 6.2 %collective-permute-start.4 = (bf16[64,1408]{1,0:T(8,128)(2,1)S(1)}, bf16[64,1408]{1,0:T(8,128)(2,1)S(1)}, u32[]{:S(2)}, u32[]{:S(2)}) collective-permute-start(bf16[64,1408]{1,0:T(8,128)(2,1)S(1)} %get-tuple-element.79), channel_id=1, source_target_pairs={{0,96},{32,0},{64,32},{96,64},{1,97},{33,1},{65,33},{97,65},{2,98}... | collective-permute-start | bytes 540680 | tf_op jit(solution)/shard_map/ppermute | solution.py:444
  21.2 3.4 %collective-permute-start.5 = (bf16[128,128]{1,0:T(8,128)(2,1)S(1)}, bf16[128,128]{1,0:T(8,128)(2,1)S(1)}, u32[]{:S(2)}, u32[]{:S(2)}) collective-permute-start(bf16[128,128]{1,0:T(8,128)(2,1)S(1)} %get-tuple-element.86), channel_id=1, source_target_pairs={{0,1},{1,0},{2,3},{3,2},{4,5},{5,4},{6,7},{7,6},{8,9},{9,8},{10,11... | collective-permute-start | bytes 98312 | tf_op jit(solution)/shard_map/ppermute | solution.py:454
  25.9 2.3 %collective-permute-start.6 = (f32[512,128]{1,0:T(8,128)S(1)}, f32[512,128]{1,0:T(8,128)S(1)}, u32[]{:S(2)}, u32[]{:S(2)}) collective-permute-start(f32[512,128]{1,0:T(8,128)S(1)} %get-tuple-element.93), channel_id=1, source_target_pairs={{0,2},{1,3},{2,0},{3,1},{4,6},{5,7},{6,4},{7,5},{8,10},{9,11},{10,... | collective-permute-start | bytes 786440 | tf_op jit(solution)/shard_map/ppermute | solution.py:398
  28.2 6.9 %collective-permute-start.7 = (f32[128,128]{1,0:T(8,128)S(1)}, f32[128,128]{1,0:T(8,128)S(1)}, u32[]{:S(2)}, u32[]{:S(2)}) collective-permute-start(f32[128,128]{1,0:T(8,128)S(1)} %get-tuple-element.99), channel_id=1, source_target_pairs={{0,1},{1,0},{2,3},{3,2},{4,5},{5,4},{6,7},{7,6},{8,9},{9,8},{10,11... | collective-permute-start | bytes 196616 | tf_op jit(solution)/shard_map/ppermute | solution.py:398
  29.3 5.8 %collective-permute-start.8 = (f32[128,128]{1,0:T(8,128)S(1)}, f32[128,128]{1,0:T(8,128)S(1)}, u32[]{:S(2)}, u32[]{:S(2)}) collective-permute-start(f32[128,128]{1,0:T(8,128)S(1)} %get-tuple-element.100), channel_id=1, source_target_pairs={{0,16},{1,17},{2,18},{3,19},{4,20},{5,21},{6,22},{7,23},{8,24},{9,... | collective-permute-start | bytes 196616 | tf_op jit(solution)/shard_map/ppermute | solution.py:398
  31.5 4.6 %collective-permute-start.9 = (f32[128,128]{1,0:T(8,128)S(1)}, f32[128,128]{1,0:T(8,128)S(1)}, u32[]{:S(2)}, u32[]{:S(2)}) collective-permute-start(f32[128,128]{1,0:T(8,128)S(1)} %get-tuple-element.101), channel_id=1, source_target_pairs={{0,17},{1,16},{2,19},{3,18},{4,21},{5,20},{6,23},{7,22},{8,25},{9,... | collective-permute-start | bytes 196616 | tf_op jit(solution)/shard_map/ppermute | solution.py:398
  32.4 16.3 %collective-permute-start.16 = (bf16[128,1408]{1,0:T(8,128)(2,1)S(1)}, bf16[128,1408]{1,0:T(8,128)(2,1)S(1)}, u32[]{:S(2)}, u32[]{:S(2)}) collective-permute-start(bf16[128,1408]{1,0:T(8,128)(2,1)S(1)} %get-tuple-element.119), channel_id=1, source_target_pairs={{0,32},{32,64},{64,96},{96,0},{1,33},{33,65},{65,97},{97,1},{2,34}... | collective-permute-start | bytes 1081352 | tf_op jit(solution)/shard_map/ppermute | solution.py:486
  33.4 15.3 %collective-permute-start.17 = (bf16[128,1408]{1,0:T(8,128)(2,1)S(1)}, bf16[128,1408]{1,0:T(8,128)(2,1)S(1)}, u32[]{:S(2)}, u32[]{:S(2)}) collective-permute-start(bf16[128,1408]{1,0:T(8,128)(2,1)S(1)} %get-tuple-element.120), channel_id=1, source_target_pairs={{0,96},{32,0},{64,32},{96,64},{1,97},{33,1},{65,33},{97,65},{2,98}... | collective-permute-start | bytes 1081352 | tf_op jit(solution)/shard_map/ppermute | solution.py:486
  36.1 7.3 %collective-permute-start.10 = (f32[128,128]{1,0:T(8,128)S(1)}, f32[128,128]{1,0:T(8,128)S(1)}, u32[]{:S(2)}, u32[]{:S(2)}) collective-permute-start(f32[128,128]{1,0:T(8,128)S(1)} %add_add_fusion.2), channel_id=1, source_target_pairs={{0,4},{1,5},{2,6},{3,7},{4,0},{5,1},{6,2},{7,3},{8,12},{9,13},{10,... | collective-permute-start | bytes 196616 | tf_op jit(solution)/shard_map/ppermute | solution.py:398
  36.2 7.3 %collective-permute-start.11 = (f32[128,128]{1,0:T(8,128)S(1)}, f32[128,128]{1,0:T(8,128)S(1)}, u32[]{:S(2)}, u32[]{:S(2)}) collective-permute-start(f32[128,128]{1,0:T(8,128)S(1)} %add_add_fusion.2), channel_id=1, source_target_pairs={{0,8},{1,9},{2,10},{3,11},{4,12},{5,13},{6,14},{7,15},{8,0},{9,1},... | collective-permute-start | bytes 196616 | tf_op jit(solution)/shard_map/ppermute | solution.py:398
  39.7 5.0 %collective-permute-start.12 = (f32[128,128]{1,0:T(8,128)S(1)}, f32[128,128]{1,0:T(8,128)S(1)}, u32[]{:S(2)}, u32[]{:S(2)}) collective-permute-start(f32[128,128]{1,0:T(8,128)S(1)} %add_add_fusion.2), channel_id=1, source_target_pairs={{0,12},{1,13},{2,14},{3,15},{4,8},{5,9},{6,10},{7,11},{8,4},{9,5},... | collective-permute-start | bytes 196616 | tf_op jit(solution)/shard_map/ppermute | solution.py:398
  44.8 9.3 %collective-permute-start.13 = (f32[128,128]{1,0:T(8,128)S(1)}, f32[128,128]{1,0:T(8,128)S(1)}, u32[]{:S(2)}, u32[]{:S(2)}) collective-permute-start(f32[128,128]{1,0:T(8,128)S(1)} %add_add_fusion.1), channel_id=1, source_target_pairs={{0,32},{1,33},{2,34},{3,35},{4,36},{5,37},{6,38},{7,39},{8,40},{9,... | collective-permute-start | bytes 196616 | tf_op jit(solution)/shard_map/ppermute | solution.py:398
  44.9 9.2 %collective-permute-start.14 = (f32[128,128]{1,0:T(8,128)S(1)}, f32[128,128]{1,0:T(8,128)S(1)}, u32[]{:S(2)}, u32[]{:S(2)}) collective-permute-start(f32[128,128]{1,0:T(8,128)S(1)} %add_add_fusion.1), channel_id=1, source_target_pairs={{0,64},{1,65},{2,66},{3,67},{4,68},{5,69},{6,70},{7,71},{8,72},{9,... | collective-permute-start | bytes 196616 | tf_op jit(solution)/shard_map/ppermute | solution.py:398
  47.7 6.4 %collective-permute-start.15 = (f32[128,128]{1,0:T(8,128)S(1)}, f32[128,128]{1,0:T(8,128)S(1)}, u32[]{:S(2)}, u32[]{:S(2)}) collective-permute-start(f32[128,128]{1,0:T(8,128)S(1)} %add_add_fusion.1), channel_id=1, source_target_pairs={{0,96},{1,97},{2,98},{3,99},{4,100},{5,101},{6,102},{7,103},{8,104... | collective-permute-start | bytes 196616 | tf_op jit(solution)/shard_map/ppermute | solution.py:398
  54.1 7.8 %collective-permute-start.20 = (f32[128,128]{1,0:T(8,128)S(1)}, f32[128,128]{1,0:T(8,128)S(1)}, u32[]{:S(2)}, u32[]{:S(2)}) collective-permute-start(f32[128,128]{1,0:T(8,128)S(1)} %add_add_fusion.refs_0_), channel_id=1, source_target_pairs={{0,17},{1,16},{2,19},{3,18},{4,21},{5,20},{6,23},{7,22},{8,25},{9,... | collective-permute-start | bytes 196616 | tf_op jit(solution)/shard_map/ppermute | solution.py:398
  55.4 7.9 %collective-permute-start.19 = (f32[128,128]{1,0:T(8,128)S(1)}, f32[128,128]{1,0:T(8,128)S(1)}, u32[]{:S(2)}, u32[]{:S(2)}) collective-permute-start(f32[128,128]{1,0:T(8,128)S(1)} %add_add_fusion.refs_0_), channel_id=1, source_target_pairs={{0,16},{1,17},{2,18},{3,19},{4,20},{5,21},{6,22},{7,23},{8,24},{9,... | collective-permute-start | bytes 196616 | tf_op jit(solution)/shard_map/ppermute | solution.py:398
  55.8 8.9 %collective-permute-start.18 = (f32[128,128]{1,0:T(8,128)S(1)}, f32[128,128]{1,0:T(8,128)S(1)}, u32[]{:S(2)}, u32[]{:S(2)}) collective-permute-start(f32[128,128]{1,0:T(8,128)S(1)} %add_add_fusion.refs_0_), channel_id=1, source_target_pairs={{0,1},{1,0},{2,3},{3,2},{4,5},{5,4},{6,7},{7,6},{8,9},{9,8},{10,11... | collective-permute-start | bytes 196616 | tf_op jit(solution)/shard_map/ppermute | solution.py:398
  57.4 7.4 %collective-permute-start.21 = (f32[128,128]{1,0:T(8,128)S(1)}, f32[128,128]{1,0:T(8,128)S(1)}, u32[]{:S(2)}, u32[]{:S(2)}) collective-permute-start(f32[128,128]{1,0:T(8,128)S(1)} %add_add_fusion.refs_0_), channel_id=1, source_target_pairs={{0,2},{1,3},{2,0},{3,1},{4,6},{5,7},{6,4},{7,5},{8,10},{9,11},{10,... | collective-permute-start | bytes 196616 | tf_op jit(solution)/shard_map/ppermute | solution.py:398
  61.9 2.9 %collective-permute-start.24 = (f32[128,128]{1,0:T(8,128)S(1)}, f32[128,128]{1,0:T(8,128)S(1)}, u32[]{:S(2)}, u32[]{:S(2)}) collective-permute-start(f32[128,128]{1,0:T(8,128)S(1)} %collective-permute-done.20.refs_3_), channel_id=1, source_target_pairs={{0,2},{1,3},{2,0},{3,1},{4,6},{5,7},{6,4},{7,5},{8,10},{9,11},{10,... | collective-permute-start | bytes 196616 | tf_op jit(solution)/shard_map/ppermute | solution.py:398
  63.2 2.3 %collective-permute-start.23 = (f32[128,128]{1,0:T(8,128)S(1)}, f32[128,128]{1,0:T(8,128)S(1)}, u32[]{:S(2)}, u32[]{:S(2)}) collective-permute-start(f32[128,128]{1,0:T(8,128)S(1)} %collective-permute-done.19.refs_2_), channel_id=1, source_target_pairs={{0,2},{1,3},{2,0},{3,1},{4,6},{5,7},{6,4},{7,5},{8,10},{9,11},{10,... | collective-permute-start | bytes 196616 | tf_op jit(solution)/shard_map/ppermute | solution.py:398
  (2 other events, 4.8 us)
